TPU v7x, 32 devices: a whole 2x2x4 slice. The times are simulated.
32 devices in a mesh: batch: 8 (over z, y), win: 4 (over x, core).
Axes of the slice: x: 2, y: 2, z: 4, core: 2. Of those that a mesh axis runs over, the one named last changes fastest.
Arguments:
- frames: bfloat16 [8, 2, 4, 16, 64, 512], P('batch', None, 'win'), may hold values from -6 to 6
- space_gain: float32 [512], replicated, may hold values from 0.1 to 1.9
- space_offset: float32 [512], replicated, may hold values from -3 to 3
- space_entry: bfloat16 [512, 1536], replicated, may hold values from -0.25 to 0.25
- space_exit: bfloat16 [512, 512], replicated, may hold values from -0.75 to 0.75
- space_bias: float32 [512], replicated, may hold values from -1.75 to 1.75
- space_weigh: float32 [512], replicated, may hold values from 0.1 to 1.9
- space_shift: float32 [512], replicated, may hold values from -3 to 3
- space_widen: bfloat16 [512, 2048], replicated, may hold values from -0.25 to 0.25
- space_lift: float32 [2048], replicated, may hold values from -3 to 3
- space_narrow: bfloat16 [2048, 512], replicated, may hold values from -0.125 to 0.125
- space_nudge: float32 [512], replicated, may hold values from -1.75 to 1.75
- time_gain: float32 [512], replicated, may hold values from 0.1 to 1.9
- time_offset: float32 [512], replicated, may hold values from -3 to 3
- time_entry: bfloat16 [512, 1536], replicated, may hold values from -0.25 to 0.25
- time_exit: bfloat16 [512, 512], replicated, may hold values from -0.375 to 0.375
- time_bias: float32 [512], replicated, may hold values from -1.75 to 1.75
- time_weigh: float32 [512], replicated, may hold values from 0.1 to 1.9
- time_shift: float32 [512], replicated, may hold values from -3 to 3
- time_widen: bfloat16 [512, 2048], replicated, may hold values from -0.25 to 0.25
- time_lift: float32 [2048], replicated, may hold values from -3 to 3
- time_narrow: bfloat16 [2048, 512], replicated, may hold values from -0.125 to 0.125
- time_nudge: float32 [512], replicated, may hold values from -1.75 to 1.75
- cotangent: bfloat16 [8, 2, 4, 16, 64, 512], P('batch', None, 'win'), may hold values from -6 to 6
- video_frames: int32 [8, 8], P('batch'), may hold values from 0 to 6, as said below
Outputs:
- result: bfloat16 [8, 2, 4, 16, 64, 512], P('batch', None, 'win')
- frames_delta: bfloat16 [8, 2, 4, 16, 64, 512], P('batch', None, 'win')
- space_gain_delta: float32 [512], P('batch')
- space_offset_delta: float32 [512], P('batch')
- space_entry_delta: float32 [512, 1536], P('batch')
- space_exit_delta: float32 [512, 512], P('batch')
- space_bias_delta: float32 [512], P('batch')
- space_weigh_delta: float32 [512], P('batch')
- space_shift_delta: float32 [512], P('batch')
- space_widen_delta: float32 [512, 2048], P('batch')
- space_lift_delta: float32 [2048], P('batch')
- space_narrow_delta: float32 [2048, 512], P('batch')
- space_nudge_delta: float32 [512], P('batch')
- time_gain_delta: float32 [512], P('batch')
- time_offset_delta: float32 [512], P('batch')
- time_entry_delta: float32 [512, 1536], P('batch')
- time_exit_delta: float32 [512, 512], P('batch')
- time_bias_delta: float32 [512], P('batch')
- time_weigh_delta: float32 [512], P('batch')
- time_shift_delta: float32 [512], P('batch')
- time_widen_delta: float32 [512, 2048], P('batch')
- time_lift_delta: float32 [2048], P('batch')
- time_narrow_delta: float32 [2048, 512], P('batch')
- time_nudge_delta: float32 [512], P('batch')
Inputs may be any that keep to these rules, and one draw needn't show every extreme that they name: `video_frames`: each row lists the frame counts of up to 8 videos of one group in frame order, some entries 0; their total is at most 8 and the frames past it are padding. Each row has exactly one video of 6 frames.
All inputs are finite; a program needn't handle non-finite values.
Results may differ from a plain program's by a relative error of at most 0.02.
Values may be sent and summed in bfloat16 or wider, within the bound.
No kernel may reach another device: no remote copies, remote signals or barrier semaphores. Data moves between devices by JAX's collectives and lax.ppermute only.
A program may use at most 320 MiB of HBM per device.

v0:
```python
import jax
import jax.numpy as jnp
from jax import lax
from jax.sharding import PartitionSpec as P

D = 512
HEADS = 8
HDIM = 64


EPS = 1e-05
NEGATIVE = -1e30
FLOAT = jnp.float32
HALF = jnp.bfloat16


def gelu_exact(values):
    return jax.nn.gelu(values, approximate=False)


def norm_forward(rows, gain, offset):
    centre = rows - jnp.mean(rows, axis=-1, keepdims=True)
    inverse = lax.rsqrt(jnp.mean(centre * centre, axis=-1, keepdims=True) + EPS)
    unit = centre * inverse
    return (unit * gain + offset, unit, inverse)


def norm_backward(normed_back, unit, inverse, gain):
    scaled = normed_back * gain
    rows_back = inverse * (
        scaled
        - jnp.mean(scaled, axis=-1, keepdims=True)
        - unit * jnp.mean(scaled * unit, axis=-1, keepdims=True)
    )
    return (rows_back, jnp.sum(normed_back * unit, axis=0), jnp.sum(normed_back, axis=0))


def weight_product(left, right):
    return lax.dot_general(left, right, (((0,), (0,)), ((), ())), preferred_element_type=FLOAT)


def transposed_product(incoming, weight):
    return lax.dot_general(incoming, weight, (((1,), (1,)), ((), ())), preferred_element_type=FLOAT)


def column_sum(values):
    return jnp.sum(values, axis=0, dtype=FLOAT)


def split_heads(triple, length, across):
    if across:
        parts = jnp.swapaxes(triple.reshape(length, -1, 3, HEADS, HDIM), 0, 1)
    else:
        parts = triple.reshape(-1, length, 3, HEADS, HDIM)
    return (parts[:, :, 0], parts[:, :, 1], parts[:, :, 2])


def attend_forward(triple, length, allowed, across):
    queries, keys, values = split_heads(triple, length, across)
    scores = jnp.einsum("gthd,gshd->ghts", queries, keys, preferred_element_type=FLOAT) * HDIM ** (
        -0.5
    )
    if allowed is not None:
        scores = jnp.where(allowed, scores, NEGATIVE)
    peak = jnp.max(scores, axis=-1, keepdims=True)
    powers = jnp.exp(scores - peak)
    probs = powers / jnp.sum(powers, axis=-1, keepdims=True)
    weights = probs.astype(HALF)
    mixed = jnp.einsum("ghts,gshd->gthd", weights, values, preferred_element_type=FLOAT).astype(
        HALF
    )
    if across:
        mixed = jnp.swapaxes(mixed, 0, 1)
    return (mixed.reshape(-1, HEADS * HDIM), (queries, keys, values, probs, weights))


def attend_backward(mixed_back, length, across, kept):
    queries, keys, values, probs, weights = kept
    if across:
        heads_back = jnp.swapaxes(mixed_back.reshape(length, -1, HEADS, HDIM), 0, 1)
    else:
        heads_back = mixed_back.reshape(-1, length, HEADS, HDIM)
    weights_back = jnp.einsum("gthd,gshd->ghts", heads_back, values, preferred_element_type=FLOAT)
    values_back = jnp.einsum("ghts,gthd->gshd", weights, heads_back, preferred_element_type=FLOAT)
    scores_back = (
        probs * (weights_back - jnp.sum(weights_back * probs, axis=-1, keepdims=True))
    ).astype(HALF)
    scale = HDIM ** (-0.5)
    queries_back = (
        jnp.einsum("ghts,gshd->gthd", scores_back, keys, preferred_element_type=FLOAT) * scale
    )
    keys_back = (
        jnp.einsum("ghts,gthd->gshd", scores_back, queries, preferred_element_type=FLOAT) * scale
    )
    stacked = jnp.stack([queries_back, keys_back, values_back], axis=2)
    if across:
        stacked = jnp.swapaxes(stacked, 0, 1)
    return stacked.reshape(-1, 3 * HEADS * HDIM).astype(HALF)


def block_forward(rows, params, length, allowed, across):
    gain, offset, entry, leave, bias, weigh, shift, widen, lift, narrow, nudge = params
    normed, unit_one, inverse_one = norm_forward(rows, gain, offset)
    normed_low = normed.astype(HALF)
    triple = jnp.dot(normed_low, entry, preferred_element_type=FLOAT).astype(HALF)
    mixed, kept = attend_forward(triple, length, allowed, across)
    middle = rows + (jnp.dot(mixed, leave, preferred_element_type=FLOAT) + bias)
    second, unit_two, inverse_two = norm_forward(middle, weigh, shift)
    second_low = second.astype(HALF)
    hidden = jnp.dot(second_low, widen, preferred_element_type=FLOAT) + lift
    active, gelu_pull = jax.vjp(gelu_exact, hidden)
    active_low = active.astype(HALF)
    output = middle + (jnp.dot(active_low, narrow, preferred_element_type=FLOAT) + nudge)
    saved = (
        normed_low,
        unit_one,
        inverse_one,
        mixed,
        kept,
        unit_two,
        inverse_two,
        second_low,
        gelu_pull,
        active_low,
    )
    return (output, saved)


def block_backward(rows, params, length, allowed, across, upstream):
    gain, offset, entry, leave, bias, weigh, shift, widen, lift, narrow, nudge = params
    unused, saved = block_forward(rows, params, length, allowed, across)
    (
        normed_low,
        unit_one,
        inverse_one,
        mixed,
        kept,
        unit_two,
        inverse_two,
        second_low,
        gelu_pull,
        active_low,
    ) = saved
    branch_back = upstream.astype(HALF)
    nudge_change = column_sum(branch_back)
    narrow_change = weight_product(active_low, branch_back)
    active_back = transposed_product(branch_back, narrow)
    hidden_back = gelu_pull(active_back)[0].astype(HALF)
    lift_change = column_sum(hidden_back)
    widen_change = weight_product(second_low, hidden_back)
    second_back = transposed_product(hidden_back, widen)
    middle_norm, weigh_change, shift_change = norm_backward(
        second_back, unit_two, inverse_two, weigh
    )
    middle_back = upstream + middle_norm
    attend_back = middle_back.astype(HALF)
    bias_change = column_sum(attend_back)
    exit_change = weight_product(mixed, attend_back)
    mixed_back = transposed_product(attend_back, leave).astype(HALF)
    triple_back = attend_backward(mixed_back, length, across, kept)
    entry_change = weight_product(normed_low, triple_back)
    normed_back = transposed_product(triple_back, entry)
    rows_norm, gain_change, offset_change = norm_backward(normed_back, unit_one, inverse_one, gain)
    changes = (
        gain_change,
        offset_change,
        entry_change,
        exit_change,
        bias_change,
        weigh_change,
        shift_change,
        widen_change,
        lift_change,
        narrow_change,
        nudge_change,
    )
    return (middle_back + rows_norm, changes)


def frame_allowed(lengths, count):
    ends = jnp.cumsum(lengths)
    positions = jnp.arange(count, dtype=jnp.int32)
    video = jnp.sum((positions[:, None] >= ends[None, :]).astype(jnp.int32), axis=1)
    video = jnp.where(positions < ends[-1], video, lengths.shape[0] + positions)
    return (video[:, None] == video[None, :]) & (positions[None, :] <= positions[:, None])


def local(
    frames,
    space_gain,
    space_offset,
    space_entry,
    space_exit,
    space_bias,
    space_weigh,
    space_shift,
    space_widen,
    space_lift,
    space_narrow,
    space_nudge,
    time_gain,
    time_offset,
    time_entry,
    time_exit,
    time_bias,
    time_weigh,
    time_shift,
    time_widen,
    time_lift,
    time_narrow,
    time_nudge,
    cotangent,
    video_frames,
):
    spatial = (
        space_gain,
        space_offset,
        space_entry,
        space_exit,
        space_bias,
        space_weigh,
        space_shift,
        space_widen,
        space_lift,
        space_narrow,
        space_nudge,
    )
    temporal = (
        time_gain,
        time_offset,
        time_entry,
        time_exit,
        time_bias,
        time_weigh,
        time_shift,
        time_widen,
        time_lift,
        time_narrow,
        time_nudge,
    )
    count = frames.shape[1] * lax.axis_size("win")
    window_tokens = frames.shape[4]
    allowed = frame_allowed(video_frames[0], count)
    rows = frames.reshape(-1, D).astype(FLOAT)
    inner, unused = block_forward(rows, spatial, window_tokens, None, False)
    inner_low = inner.astype(HALF).reshape(frames.shape)
    arranged = lax.all_to_all(inner_low, "win", split_axis=3, concat_axis=2, tiled=True)
    middle_rows = arranged.reshape(-1, D).astype(FLOAT)
    outer, unused_too = block_forward(middle_rows, temporal, count, allowed, True)
    outer_low = outer.astype(HALF).reshape(arranged.shape)
    outcome = lax.all_to_all(outer_low, "win", split_axis=2, concat_axis=3, tiled=True)
    upstream = lax.all_to_all(cotangent, "win", split_axis=3, concat_axis=2, tiled=True)
    middle_back, time_changes = block_backward(
        middle_rows, temporal, count, allowed, True, upstream.reshape(-1, D).astype(FLOAT)
    )
    inner_back = middle_back.astype(HALF).reshape(arranged.shape)
    returned = lax.all_to_all(inner_back, "win", split_axis=2, concat_axis=3, tiled=True)
    rows_back, space_changes = block_backward(
        rows, spatial, window_tokens, None, False, returned.reshape(-1, D).astype(FLOAT)
    )
    shares = (
        lax.psum_scatter(
            space_changes[0].astype(jnp.bfloat16), "batch", scatter_dimension=0, tiled=True
        ).astype(jnp.float32),
        lax.psum_scatter(
            space_changes[1].astype(jnp.bfloat16), "batch", scatter_dimension=0, tiled=True
        ).astype(jnp.float32),
        lax.psum_scatter(
            space_changes[2].astype(jnp.bfloat16), "batch", scatter_dimension=0, tiled=True
        ).astype(jnp.float32),
        lax.psum_scatter(
            space_changes[3].astype(jnp.bfloat16), "batch", scatter_dimension=0, tiled=True
        ).astype(jnp.float32),
        lax.psum_scatter(
            space_changes[4].astype(jnp.bfloat16), "batch", scatter_dimension=0, tiled=True
        ).astype(jnp.float32),
        lax.psum_scatter(
            space_changes[5].astype(jnp.bfloat16), "batch", scatter_dimension=0, tiled=True
        ).astype(jnp.float32),
        lax.psum_scatter(
            space_changes[6].astype(jnp.bfloat16), "batch", scatter_dimension=0, tiled=True
        ).astype(jnp.float32),
        lax.psum_scatter(
            space_changes[7].astype(jnp.bfloat16), "batch", scatter_dimension=0, tiled=True
        ).astype(jnp.float32),
        lax.psum_scatter(
            space_changes[8].astype(jnp.bfloat16), "batch", scatter_dimension=0, tiled=True
        ).astype(jnp.float32),
        lax.psum_scatter(
            space_changes[9].astype(jnp.bfloat16), "batch", scatter_dimension=0, tiled=True
        ).astype(jnp.float32),
        lax.psum_scatter(
            space_changes[10].astype(jnp.bfloat16), "batch", scatter_dimension=0, tiled=True
        ).astype(jnp.float32),
        lax.psum_scatter(
            time_changes[0].astype(jnp.bfloat16), "batch", scatter_dimension=0, tiled=True
        ).astype(jnp.float32),
        lax.psum_scatter(
            time_changes[1].astype(jnp.bfloat16), "batch", scatter_dimension=0, tiled=True
        ).astype(jnp.float32),
        lax.psum_scatter(
            time_changes[2].astype(jnp.bfloat16), "batch", scatter_dimension=0, tiled=True
        ).astype(jnp.float32),
        lax.psum_scatter(
            time_changes[3].astype(jnp.bfloat16), "batch", scatter_dimension=0, tiled=True
        ).astype(jnp.float32),
        lax.psum_scatter(
            time_changes[4].astype(jnp.bfloat16), "batch", scatter_dimension=0, tiled=True
        ).astype(jnp.float32),
        lax.psum_scatter(
            time_changes[5].astype(jnp.bfloat16), "batch", scatter_dimension=0, tiled=True
        ).astype(jnp.float32),
        lax.psum_scatter(
            time_changes[6].astype(jnp.bfloat16), "batch", scatter_dimension=0, tiled=True
        ).astype(jnp.float32),
        lax.psum_scatter(
            time_changes[7].astype(jnp.bfloat16), "batch", scatter_dimension=0, tiled=True
        ).astype(jnp.float32),
        lax.psum_scatter(
            time_changes[8].astype(jnp.bfloat16), "batch", scatter_dimension=0, tiled=True
        ).astype(jnp.float32),
        lax.psum_scatter(
            time_changes[9].astype(jnp.bfloat16), "batch", scatter_dimension=0, tiled=True
        ).astype(jnp.float32),
        lax.psum_scatter(
            time_changes[10].astype(jnp.bfloat16), "batch", scatter_dimension=0, tiled=True
        ).astype(jnp.float32),
    )
    totals = (
        lax.psum(shares[0].astype(jnp.bfloat16), "win").astype(jnp.float32),
        lax.psum(shares[1].astype(jnp.bfloat16), "win").astype(jnp.float32),
        lax.psum(shares[2].astype(jnp.bfloat16), "win").astype(jnp.float32),
        lax.psum(shares[3].astype(jnp.bfloat16), "win").astype(jnp.float32),
        lax.psum(shares[4].astype(jnp.bfloat16), "win").astype(jnp.float32),
        lax.psum(shares[5].astype(jnp.bfloat16), "win").astype(jnp.float32),
        lax.psum(shares[6].astype(jnp.bfloat16), "win").astype(jnp.float32),
        lax.psum(shares[7].astype(jnp.bfloat16), "win").astype(jnp.float32),
        lax.psum(shares[8].astype(jnp.bfloat16), "win").astype(jnp.float32),
        lax.psum(shares[9].astype(jnp.bfloat16), "win").astype(jnp.float32),
        lax.psum(shares[10].astype(jnp.bfloat16), "win").astype(jnp.float32),
        lax.psum(shares[11].astype(jnp.bfloat16), "win").astype(jnp.float32),
        lax.psum(shares[12].astype(jnp.bfloat16), "win").astype(jnp.float32),
        lax.psum(shares[13].astype(jnp.bfloat16), "win").astype(jnp.float32),
        lax.psum(shares[14].astype(jnp.bfloat16), "win").astype(jnp.float32),
        lax.psum(shares[15].astype(jnp.bfloat16), "win").astype(jnp.float32),
        lax.psum(shares[16].astype(jnp.bfloat16), "win").astype(jnp.float32),
        lax.psum(shares[17].astype(jnp.bfloat16), "win").astype(jnp.float32),
        lax.psum(shares[18].astype(jnp.bfloat16), "win").astype(jnp.float32),
        lax.psum(shares[19].astype(jnp.bfloat16), "win").astype(jnp.float32),
        lax.psum(shares[20].astype(jnp.bfloat16), "win").astype(jnp.float32),
        lax.psum(shares[21].astype(jnp.bfloat16), "win").astype(jnp.float32),
    )
    space_total = totals[0:11]
    time_total = totals[11:22]
    frames_back = rows_back.astype(HALF).reshape(frames.shape)
    return (
        outcome,
        frames_back,
        space_total[0],
        space_total[1],
        space_total[2],
        space_total[3],
        space_total[4],
        space_total[5],
        space_total[6],
        space_total[7],
        space_total[8],
        space_total[9],
        space_total[10],
        time_total[0],
        time_total[1],
        time_total[2],
        time_total[3],
        time_total[4],
        time_total[5],
        time_total[6],
        time_total[7],
        time_total[8],
        time_total[9],
        time_total[10],
    )


def solution(mesh):
    placed = (
        P("batch", None, "win", None, None, None),
        P(),
        P(),
        P(),
        P(),
        P(),
        P(),
        P(),
        P(),
        P(),
        P(),
        P(),
        P(),
        P(),
        P(),
        P(),
        P(),
        P(),
        P(),
        P(),
        P(),
        P(),
        P(),
        P("batch", None, "win", None, None, None),
        P("batch", None),
    )
    return jax.shard_map(
        local,
        mesh=mesh,
        in_specs=placed,
        out_specs=(
            P("batch", None, "win", None, None, None),
            P("batch", None, "win", None, None, None),
            P("batch"),
            P("batch"),
            P("batch", None),
            P("batch", None),
            P("batch"),
            P("batch"),
            P("batch"),
            P("batch", None),
            P("batch"),
            P("batch", None),
            P("batch"),
            P("batch"),
            P("batch"),
            P("batch", None),
            P("batch", None),
            P("batch"),
            P("batch"),
            P("batch"),
            P("batch", None),
            P("batch"),
            P("batch", None),
            P("batch"),
        ),
        check_vma=False,
    )
```

profile of v0, /device:TPU:0, one launch (start us, length us, event | category | flops | bytes accessed | tf_op | source)
XLA Modules:
  0.0 1094.2 jit_solution(1764992404015609112)
XLA Ops:
  14.3 5.3 convolution_convert_fusion.1
  19.6 16.3 %reshape.390 = bf16[32,64,3,8,64]{4,3,2,1,0:T(8,128)(2,1)} reshape(bf16[2048,1536]{1,0:T(8,128)(2,1)} %convolution_convert_fusion.1) | data formatting | bytes 12582912 | tf_op jit(solution)/shard_map/reshape | solution.py:54
  35.9 7.1 fusion.91
  50.7 6.8 copy.218
  57.5 7.9 convert_bitcast_fusion.1
  65.5 6.8 copy.172
  72.2 6.5 reshape.391
  85.6 43.8 %multiply_convert_fusion.1 = (bf16[2048,2048]{1,0:T(8,128)(2,1)S(1)}, f32[2048,2048]{1,0:T(8,128)}, f32[2048,2048]{1,0:T(8,128)}) fusion(f32[2048]{0:T(1024)S(1)} %copy-done.77, bf16[512,2048]{1,0:T(8,128)(2,1)S(1)} %copy-done.72, f32[2048,512]{1,0:T(8,128)S(1)} %get-tuple-element.210, f32[512]{0:T(512)S(1)} %copy-done.84, f32[512]{0:T(512)S(1)} %copy-done.65, ...), kind=kOutput, calls=%fused_computation.23 | convolution fusion | flops 4577034240 | bytes 48263168 | tf_op jit(solution)/shard_map/dot_general | solution.py:110
  129.4 4.8 add_convert_fusion.4
  135.8 4.5 all-to-all-start
  145.0 21.6 %all-to-all-done = bf16[1,2,1,16,64,512]{5,4,1,2,0,3:T(8,128)(2,1)} async-done(((bf16[1,2,1,16,64,512]{5,4,1,2,0,3:T(8,128)(2,1)}), bf16[1,2,1,16,64,512]{5,4,1,2,0,3:T(8,128)(2,1)}, u32[]{:S(2)}, u32[]{:S(2)}) %all-to-all-start) | async-done | bytes 2097184 | tf_op jit(solution)/shard_map/all_to_all | solution.py:247
  166.6 4.5 all-to-all-start.2
  178.0 5.3 convolution_convert_fusion
  183.3 16.2 %reshape.405 = bf16[8,256,3,8,64]{4,3,2,1,0:T(8,128)(2,1)} reshape(bf16[2048,1536]{1,0:T(8,128)(2,1)} %convolution_convert_fusion) | data formatting | bytes 12582912 | tf_op jit(solution)/shard_map/reshape | solution.py:52
  199.6 23.7 %copy.242 = bf16[8,256,3,8,64]{4,0,3,1,2:T(8,128)(2,1)S(1)} copy(bf16[8,256,3,8,64]{4,3,2,1,0:T(8,128)(2,1)} %reshape.405) | data formatting | bytes 12582912 | tf_op jit(solution)/shard_map/reshape | solution.py:52
  223.2 4.5 copy-done.2
  227.7 5.5 fusion.71
  233.3 11.9 %fusion.94 = (f32[256,8,8]{2,1,0:T(8,128)S(1)}, f32[256,8,8,8]{2,3,1,0:T(8,128)S(1)}) fusion(f32[256,8,8,8]{2,3,1,0:T(8,128)} %fusion.71, pred[8,8]{0,1:T(8,128)(4,1)S(1)} %fusion.79), kind=kOutput, calls=%fused_computation.196 | output fusion | flops 786439 | bytes 1114176 | tf_op jit(solution)/shard_map/sub | solution.py:66
  248.7 6.4 convert_bitcast_fusion
  255.1 7.3 copy.178
  270.9 43.7 %multiply_convert_fusion = (bf16[2048,2048]{1,0:T(8,128)(2,1)}, f32[2048,2048]{1,0:T(8,128)}, f32[2048,2048]{1,0:T(8,128)}) fusion(f32[2048]{0:T(1024)S(1)} %copy-done.76, bf16[512,2048]{1,0:T(8,128)(2,1)S(1)} %copy-done, f32[2048,512]{1,0:T(8,128)S(1)} %get-tuple-element.215, f32[512]{0:T(512)S(1)} %copy-done.82, f32[512]{0:T(512)S(1)} %copy-done.64, ...), kind=kOutput, calls=%fused_computation.10 | convolution fusion | flops 4577034240 | bytes 48263168 | tf_op jit(solution)/shard_map/dot_general | solution.py:110
  317.8 22.1 %fusion.97 = (bf16[2048]{0:T(1024)(128)(2,1)}, bf16[2048,2048]{1,0:T(8,128)(2,1)}) fusion(f32[2048,2048]{1,0:T(8,128)} %get-tuple-element.201, bf16[2048,512]{1,0:T(8,128)(2,1)} %bitcast.233, bf16[2048,512]{1,0:T(8,128)(2,1)} %param.46, f32[2048,2048]{1,0:T(8,128)} %get-tuple-element.216, f32[2048]{0:T(1024)S(1)} %copy-done.76), kind=kOutput, calls=%fused_computation.199 | convolution fusion | flops 4362074112 | bytes 46149632 | tf_op jit(solution)/shard_map/dot_general | solution.py:43
  339.9 11.4 %multiply_reduce_fusion.3 = (bf16[512]{0:T(512)(128)(2,1)}, f32[2048]{0:T(1024)S(1)}, f32[2048]{0:T(1024)S(1)}, bf16[512]{0:T(512)(128)(2,1)}, f32[2048,512]{1,0:T(8,128)S(1)}) fusion(f32[2048,512]{1,0:T(8,128)} %copy-done.15, f32[2048]{0:T(1024)S(1)} %add_rsqrt_fusion.2, f32[2048]{0:T(1024)S(1)} %broadcast_multiply_fusion.10, f32[512]{0:T(512)S(1)} %copy-done.64, ...), kind=kOutput, calls=%fused_computation.111 | convolution fusion | flops 4304399360 | bytes 18911232 | tf_op jit(solution)/shard_map/dot_general | solution.py:43
  362.0 7.5 copy.184
  369.5 10.3 multiply_reduce_fusion.1
  379.7 8.7 multiply_convert_fusion.3
  388.4 6.5 multiply_bitcast_fusion.3
  394.9 7.7 multiply_bitcast_fusion.2
  402.6 9.0 convolution_bitcast_fusion.1
  411.7 11.2 %fusion.14 = bf16[8,256,3,8,64]{4,0,3,1,2:T(8,128)(2,1)} fusion(bf16[256,8,1,8,64]{4,1,3,0,2:T(8,128)(2,1)} %convolution_bitcast_fusion.1, bf16[256,8,1,8,64]{4,1,3,0,2:T(8,128)(2,1)} %multiply_bitcast_fusion.2, bf16[256,8,1,8,64]{4,1,3,0,2:T(8,128)(2,1)} %multiply_bitcast_fusion.3), kind=kLoop, calls=%fused_computation.38 | loop fusion | flops 6291456 | bytes 12582912 | tf_op jit(solution)/shard_map/convert_element_type | solution.py:98
  422.9 18.0 %copy.187 = bf16[8,256,3,8,64]{1,0,4,3,2:T(8,128)(2,1)} copy(bf16[8,256,3,8,64]{4,0,3,1,2:T(8,128)(2,1)} %fusion.14) | data formatting | bytes 12582912 | tf_op jit(solution)/shard_map/convert_element_type | solution.py:98
  440.9 5.6 copy.223
  446.6 8.1 fusion.37
  463.5 4.9 convolution_convert_fusion.10
  468.4 20.7 %all-to-all-done.3 = bf16[1,2,4,4,64,512]{5,4,3,1,0,2:T(8,128)(2,1)S(1)} async-done(((bf16[1,2,4,4,64,512]{5,4,3,1,0,2:T(8,128)(2,1)}), bf16[1,2,4,4,64,512]{5,4,3,1,0,2:T(8,128)(2,1)S(1)}, u32[]{:S(2)}, u32[]{:S(2)}) %all-to-all-start.3) | async-done | bytes 2097184 | tf_op jit(solution)/shard_map/all_to_all | solution.py:257
  490.8 21.9 %fusion.96 = (bf16[2048]{0:T(1024)(128)(2,1)S(1)}, bf16[2048,2048]{1,0:T(8,128)(2,1)}) fusion(f32[2048,2048]{1,0:T(8,128)} %get-tuple-element.203, bf16[2048,512]{1,0:T(8,128)(2,1)} %bitcast.235, bf16[2048,512]{1,0:T(8,128)(2,1)} %param.35, f32[2048,2048]{1,0:T(8,128)} %get-tuple-element.211, f32[2048]{0:T(1024)S(1)} %copy-done.78), kind=kOutput, calls=%fused_computation.198 | convolution fusion | flops 4362074112 | bytes 46149632 | tf_op jit(solution)/shard_map/dot_general | solution.py:43
  512.8 10.8 multiply_reduce_fusion.4
  532.0 7.5 convolution_convert_fusion.4
  540.0 11.0 %convolution_convert_fusion.3 = bf16[512,2048]{1,0:T(8,128)(2,1)} fusion(bf16[2048,2048]{1,0:T(8,128)(2,1)} %get-tuple-element.228, f32[2048,512]{1,0:T(8,128)} %copy-done.15, f32[512]{0:T(512)S(1)} %copy-done.83, f32[512]{0:T(512)S(1)} %copy-done.64, f32[2048]{0:T(1024)S(1)} %add_rsqrt_fusion.2, f32[2048]{0:T(1024)S(1)} %broadcast_multiply_fusion.10), kind=kOutput, calls=%fused_computation.148 | convolution fusion | flops 4301258752 | bytes 14700544 | tf_op jit(solution)/shard_map/dot_general | solution.py:39
  553.2 9.6 convolution_convert_fusion.2
  563.0 4.8 convolution_convert_fusion.8
  567.8 6.2 reshape.401
  574.0 6.8 copy.198
  580.9 11.3 %multiply_reduce_fusion = (f32[32,8,64]{2,1,0:T(8,128)S(1)}, f32[32,8,64,64]{2,3,1,0:T(8,128)}) fusion(f32[32,8,64,64]{2,3,1,0:T(8,128)} %get-tuple-element.208, f32[32,8,64]{2,1,0:T(8,128)S(1)} %copy-done.31, bf16[32,64,8,64]{1,3,2,0:T(8,128)(2,1)} %copy.198, bf16[32,64,1,8,64]{1,4,3,0,2:T(8,128)(2,1)} %copy.218), kind=kOutput, calls=%fused_computation.43 | convolution fusion | flops 137347072 | bytes 12713984 | tf_op jit(solution)/shard_map/gthd,gshd->ghts/dot_general | solution.py:83
  592.2 7.4 multiply_convert_fusion.2
  599.6 6.1 multiply_bitcast_fusion.1
  608.9 9.2 convolution_bitcast_fusion
  618.0 6.6 maximum_convert_fusion.1
  624.6 13.7 %copy.201 = bf16[32,64,3,8,64]{4,3,2,1,0:T(8,128)(2,1)} copy(bf16[32,64,3,8,64]{4,1,3,0,2:T(8,128)(2,1)S(1)} %maximum_convert_fusion.1) | data formatting | bytes 12582912 | tf_op jit(solution)/shard_map/convert_element_type | solution.py:98
  638.4 16.9 %convert_element_type.378 = bf16[2048,1536]{1,0:T(8,128)(2,1)} reshape(bf16[32,64,3,8,64]{4,3,2,1,0:T(8,128)(2,1)} %copy.201) | data formatting | bytes 12582912 | tf_op jit(solution)/shard_map/convert_element_type | solution.py:98
  655.3 8.1 convolution_convert_fusion.7
  663.4 9.9 convolution_convert_fusion.5
  673.6 11.0 %convolution_convert_fusion.6 = bf16[512,2048]{1,0:T(8,128)(2,1)} fusion(bf16[2048,2048]{1,0:T(8,128)(2,1)} %get-tuple-element.226, f32[2048,512]{1,0:T(8,128)} %copy-done.13, f32[512]{0:T(512)S(1)} %copy-done.85, f32[512]{0:T(512)S(1)} %copy-done.66, f32[2048]{0:T(1024)S(1)} %copy-done.53, f32[2048]{0:T(1024)S(1)} %copy-done.41), kind=kOutput, calls=%fused_computation.151 | convolution fusion | flops 4301258752 | bytes 14700544 | tf_op jit(solution)/shard_map/dot_general | solution.py:39
  684.6 9.9 add_convert_fusion.2
  696.2 4.6 all-to-all-start.1
  704.7 8.1 fusion.60
  712.9 23.1 %reduce-scatter.21.cloned.1.call-done = bf16[64,2048]{1,0:T(8,128)(2,1)} async-done(((bf16[512,2048]{1,0:T(8,128)(2,1)}), bf16[64,2048]{1,0:T(8,128)(2,1)}) %reduce-scatter.21.cloned.1.call-update) | async-done | bytes 262160 | tf_op jit(solution)/shard_map/reduce_scatter | solution.py:316
  736.1 70.8 %reduce-scatter.23.cloned.1.call-done = bf16[256,512]{1,0:T(8,128)(2,1)} async-done(((bf16[2048,512]{1,0:T(8,128)(2,1)}), bf16[256,512]{1,0:T(8,128)(2,1)}) %reduce-scatter.23.cloned.1.call-update) | async-done | bytes 262160 | tf_op jit(solution)/shard_map/reduce_scatter | solution.py:322
  806.9 67.5 %reduce-scatter.9.cloned.1.call-done = bf16[64,1536]{1,0:T(8,128)(2,1)} async-done(((bf16[512,1536]{1,0:T(8,128)(2,1)}), bf16[64,1536]{1,0:T(8,128)(2,1)}) %reduce-scatter.9.cloned.1.call-update) | async-done | bytes 196624 | tf_op jit(solution)/shard_map/reduce_scatter | solution.py:268
  874.4 70.3 %reduce-scatter.15.cloned.1.call-done = bf16[256,512]{1,0:T(8,128)(2,1)} async-done(((bf16[2048,512]{1,0:T(8,128)(2,1)}), bf16[256,512]{1,0:T(8,128)(2,1)}) %reduce-scatter.15.cloned.1.call-update) | async-done | bytes 262160 | tf_op jit(solution)/shard_map/reduce_scatter | solution.py:289
  944.7 71.0 %reduce-scatter.13.cloned.1.call-done = bf16[64,2048]{1,0:T(8,128)(2,1)} async-done(((bf16[512,2048]{1,0:T(8,128)(2,1)}), bf16[64,2048]{1,0:T(8,128)(2,1)}) %reduce-scatter.13.cloned.1.call-update) | async-done | bytes 262160 | tf_op jit(solution)/shard_map/reduce_scatter | solution.py:283
  1017.7 34.8 %all-reduce.14 = (bf16[512]{0:T(512)(128)(2,1)S(1)}, bf16[512]{0:T(512)(128)(2,1)S(1)}, bf16[512]{0:T(512)(128)(2,1)S(1)}, bf16[512]{0:T(512)(128)(2,1)S(1)}, bf...) all-reduce(bf16[512]{0:T(512)(128)(2,1)S(1)} %get-tuple-element.150, ...), channel_id=2, replica_groups=mesh['batch'=8,'win'=4] {'batch'}, use_global_device_ids=true, to_apply=%region_25.26.clone | all-reduce | flops 10240 | bytes 40960
  1053.6 6.4 all-reduce.15
  1070.6 4.7 fusion.59
  (305 shorter events, 115.2 us)
Async XLA Ops:
  7.2 263.7 %copy-start = (bf16[512,2048]{1,0:T(8,128)(2,1)S(1)}, bf16[512,2048]{1,0:T(8,128)(2,1)}, u32[]{:S(2)}) copy-start(bf16[512,2048]{1,0:T(8,128)(2,1)} %param.44) | copy-start | bytes 6291460
  9.3 10.2 copy-start.32
  11.9 7.7 copy-start.42
  11.9 7.7 copy-start.36
  12.0 7.6 copy-start.44
  82.4 47.0 %copy-start.13 = (f32[2048,512]{1,0:T(8,128)}, f32[2048,512]{1,0:T(8,128)S(1)}, u32[]{:S(2)}) copy-start(f32[2048,512]{1,0:T(8,128)S(1)} %get-tuple-element.210) | copy-start | bytes 12582916
  82.5 46.9 %copy-start.40 = (f32[2048]{0:T(1024)}, f32[2048]{0:T(1024)S(1)}, u32[]{:S(2)}) copy-start(f32[2048]{0:T(1024)S(1)} %broadcast_multiply_fusion.11) | copy-start | bytes 24580
  85.6 43.8 %copy-start.52 = (f32[2048]{0:T(1024)}, f32[2048]{0:T(1024)S(1)}, u32[]{:S(2)}) copy-start(f32[2048]{0:T(1024)S(1)} %add_rsqrt_fusion.3) | copy-start | bytes 24580
  85.6 43.8 %copy-start.71 = (bf16[2048,512]{1,0:T(8,128)(2,1)S(1)}, bf16[2048,512]{1,0:T(8,128)(2,1)}, u32[]{:S(2)}) copy-start(bf16[2048,512]{1,0:T(8,128)(2,1)} %param.35) | copy-start | bytes 6291460
  85.6 43.8 %copy-start.80 = (f32[512]{0:T(512)S(1)}, f32[512]{0:T(512)}, u32[]{:S(2)}) copy-start(f32[512]{0:T(512)} %param.36) | copy-start | bytes 6148
  135.8 30.8 %all-to-all-start = ((bf16[1,2,1,16,64,512]{5,4,1,2,0,3:T(8,128)(2,1)}), bf16[1,2,1,16,64,512]{5,4,1,2,0,3:T(8,128)(2,1)}, u32[]{:S(2)}, u32[]{:S(2)}) async-start(bf16[1,2,1,16,64,512]{5,4,1,2,0,3:T(8,128)(2,1)} %copy.173), calls=%async_computation | async-start | bytes 4194304 | tf_op jit(solution)/shard_map/all_to_all | solution.py:247
  145.0 30.7 %copy-start.54 = (f32[512]{0:T(512)S(1)}, f32[512]{0:T(512)}, u32[]{:S(2)}) copy-start(f32[512]{0:T(512)} %param.37) | copy-start | bytes 6148
  145.0 30.7 %copy-start.58 = (f32[512]{0:T(512)S(1)}, f32[512]{0:T(512)}, u32[]{:S(2)}) copy-start(f32[512]{0:T(512)} %param.38) | copy-start | bytes 6148
  166.6 148.0 %all-to-all-start.2 = ((bf16[1,2,1,16,64,512]{5,4,2,1,0,3:T(8,128)(2,1)}), bf16[1,2,1,16,64,512]{5,4,2,1,0,3:T(8,128)(2,1)}, u32[]{:S(2)}, u32[]{:S(2)}) async-start(bf16[1,2,1,16,64,512]{5,4,2,1,0,3:T(8,128)(2,1)} %copy.181), calls=%async_computation.2 | async-start | bytes 4194304 | tf_op jit(solution)/shard_map/all_to_all | solution.py:252
  173.0 10.3 copy-start.34
  173.1 10.2 copy-start.46
  175.6 7.7 copy-start.38
  175.7 7.6 copy-start.48
  339.9 11.4 %copy-start.16 = (f32[2048,512]{1,0:T(8,128)S(1)}, f32[2048,512]{1,0:T(8,128)}, u32[]{:S(2)}) copy-start(f32[2048,512]{1,0:T(8,128)} %copy-done.15) | copy-start | bytes 12582916
  339.9 11.4 %copy-start.18 = (bf16[1,2,1,16,64,512]{5,4,3,1,2,0:T(8,128)(2,1)S(1)}, bf16[1,2,1,16,64,512]{5,4,3,1,2,0:T(8,128)(2,1)}, u32[]{:S(2)}) copy-start(bf16[1,2,1,16,64,512]{5,4,3,1,2,0:T(8,128)(2,1)} %copy.182) | copy-start | bytes 6291460
  369.4 18.9 %slice-start = ((s8[12582912]{0:T(1024)(128)(4,1)}), s8[4194304]{0:T(1024)(128)(4,1)S(1)}, s32[]{:S(2)}) async-start(s8[12582912]{0:T(1024)(128)(4,1)} %bitcast.226), calls=%async_computation.21 | async-start | bytes 8388608
  369.5 18.9 %slice-start.1 = ((s8[12582912]{0:T(1024)(128)(4,1)}), s8[4194304]{0:T(1024)(128)(4,1)S(1)}, s32[]{:S(2)}) async-start(s8[12582912]{0:T(1024)(128)(4,1)} %bitcast.226), calls=%async_computation.22 | async-start | bytes 8388608
  379.7 8.7 slice-start.2
  446.6 8.1 copy-start.22
  446.6 8.1 copy-start.10
  459.8 29.3 %all-to-all-start.3 = ((bf16[1,2,4,4,64,512]{5,4,3,1,0,2:T(8,128)(2,1)}), bf16[1,2,4,4,64,512]{5,4,3,1,0,2:T(8,128)(2,1)S(1)}, u32[]{:S(2)}, u32[]{:S(2)}) async-start(bf16[1,2,4,4,64,512]{5,4,3,1,0,2:T(8,128)(2,1)} %copy.188), calls=%async_computation.3 | async-start | bytes 4194304 | tf_op jit(solution)/shard_map/all_to_all | solution.py:257
  463.4 249.5 %reduce-scatter.19.cloned.1.call-start = ((), (), s32[]{:S(2)}) async-start(), calls=%async_computation.17 | async-start | bytes 589824 | tf_op jit(solution)/shard_map/reduce_scatter | solution.py:304
  468.3 22.5 %copy-start.78 = (f32[2048]{0:T(1024)S(1)}, f32[2048]{0:T(1024)}, u32[]{:S(2)}) copy-start(f32[2048]{0:T(1024)} %param.34) | copy-start | bytes 24580
  468.4 244.5 %reduce-scatter.11.cloned.1.call-start = ((), (), s32[]{:S(2)}) async-start(), calls=%async_computation.13 | async-start | bytes 589824 | tf_op jit(solution)/shard_map/reduce_scatter | solution.py:271
  489.1 23.7 %copy-start.11 = (bf16[1,2,4,4,64,512]{5,4,3,1,0,2:T(8,128)(2,1)}, bf16[1,2,4,4,64,512]{5,4,3,1,0,2:T(8,128)(2,1)S(1)}, u32[]{:S(2)}) copy-start(bf16[1,2,4,4,64,512]{5,4,3,1,0,2:T(8,128)(2,1)S(1)} %all-to-all-done.3) | copy-start | bytes 6291460
  490.8 22.0 %copy-start.41 = (f32[2048]{0:T(1024)S(1)}, f32[2048]{0:T(1024)}, u32[]{:S(2)}) copy-start(f32[2048]{0:T(1024)} %copy-done.40) | copy-start | bytes 24580
  490.8 22.0 %copy-start.53 = (f32[2048]{0:T(1024)S(1)}, f32[2048]{0:T(1024)}, u32[]{:S(2)}) copy-start(f32[2048]{0:T(1024)} %copy-done.52) | copy-start | bytes 24580
  490.8 22.0 %copy-start.66 = (f32[512]{0:T(512)S(1)}, f32[512]{0:T(512)}, u32[]{:S(2)}) copy-start(f32[512]{0:T(512)} %param.31) | copy-start | bytes 6148
  512.8 10.8 copy-start.14
  512.8 10.8 copy-start.20
  529.7 183.2 %reduce-scatter.17.cloned.1.call-start = ((), (), s32[]{:S(2)}) async-start(), calls=%async_computation.16 | async-start | bytes 1769472 | tf_op jit(solution)/shard_map/reduce_scatter | solution.py:301
  532.0 8.1 copy-start.83
  539.5 11.6 %copy-start.5 = (bf16[1,2,1,16,64,512]{5,4,3,2,1,0:T(8,128)(2,1)S(1)}, bf16[1,2,1,16,64,512]{5,4,3,2,1,0:T(8,128)(2,1)}, u32[]{:S(2)}) copy-start(bf16[1,2,1,16,64,512]{5,4,3,2,1,0:T(8,128)(2,1)} %param.25) | copy-start | bytes 6291460
  539.5 11.6 %copy-start.33 = (f32[2,16,64]{2,1,0:T(8,128)S(1)}, f32[2,16,64]{2,1,0:T(8,128)}, u32[]{:S(2)}) copy-start(f32[2,16,64]{2,1,0:T(8,128)} %copy-done.32) | copy-start | bytes 24580
  539.5 11.6 %copy-start.37 = (f32[2,16,64]{2,1,0:T(8,128)S(1)}, f32[2,16,64]{2,1,0:T(8,128)}, u32[]{:S(2)}) copy-start(f32[2,16,64]{2,1,0:T(8,128)} %copy-done.36) | copy-start | bytes 24580
  539.6 11.6 %copy-start.57 = (f32[512]{0:T(512)S(1)}, f32[512]{0:T(512)}, u32[]{:S(2)}) copy-start(f32[512]{0:T(512)} %param.26) | copy-start | bytes 6148
  539.6 11.6 %copy-start.61 = (f32[512]{0:T(512)S(1)}, f32[512]{0:T(512)}, u32[]{:S(2)}) copy-start(f32[512]{0:T(512)} %param.27) | copy-start | bytes 6148
  539.6 196.5 %reduce-scatter.21.cloned.1.call-start = ((), (), s32[]{:S(2)}) async-start(), calls=%async_computation.18 | async-start | bytes 2359296 | tf_op jit(solution)/shard_map/reduce_scatter | solution.py:316
  551.1 255.8 %reduce-scatter.23.cloned.1.call-start = ((), (), s32[]{:S(2)}) async-start(), calls=%async_computation.19 | async-start | bytes 2359296 | tf_op jit(solution)/shard_map/reduce_scatter | solution.py:322
  553.2 9.8 copy-start.29
  562.8 311.6 %reduce-scatter.9.cloned.1.call-start = ((), (), s32[]{:S(2)}) async-start(), calls=%async_computation.12 | async-start | bytes 1769472 | tf_op jit(solution)/shard_map/reduce_scatter | solution.py:268
  608.9 9.2 copy-start.12
  663.3 10.3 copy-start.85
  663.4 281.3 %reduce-scatter.15.cloned.1.call-start = ((), (), s32[]{:S(2)}) async-start(), calls=%async_computation.15 | async-start | bytes 2359296 | tf_op jit(solution)/shard_map/reduce_scatter | solution.py:289
  673.3 11.3 %copy-start.86 = (f32[512]{0:T(512)S(1)}, f32[512]{0:T(512)}, u32[]{:S(2)}) copy-start(f32[512]{0:T(512)} %param.47) | copy-start | bytes 6148
  673.3 342.3 %reduce-scatter.13.cloned.1.call-start = ((), (), s32[]{:S(2)}) async-start(), calls=%async_computation.14 | async-start | bytes 2359296 | tf_op jit(solution)/shard_map/reduce_scatter | solution.py:283
  696.2 8.5 copy-start.43
  696.2 8.5 copy-start.45
  696.2 371.1 %all-to-all-start.1 = ((bf16[1,2,4,4,64,512]{5,4,3,1,0,2:T(8,128)(2,1)}), bf16[1,2,4,4,64,512]{5,4,3,1,0,2:T(8,128)(2,1)}, u32[]{:S(2)}, u32[]{:S(2)}) async-start(bf16[1,2,4,4,64,512]{5,4,3,1,0,2:T(8,128)(2,1)} %copy.179), calls=%async_computation.1 | async-start | bytes 4194304 | tf_op jit(solution)/shard_map/all_to_all | solution.py:251
  700.8 374.5 %all-reduce.19.cloned.1.call-start = ((), (), s32[]{:S(2)}) async-start(), calls=%async_computation.20 | async-start | bytes 3145728 | tf_op jit(solution)/shard_map/psum | solution.py:332
  704.7 313.0 %copy-start.62 = (bf16[512]{0:T(512)(128)(2,1)S(1)}, bf16[512]{0:T(512)(128)(2,1)}, u32[]{:S(2)}) copy-start(bf16[512]{0:T(512)(128)(2,1)} %get-tuple-element.196) | copy-start | bytes 3076
  704.7 313.0 %copy-start.63 = (bf16[2048]{0:T(1024)(128)(2,1)S(1)}, bf16[2048]{0:T(1024)(128)(2,1)}, u32[]{:S(2)}) copy-start(bf16[2048]{0:T(1024)(128)(2,1)} %get-tuple-element.227) | copy-start | bytes 12292
  704.7 313.0 %copy-start.67 = (bf16[512]{0:T(512)(128)(2,1)S(1)}, bf16[512]{0:T(512)(128)(2,1)}, u32[]{:S(2)}) copy-start(bf16[512]{0:T(512)(128)(2,1)} %get-tuple-element.144) | copy-start | bytes 3076
  704.7 313.0 %copy-start.68 = (bf16[512]{0:T(512)(128)(2,1)S(1)}, bf16[512]{0:T(512)(128)(2,1)}, u32[]{:S(2)}) copy-start(bf16[512]{0:T(512)(128)(2,1)} %get-tuple-element.156) | copy-start | bytes 3076
  704.7 313.0 %copy-start.69 = (bf16[512]{0:T(512)(128)(2,1)S(1)}, bf16[512]{0:T(512)(128)(2,1)}, u32[]{:S(2)}) copy-start(bf16[512]{0:T(512)(128)(2,1)} %get-tuple-element.148) | copy-start | bytes 3076
  704.7 313.0 %copy-start.70 = (bf16[512]{0:T(512)(128)(2,1)S(1)}, bf16[512]{0:T(512)(128)(2,1)}, u32[]{:S(2)}) copy-start(bf16[512]{0:T(512)(128)(2,1)} %get-tuple-element.157) | copy-start | bytes 3076
  1070.6 16.7 %copy-start.1 = (bf16[512,2048]{1,0:T(8,128)(2,1)S(1)}, bf16[512,2048]{1,0:T(8,128)(2,1)}, u32[]{:S(2)}) copy-start(bf16[512,2048]{1,0:T(8,128)(2,1)} %param.44) | copy-start | bytes 6291460
  1075.3 10.6 copy-start.51
  1075.3 11.3 %copy-start.50 = (bf16[64,512]{1,0:T(8,128)(2,1)S(1)}, bf16[64,512]{1,0:T(8,128)(2,1)}, u32[]{:S(2)}) copy-start(bf16[64,512]{1,0:T(8,128)(2,1)} %get-tuple-element.193) | copy-start | bytes 196612
  (42 other events, 173.0 us)
Sparse Core Ops, SparseCore 0:
  468.5 64.5 reduce-scatter.18
  537.3 60.9 reduce-scatter.10
  601.7 63.8 reduce-scatter.16
  669.4 66.6 reduce-scatter.20
  739.9 66.9 reduce-scatter.22
  810.5 63.7 reduce-scatter.8
  877.9 66.7 reduce-scatter.14
  948.8 66.8 reduce-scatter.12
  1018.5 43.3 all-reduce.18
where the time goes:
time: 1110 us; the launch traced here: 1090 us
  matrix products  356 us (32%)
  waiting for transfers between devices  345 us (31%)
  local copies, waits for them, and re-layouts  210 us (19%)
  other arithmetic  107 us (10%)
  blocking collectives  41.3 us (4%)
  starting transfers between devices  18.4 us (2%)
  between operations  16.8 us (2%)
    dot_general x8, matrix products, transposed_product(): lax.dot_general(incoming, weight, (((1,), (1,)), ((), ())), preferred_ele...  88.5 us
    dot_general x2, matrix products, block_forward(): hidden = jnp.dot(second_low, widen, preferred_element_type=FLOAT) + lift  87.5 us
    reduce_scatter x1, waiting for transfers between devices, local(): lax.psum_scatter(space_changes[7].astype(jnp.bfloat16), 'batch', scatter_...  71 us
    reduce_scatter x1, waiting for transfers between devices, local(): lax.psum_scatter(time_changes[9].astype(jnp.bfloat16), 'batch', scatter_d...  70.8 us
    reduce_scatter x1, waiting for transfers between devices, local(): lax.psum_scatter(space_changes[9].astype(jnp.bfloat16), 'batch', scatter_...  70.3 us
    reduce_scatter x1, waiting for transfers between devices, local(): lax.psum_scatter(space_changes[2].astype(jnp.bfloat16), 'batch', scatter_...  67.5 us
    dot_general x8, matrix products, weight_product(): lax.dot_general(left, right, (((0,), (0,)), ((), ())), preferred_element_...  63.9 us
    convert_element_type x3, local copies, waits for them, and re-layouts, attend_backward(): return stacked.reshape(-1, 3 * HEADS * HDIM).astype(HALF)  48.6 us
  transfers between devices with their start and end apart: 13, of which 7 were waited for; matrix products, arithmetic and copies ran while one was open for 34% of the time, Pallas kernels for 0%

commit v1 on v0

v1 whole, which is shorter than its diff:
```python
import functools

import jax
import jax.numpy as jnp
from jax import lax
from jax.experimental import pallas as pl
from jax.experimental.pallas import tpu as pltpu
from jax.sharding import PartitionSpec as P

D = 512
HEADS = 8
HDIM = 64
FF = 2048
PAIR = 2 * HDIM
PAIRS = HEADS // 2
CHUNK = 512
CHUNKS = FF // CHUNK
EPS = 1e-05
NEGATIVE = -1e30
FLOAT = jnp.float32
HALF = jnp.bfloat16
HALVES = 2
UNITS = 16
VMEM = 40 << 20

NORMED, MIXED, SECOND, ACTIVE = 0, 1, 2, 3
LEFTS = 3 + CHUNKS
TRIPLE_BACK, ATTEND_BACK, HIDDEN_BACK, BRANCH_BACK = 0, 3, 4, 4 + CHUNKS
RIGHTS = 5 + CHUNKS
GAIN, OFFSET, BIAS, WEIGH, SHIFT, NUDGE, LIFT = 0, 1, 2, 3, 4, 5, 6
SUMS = 6 + CHUNKS


def dot(left, right):
    return lax.dot_general(left, right, (((1,), (0,)), ((), ())), preferred_element_type=FLOAT)


def dot_right(left, right):
    return lax.dot_general(left, right, (((1,), (1,)), ((), ())), preferred_element_type=FLOAT)


def dot_left(left, right):
    return lax.dot_general(left, right, (((0,), (0,)), ((), ())), preferred_element_type=FLOAT)


def unit_of(rows):
    centre = rows - jnp.mean(rows, axis=-1, keepdims=True)
    inverse = lax.rsqrt(jnp.mean(centre * centre, axis=-1, keepdims=True) + EPS)
    return centre * inverse, inverse


def norm_back(scaled, unit, inverse):
    return inverse * (
        scaled
        - jnp.mean(scaled, axis=-1, keepdims=True)
        - unit * jnp.mean(scaled * unit, axis=-1, keepdims=True)
    )


def gelu_pair(hidden):
    half = 0.5 * lax.erf(hidden * 0.7071067811865476) + 0.5
    bell = jnp.exp(hidden * hidden * -0.5) * 0.3989422804014327
    return hidden * half, half + hidden * bell


def column_sum(values):
    return jnp.sum(values, axis=0, keepdims=True)


def first_head(rows):
    return lax.broadcasted_iota(jnp.int32, (rows, PAIR), 1) < HDIM


def spread(pair, first):
    zero = jnp.zeros_like(pair)
    return jnp.concatenate([jnp.where(first, pair, zero), jnp.where(first, zero, pair)], axis=0)


def gathered(both, first, rows):
    return jnp.where(first, both[:rows], both[rows:])


def attend_units(blocks):
    units = [(block, pair) for block in range(blocks) for pair in range(PAIRS)]
    return [units[start : start + UNITS] for start in range(0, len(units), UNITS)]


def columns(pair, part=0):
    start = part * D + pair * PAIR
    return slice(start, start + PAIR)


def attend_forward(triple, mixed, weights, blocks, rows, mask):
    first = first_head(rows)
    for units in attend_units(blocks):
        spans = [slice(block * rows, block * rows + rows) for block, _ in units]
        queries = [spread(triple[s, columns(p)], first) for s, (_, p) in zip(spans, units)]
        scores = [dot_right(triple[s, columns(p, 1)], q) for q, s, (_, p) in zip(queries, spans, units)]
        if mask is not None:
            scores = [score + mask for score in scores]
        powers = [
            jnp.exp((score - jnp.max(score, axis=0, keepdims=True)) * HDIM ** (-0.5)) for score in scores
        ]
        probs = [
            (power * (1.0 / jnp.sum(power, axis=0, keepdims=True))).astype(HALF) for power in powers
        ]
        both = [dot_left(prob, triple[s, columns(p, 2)]) for prob, s, (_, p) in zip(probs, spans, units)]
        for value, prob, s, (block, p) in zip(both, probs, spans, units):
            weights[block, p] = prob
            mixed[s, columns(p)] = gathered(value, first, rows).astype(HALF)


def attend_backward(triple, weights, mixed_back, put, blocks, rows):
    first = first_head(rows)
    scale = HDIM ** (-0.5)
    for units in attend_units(blocks):
        spans = [slice(block * rows, block * rows + rows) for block, _ in units]
        mixes = [spread(mixed_back[s, columns(p)], first) for s, (_, p) in zip(spans, units)]
        probs = [weights[block, p] for block, p in units]
        values_back = [dot(prob, mix) for prob, mix in zip(probs, mixes)]
        weights_back = [
            dot_right(triple[s, columns(p, 2)], mix) for mix, s, (_, p) in zip(mixes, spans, units)
        ]
        scores_back = []
        for prob, back in zip(probs, weights_back):
            wide = prob.astype(FLOAT)
            inside = back - jnp.sum(back * wide, axis=0, keepdims=True)
            scores_back.append((wide * inside * scale).astype(HALF))
        queries = [spread(triple[s, columns(p)], first) for s, (_, p) in zip(spans, units)]
        keys_back = [dot(score, query) for score, query in zip(scores_back, queries)]
        both = [
            dot_left(score, triple[s, columns(p, 1)])
            for score, s, (_, p) in zip(scores_back, spans, units)
        ]
        for key, value, pair, s, (_, p) in zip(keys_back, values_back, both, spans, units):
            put(s, p, 0, gathered(pair, first, rows).astype(HALF))
            put(s, p, 1, key.astype(HALF))
            put(s, p, 2, value.astype(HALF))


def whole(shape):
    return pl.BlockSpec(shape, lambda *_: (0,) * len(shape), pipeline_mode=pl.Buffered(1))


def run(body, name, grid, scalars, ins, outs, scratch=(), aliases=None, after=(), flops=0, moved=0):
    aliases = aliases or {}
    anywhere = pl.BlockSpec(memory_space=pl.ANY)
    first = len(scalars) + len(ins)
    extra = [*aliases.values(), *after]

    def inner(*refs):
        body(*refs[:first], *refs[first + len(extra) :])

    return pl.pallas_call(
        inner,
        out_shape=[jax.ShapeDtypeStruct(shape, kind) for shape, kind, _ in outs],
        grid_spec=pltpu.PrefetchScalarGridSpec(
            num_scalar_prefetch=len(scalars),
            grid=grid,
            in_specs=[spec for _, spec in ins] + [anywhere] * len(extra),
            out_specs=[spec for _, _, spec in outs],
            scratch_shapes=list(scratch),
        ),
        input_output_aliases={first + at: out for at, out in enumerate(aliases)},
        compiler_params=pltpu.CompilerParams(vmem_limit_bytes=VMEM),
        cost_estimate=pl.CostEstimate(flops=flops, bytes_accessed=moved, transcendentals=0),
        name=name,
    )(*scalars, *[array for array, _ in ins], *extra)


def plain(arrays):
    return [(array, whole(array.shape)) for array in arrays]


def slab_spec(slabs, rows, at):
    return pl.BlockSpec((slabs, rows, D), lambda *i: (0, at(*i), 0))


def row_spec(rows, width, at):
    return pl.BlockSpec((rows, width), lambda *i: (at(*i), 0))


def space_forward_body(place, rows_in, cotangent, *refs, window, pieces):
    gain, offset, entry, leave, bias, weigh, shift, widen, lift, narrow, nudge = refs[:11]
    inners, cuts = refs[11 : 11 + pieces], refs[11 + pieces : 11 + 2 * pieces]
    lefts, triple, weights, middles, slopes = refs[11 + 2 * pieces :]
    step = pl.program_id(0)
    shape = rows_in.shape
    rows = rows_in[...].reshape(-1, D).astype(FLOAT)
    count = rows.shape[0]
    unit, _ = unit_of(rows)
    normed = (unit * gain[...] + offset[...]).astype(HALF)
    lefts[NORMED] = normed
    triple[...] = dot(normed, entry[...]).astype(HALF)
    attend_forward(triple, lefts.at[MIXED], weights, count // window, window, None)
    middle = rows + dot(lefts[MIXED], leave[...]) + bias[...]
    middles[...] = middle
    unit_two, _ = unit_of(middle)
    second = (unit_two * weigh[...] + shift[...]).astype(HALF)
    lefts[SECOND] = second
    total = middle + nudge[...]
    for chunk in range(CHUNKS):
        at = slice(chunk * CHUNK, (chunk + 1) * CHUNK)
        active, slope = gelu_pair(dot(second, widen[:, at]) + lift[:, at])
        active = active.astype(HALF)
        lefts[ACTIVE + chunk] = active
        slopes[:, at] = slope.astype(HALF)
        total = total + dot(active, narrow[at, :])
    inner = total.astype(HALF).reshape(shape)
    for piece in range(pieces):

        @pl.when(step == piece)
        def _(piece=piece):
            inners[piece][...] = inner
            cuts[piece][...] = cotangent[...]


def space_forward(place, frames, cotangent, params, half, pieces, before):
    per_group, windows, window, _ = frames.shape
    each = windows // pieces // HALVES
    block = (per_group, each, window, D)
    rows = per_group * each * window
    count = rows * pieces * HALVES
    cut = pl.BlockSpec(block, lambda i, place: (0, (place[0] ^ i) * HALVES + half, 0, 0))
    at = lambda i, place: half * pieces + i
    attended = (rows // window, PAIRS, window, 2 * window)
    outs = [(block, HALF, pl.BlockSpec(block, lambda i, place: (0, 0, 0, 0)))] * (2 * pieces)
    outs += [
        ((LEFTS, count, D), HALF, slab_spec(LEFTS, rows, at)),
        ((count, 3 * D), HALF, row_spec(rows, 3 * D, at)),
        (
            (count // window, *attended[1:]),
            HALF,
            pl.BlockSpec(attended, lambda i, place: (at(i, place), 0, 0, 0)),
        ),
        ((count, D), FLOAT, row_spec(rows, D, at)),
        ((count, FF), HALF, row_spec(rows, FF, at)),
    ]
    made = run(
        functools.partial(space_forward_body, window=window, pieces=pieces),
        "space_forward",
        (pieces,),
        [place],
        [(frames, cut), (cotangent, cut)] + plain(params),
        outs,
        aliases={2 * pieces + number: array for number, array in enumerate(before)},
        flops=2 * rows * pieces * D * (4 * D + 2 * FF),
        moved=rows * pieces * (8 * D + 2 * LEFTS * D + 10 * D + 4 * D + 2 * FF),
    )
    return made[:pieces], made[pieces : 2 * pieces], made[2 * pieces :]


def by_position(refs, frames_of, positions):
    parts = [ref[frame].astype(FLOAT) for ref in refs for frame in range(frames_of)]
    return jnp.concatenate(
        [part[start : start + 8] for start in range(0, positions, 8) for part in parts], axis=0
    )


def by_frame(values, refs, frames_of, positions):
    total = len(refs) * frames_of
    for at, ref in enumerate(refs):
        for frame in range(frames_of):
            number = at * frames_of + frame
            ref[frame] = jnp.concatenate(
                [
                    values[(group * total + number) * 8 : (group * total + number) * 8 + 8]
                    for group in range(positions // 8)
                ],
                axis=0,
            ).astype(HALF)


def fill_mask(mask, place, lengths, per_group, pieces):
    window = mask.shape[0]
    key = lax.broadcasted_iota(jnp.int32, mask.shape, 0)
    query = lax.broadcasted_iota(jnp.int32, mask.shape, 1) % window
    frames = []
    for row in (query, key):
        number = row // 8
        frames.append((number % per_group) * pieces + ((number // per_group) ^ place[0]))
    videos = [jnp.zeros_like(frame) for frame in frames]
    entries = lengths.shape[1]
    end = 0
    for entry in range(entries):
        end = end + lengths[0, entry]
        videos = [v + (f >= end).astype(jnp.int32) for v, f in zip(videos, frames)]
    videos = [jnp.where(f < end, v, entries + f) for v, f in zip(videos, frames)]
    allowed = (videos[0] == videos[1]) & (frames[1] <= frames[0]) & (query % 8 == key % 8)
    mask[...] = jnp.where(allowed, 0.0, NEGATIVE)


def time_body(place, lengths, *refs, pieces):
    inners, cotangents = refs[:pieces], refs[pieces : 2 * pieces]
    gain, offset, entry, leave, bias, weigh, shift, widen, lift, narrow, nudge = refs[
        2 * pieces : 2 * pieces + 11
    ]
    refs = refs[2 * pieces + 11 :]
    results, backs = refs[:pieces], refs[pieces : 2 * pieces]
    lefts, rights, sums, triple, weights, mixed_back, mask = refs[2 * pieces :]
    frames_of, positions, _ = inners[0].shape
    window = 8 * pieces * frames_of
    rows = by_position(inners, frames_of, positions)
    blocks = rows.shape[0] // window

    @pl.when(pl.program_id(0) == 0)
    def _():
        sums[...] = jnp.zeros_like(sums)
        fill_mask(mask, place, lengths, frames_of, pieces)

    unit, inverse = unit_of(rows)
    normed = (unit * gain[...] + offset[...]).astype(HALF)
    lefts[NORMED] = normed
    triple[...] = dot(normed, entry[...]).astype(HALF)
    attend_forward(triple, lefts.at[MIXED], weights, blocks, window, mask[...])
    middle = rows + dot(lefts[MIXED], leave[...]) + bias[...]
    unit_two, inverse_two = unit_of(middle)
    second = (unit_two * weigh[...] + shift[...]).astype(HALF)
    lefts[SECOND] = second
    upstream = by_position(cotangents, frames_of, positions)
    branch_back = upstream.astype(HALF)
    rights[BRANCH_BACK] = branch_back
    sums[NUDGE] += column_sum(upstream)
    total = middle + nudge[...]
    second_back = jnp.zeros_like(middle)
    for chunk in range(CHUNKS):
        at = slice(chunk * CHUNK, (chunk + 1) * CHUNK)
        active, slope = gelu_pair(dot(second, widen[:, at]) + lift[:, at])
        active = active.astype(HALF)
        lefts[ACTIVE + chunk] = active
        hidden_back = dot_right(branch_back, narrow[at, :]) * slope
        hidden_low = hidden_back.astype(HALF)
        rights[HIDDEN_BACK + chunk] = hidden_low
        sums[LIFT + chunk] += column_sum(hidden_back)
        total = total + dot(active, narrow[at, :])
        second_back = second_back + dot_right(hidden_low, widen[:, at])
    by_frame(total, results, frames_of, positions)
    sums[WEIGH] += column_sum(second_back * unit_two)
    sums[SHIFT] += column_sum(second_back)
    middle_back = upstream + norm_back(second_back * weigh[...], unit_two, inverse_two)
    attend_back = middle_back.astype(HALF)
    rights[ATTEND_BACK] = attend_back
    sums[BIAS] += column_sum(middle_back)
    mixed_back[...] = dot_right(attend_back, leave[...]).astype(HALF)

    def put(span, pair, part, value):
        rights[TRIPLE_BACK + part, span, columns(pair)] = value

    attend_backward(triple, weights, mixed_back, put, blocks, window)
    normed_back = jnp.zeros_like(middle)
    for part in range(3):
        normed_back = normed_back + dot_right(
            rights[TRIPLE_BACK + part], entry[:, part * D : (part + 1) * D]
        )
    sums[GAIN] += column_sum(normed_back * unit)
    sums[OFFSET] += column_sum(normed_back)
    rows_back = middle_back + norm_back(normed_back * gain[...], unit, inverse)
    by_frame(rows_back, backs, frames_of, positions)


def time_block(place, lengths, inners, cotangents, params, half, before, step_rows=256):
    pieces = len(inners)
    per_group, each, window, _ = inners[0].shape
    positions = each * window
    flat = (per_group, positions, D)
    frames = per_group * pieces
    batch = min(max(step_rows // frames, 16), positions)
    rows = batch * frames
    steps = positions // batch
    count = positions * frames
    attended = 8 * frames
    spec = pl.BlockSpec((per_group, batch, D), lambda i, *_: (0, i, 0))
    at = lambda i, *_: half * steps + i
    outs = [(flat, HALF, spec)] * (2 * pieces)
    outs += [
        ((LEFTS, HALVES * count, D), HALF, slab_spec(LEFTS, rows, at)),
        ((RIGHTS, HALVES * count, D), HALF, slab_spec(RIGHTS, rows, at)),
        ((SUMS, 1, D), FLOAT, whole((SUMS, 1, D))),
    ]
    made = run(
        functools.partial(time_body, pieces=pieces),
        "time_block",
        (steps,),
        [place, lengths],
        [(array.reshape(flat), spec) for array in (*inners, *cotangents)] + plain(params),
        outs,
        scratch=[
            pltpu.VMEM((rows, 3 * D), HALF),
            pltpu.VMEM((rows // attended, PAIRS, attended, 2 * attended), HALF),
            pltpu.VMEM((rows, D), HALF),
            pltpu.VMEM((attended, 2 * attended), FLOAT),
        ],
        aliases={2 * pieces + number: array for number, array in enumerate(before)},
        flops=4 * count * D * (4 * D + 2 * FF),
        moved=count * 2 * D * (4 + LEFTS + RIGHTS) + 2 * D * (4 * D + 2 * FF),
    )
    shape = (per_group, each, window, D)
    results = [array.reshape(shape) for array in made[:pieces]]
    backs = [array.reshape(shape) for array in made[pieces : 2 * pieces]]
    return results, backs, made[2 * pieces : 2 * pieces + 2], made[2 * pieces + 2]


def feed_back_body(place, *refs, pieces):
    weigh, widen, narrow = refs[:3]
    backs, results = refs[3 : 3 + pieces], refs[3 + pieces : 3 + 2 * pieces]
    middles, slopes, outcome, rights, middles_back, sums, upstream_low = refs[3 + 2 * pieces :]
    step = pl.program_id(0)

    @pl.when(step == 0)
    def _():
        sums[...] = jnp.zeros_like(sums)

    for piece in range(pieces):

        @pl.when(step == piece)
        def _(piece=piece):
            upstream_low[...] = backs[piece][...].reshape(-1, D)
            outcome[...] = results[piece][...]

    branch_back = upstream_low[...]
    rights[4] = branch_back
    upstream = branch_back.astype(FLOAT)
    sums[NUDGE] += column_sum(upstream)
    second_back = jnp.zeros_like(upstream)
    for chunk in range(CHUNKS):
        at = slice(chunk * CHUNK, (chunk + 1) * CHUNK)
        hidden_back = dot_right(branch_back, narrow[at, :]) * slopes[:, at].astype(FLOAT)
        hidden_low = hidden_back.astype(HALF)
        rights[chunk] = hidden_low
        sums[LIFT + chunk] += column_sum(hidden_back)
        second_back = second_back + dot_right(hidden_low, widen[:, at])
    unit_two, inverse_two = unit_of(middles[...])
    sums[WEIGH] += column_sum(second_back * unit_two)
    sums[SHIFT] += column_sum(second_back)
    middle_back = upstream + norm_back(second_back * weigh[...], unit_two, inverse_two)
    middles_back[...] = middle_back
    sums[BIAS] += column_sum(middle_back)


def feed_back(place, shape, params, backs, results, middles, slopes, after):
    pieces = len(backs)
    per_group, windows, window, _ = shape
    block = backs[0].shape
    rows = per_group * block[1] * window
    count = rows * pieces
    across = pieces // HALVES
    cut = pl.BlockSpec(block, lambda i, place: (0, (place[0] ^ (i % across)) * HALVES + i // across, 0, 0))
    at = lambda i, place: i
    ins = plain([params[5], params[7], params[9]]) + plain(backs) + plain(results)
    ins += [(middles, row_spec(rows, D, at)), (slopes, row_spec(rows, FF, at))]
    return run(
        functools.partial(feed_back_body, pieces=pieces),
        "feed_back",
        (pieces,),
        [place],
        ins,
        [
            (shape, HALF, cut),
            ((CHUNKS + 1, count, D), HALF, slab_spec(CHUNKS + 1, rows, at)),
            ((count, D), FLOAT, row_spec(rows, D, at)),
            ((SUMS, 1, D), FLOAT, whole((SUMS, 1, D))),
        ],
        scratch=[pltpu.VMEM((rows, D), HALF)],
        after=after,
        flops=4 * count * D * FF,
        moved=count * (8 * D + 2 * (CHUNKS + 1) * D + 8 * D + 2 * FF),
    )


def attention_back_body(place, rows_in, gain, entry, leave, triple, weights, middles_back, *refs, window):
    delta, rights, sums, mixed_back = refs
    step = pl.program_id(0)

    @pl.when(step == 0)
    def _():
        sums[...] = jnp.zeros_like(sums)

    shape = rows_in.shape
    middle_back = middles_back[...]
    attend_back = middle_back.astype(HALF)
    rights[3] = attend_back
    mixed_back[...] = dot_right(attend_back, leave[...]).astype(HALF)

    def put(span, pair, part, value):
        rights[part, span, columns(pair)] = value

    attend_backward(triple, weights, mixed_back, put, middle_back.shape[0] // window, window)
    normed_back = jnp.zeros_like(middle_back)
    for part in range(3):
        normed_back = normed_back + dot_right(rights[part], entry[:, part * D : (part + 1) * D])
    unit, inverse = unit_of(rows_in[...].reshape(-1, D).astype(FLOAT))
    sums[GAIN] += column_sum(normed_back * unit)
    sums[OFFSET] += column_sum(normed_back)
    rows_back = middle_back + norm_back(normed_back * gain[...], unit, inverse)
    delta[...] = rows_back.astype(HALF).reshape(shape)


def attention_back(place, frames, params, triple, weights, middles_back, pieces, after):
    per_group, windows, window, _ = frames.shape
    block = (per_group, windows // pieces, window, D)
    rows = per_group * block[1] * window
    count = rows * pieces
    across = pieces // HALVES
    cut = pl.BlockSpec(block, lambda i, place: (0, (place[0] ^ (i % across)) * HALVES + i // across, 0, 0))
    at = lambda i, place: i
    attended = (rows // window, PAIRS, window, 2 * window)
    ins = [(frames, cut)] + plain([params[0], params[2], params[3]])
    ins += [
        (triple, row_spec(rows, 3 * D, at)),
        (weights, pl.BlockSpec(attended, lambda i, place: (i, 0, 0, 0))),
        (middles_back, row_spec(rows, D, at)),
    ]
    return run(
        functools.partial(attention_back_body, window=window),
        "attention_back",
        (pieces,),
        [place],
        ins,
        [
            (frames.shape, HALF, cut),
            ((4, count, D), HALF, slab_spec(4, rows, at)),
            ((SUMS, 1, D), FLOAT, whole((SUMS, 1, D))),
        ],
        scratch=[pltpu.VMEM((rows, D), HALF)],
        after=after,
        flops=8 * count * D * D,
        moved=count * D * 2 * (3 + 1 + 2 + 4 + 2),
    )


def gradient_body(core, left_at, right_at, left, right, *outs, narrows, sent):
    step = pl.program_id(0)
    value = dot_left(left[0], right[0]).astype(HALF)
    if narrows:
        away, own = outs[:2]
        outs = outs[2:]
        _, shards, rows, _ = away.shape
        parts = value.reshape(shards, 4, rows, CHUNK)

        @pl.when(step < narrows)
        def _():
            for sub in range(2):
                for shard in range(shards):
                    one, two = parts[shard, sub], parts[shard, 2 + sub]
                    own[sub, shard] = jnp.where(core[0] == 0, one, two)
                    away[sub, shard] = jnp.where(core[0] == 0, two, one)

    if sent:
        away, own = outs

        @pl.when((step >= narrows) & (step < narrows + sent))
        def _():
            away[0] = value.reshape(away.shape[1:])

        @pl.when(step >= narrows + sent)
        def _():
            own[0] = value.reshape(own.shape[1:])


def gradient_tiles(core, lefts, rights, narrow, tiles, batch, after=()):
    sent = len(tiles) // 2
    narrows = 0 if narrow is None else CHUNKS
    order = [jnp.arange(sent) + sent * (1 - core), jnp.arange(sent) + sent * core]
    order = jnp.concatenate(order).astype(jnp.int32)
    tables = []
    for which in range(2):
        table = jnp.array([tile[which] for tile in tiles], jnp.int32)[order]
        first = [ACTIVE + i if which == 0 else narrow for i in range(narrows)]
        tables.append(jnp.concatenate([jnp.array(first, jnp.int32), table]))
    count = lefts.shape[1]
    block = (1, count, CHUNK)
    rows = D // batch
    outs = []
    if narrows:
        shards = batch // CHUNKS
        spec = pl.BlockSpec(
            (2, shards, rows, CHUNK), lambda i, *_: (0, jnp.minimum(i, narrows - 1), 0, 0)
        )
        outs += [((2, batch, rows, CHUNK), HALF, spec)] * 2
    if sent:
        for start in (narrows, narrows + sent):
            spec = pl.BlockSpec(
                (1, batch, rows, CHUNK),
                lambda i, *_, start=start: (jnp.clip(i - start, 0, sent - 1), 0, 0, 0),
            )
            outs.append(((sent, batch, rows, CHUNK), HALF, spec))
    made = run(
        functools.partial(gradient_body, narrows=narrows, sent=sent),
        "gradient_tiles",
        (narrows + len(tiles),),
        [core.reshape(1), *tables],
        [
            (lefts, pl.BlockSpec(block, lambda i, core, left, right: (left[i], 0, 0))),
            (rights, pl.BlockSpec(block, lambda i, core, left, right: (right[i], 0, 0))),
        ],
        outs,
        after=after,
        flops=2 * count * CHUNK * CHUNK * (narrows + len(tiles)),
        moved=4 * count * CHUNK * (narrows + len(tiles)),
    )
    return made[::2], made[1::2]


def swap(value, axis, mask):
    size = lax.axis_size(axis)
    if mask == 0:
        return value
    return lax.ppermute(value, axis, [(i, i ^ mask) for i in range(size)])


def move(value, batch_mask, win_mask):
    if batch_mask == 0:
        return swap(value, "win", win_mask)
    if win_mask == 0:
        return swap(value, "batch", batch_mask)
    batch, win = lax.axis_size("batch"), lax.axis_size("win")
    pairs = [
        (b * win + w, (b ^ batch_mask) * win + (w ^ win_mask)) for b in range(batch) for w in range(win)
    ]
    return lax.ppermute(value, ("batch", "win"), pairs)


def exchange(arrays):
    made = {k: swap(arrays[k], "win", k) for k in reversed(range(len(arrays)))}
    return [made[k] for k in range(len(arrays))]


def split_body(place, *refs, groups, across):
    own, got, outs = refs[:groups], refs[groups : 2 * groups], refs[2 * groups :]
    column, row = place[1], place[2]
    width = CHUNK // across
    at = 0
    for one, two in zip(own, got):
        rows = one.shape[3]
        for tile in range(one.shape[0]):
            for piece, out in enumerate(outs):
                y = row ^ (piece % 2)
                x = pl.ds(pl.multiple_of((column ^ (piece // 2)) * width, width), width)
                total = one[tile, :, y, :, x].astype(FLOAT) + two[tile, :, y, :, x].astype(FLOAT)
                out[:, at : at + rows] = total.astype(HALF)
            at += rows


def merge_body(place, *refs, inputs):
    ins, outs = refs[:inputs], refs[inputs:]
    for piece, out in enumerate(outs):
        z = place[3] ^ piece
        total = ins[0][z].astype(FLOAT)
        for ref in ins[1:]:
            total = total + ref[z].astype(FLOAT)
        out[...] = total.astype(HALF)


def last_body(*refs):
    ins, out = refs[:-1], refs[-1]
    total = ins[0][...].astype(FLOAT)
    for ref in ins[1:]:
        total = total + ref[...].astype(FLOAT)
    out[...] = total.astype(HALF)


def unpack_body(place, *refs, pieces, across, layout):
    ins, outs, held = refs[:pieces], refs[pieces:-1], refs[-1]
    width = CHUNK // across
    for piece, ref in enumerate(ins):
        x = pl.ds(pl.multiple_of((place[1] ^ (piece // 2)) * width, width), width)
        held[place[4] ^ (piece % 2), :, x] = ref[...].astype(FLOAT)
    for out, places in zip(outs, layout):
        for core, start, rows, left, wide, row, column in places:
            out[row : row + rows, column : column + wide] = held[
                core, start : start + rows, left : left + wide
            ]


class Reduction:
    def __init__(self, place, away, own):
        self.place = place
        self.batch, self.win = lax.axis_size("batch"), lax.axis_size("win")
        self.across, self.depth = self.win // 2, self.batch // 2
        cut = lambda a: a.reshape(-1, self.depth, 2, *a.shape[2:])
        self.own = [cut(a) for a in own]
        self.got = [swap(cut(a), "win", 1) for a in away]
        self.rows = sum(a.shape[0] * a.shape[3] for a in self.own)
        self.width = CHUNK // self.across

    def cores(self, after=()):
        shape = (self.depth, self.rows, self.width)
        pieces = run(
            functools.partial(split_body, groups=len(self.own), across=self.across),
            "sum_cores",
            (1,),
            [self.place],
            plain(self.own + self.got),
            [(shape, HALF, whole(shape))] * (2 * self.across),
            after=after,
        )
        self.mark = pieces[:1]
        self.pieces = [move(a, number % 2, 2 * (number // 2)) for number, a in enumerate(pieces)]

    def chips(self, after=()):
        shape = (self.rows, self.width)
        pieces = run(
            functools.partial(merge_body, inputs=len(self.pieces)),
            "sum_chips",
            (1,),
            [self.place],
            plain(self.pieces),
            [(shape, HALF, whole(shape))] * self.depth,
            after=after,
        )
        self.mark = pieces[:1]
        self.pieces = [swap(a, "batch", 2 * number) for number, a in enumerate(pieces)]

    def last(self, after=()):
        shape = (self.rows, self.width)
        outs = [(shape, HALF, whole(shape))]
        (total,) = run(last_body, "sum_last", (1,), [], plain(self.pieces), outs, after=after)
        self.mark = [total]
        self.pieces = [swap(total, "win", number) for number in range(self.win)]

    def unpack(self, layout, shapes):
        return run(
            functools.partial(
                unpack_body, pieces=self.win, across=self.across, layout=layout
            ),
            "unpack",
            (1,),
            [self.place],
            plain(self.pieces),
            [(s, FLOAT, whole(s)) for s in shapes],
            scratch=[pltpu.VMEM((2, self.rows, CHUNK), FLOAT)],
        )


SMALL_ROWS = 16


def small_tiles(core, sums, batch):
    vectors = sums[:6, 0].reshape(6, batch, D // batch).swapaxes(0, 1).reshape(batch, -1)
    lifts = sums[LIFT:, 0].reshape(batch, FF // batch)
    both = [jnp.pad(a, ((0, 0), (0, CHUNK - a.shape[1]))).astype(HALF) for a in (vectors, lifts)]
    both = [jnp.broadcast_to(a[None, :, None], (1, batch, SMALL_ROWS, CHUNK)) for a in both]
    own = jnp.where(core == 0, both[0], both[1])
    away = jnp.where(core == 0, both[1], both[0])
    return away, own


ENTRY_TILES = [(NORMED, TRIPLE_BACK + part) for part in range(3)] + [(MIXED, ATTEND_BACK)]
WIDEN_TILES = [(SECOND, HIDDEN_BACK + chunk) for chunk in range(CHUNKS)]
TIME_TILES = WIDEN_TILES[:2] + ENTRY_TILES[:2] + WIDEN_TILES[2:] + ENTRY_TILES[2:]


def entry_places(rows, start):
    spot = lambda tile: (tile // 2, start + tile % 2 * rows, rows, 0, CHUNK)
    return [
        [(*spot(part), 0, part * CHUNK) for part in range(3)],
        [(*spot(3), 0, 0)],
    ], [(rows, 3 * D), (rows, D)]


def widen_places(rows, start):
    narrows = [(sub // 2, start + sub % 2 * rows, rows, 0, CHUNK, sub * rows, 0) for sub in range(4)]
    start += 2 * rows
    widens = [
        (chunk // 2, start + chunk % 2 * rows, rows, 0, CHUNK, 0, chunk * CHUNK) for chunk in range(CHUNKS)
    ]
    return [widens, narrows], [(rows, FF), (4 * rows, D)]


def small_places(rows, start):
    layout = [[(0, start, 1, number * rows, rows, 0, 0)] for number in range(6)]
    layout.append([(1, start, 1, 0, 4 * rows, 0, 0)])
    return layout, [(1, rows)] * 6 + [(1, 4 * rows)]


def local(*args):
    frames, cotangent, video_frames = args[0], args[23], args[24]
    space = [a.reshape(1, -1) if a.ndim == 1 else a for a in args[1:12]]
    time = [a.reshape(1, -1) if a.ndim == 1 else a for a in args[12:23]]
    batch, win = lax.axis_size("batch"), lax.axis_size("win")
    here, group = lax.axis_index("win"), lax.axis_index("batch")
    core = here % 2
    place = jnp.stack([here, here // 2, group % 2, group // 2, core]).astype(jnp.int32)
    _, per_group, _, windows, window, _ = frames.shape
    shape = (per_group, windows, window, D)
    rows_in, cotangent = frames.reshape(shape), cotangent.reshape(shape)
    rows = D // batch

    kept, inners, cotangents = [], [], []
    for half in range(HALVES):
        inner, cut, kept = space_forward(place, rows_in, cotangent, space, half, win, kept)
        inners.append(exchange(inner))
        cotangents.append(exchange(cut))
    space_lefts, triple, weights, middles, slopes = kept
    results, backs, slabs, time_sums = [], [], [], []
    for half in range(HALVES):
        result, back, slabs, sums = time_block(
            place, video_frames, inners[half], cotangents[half], time, half, slabs
        )
        backs += exchange(back)
        results += exchange(result)
        time_sums.append(sums)
    time_lefts, time_rights = slabs

    away, own = gradient_tiles(
        core, time_lefts, time_rights, BRANCH_BACK, TIME_TILES, batch
    )
    mark = own[:1]
    small_away, small_own = small_tiles(core, sum(time_sums), batch)
    time_sum = Reduction(place, [*away, small_away], [*own, small_own])
    outcome, feed_rights, middles_back, feed_sums = feed_back(
        place, shape, space, backs, results, middles, slopes, mark
    )
    time_sum.cores([middles_back])
    away, own = gradient_tiles(
        core,
        space_lefts,
        feed_rights,
        CHUNKS,
        [(SECOND, chunk) for chunk in range(CHUNKS)],
        batch,
        time_sum.mark,
    )
    feed_sum = Reduction(place, away, own)
    delta, attend_rights, attend_sums = attention_back(
        place, rows_in, space, triple, weights, middles_back, 2 * win, own[:1]
    )
    time_sum.chips([delta])
    feed_sum.cores(time_sum.mark)
    away, own = gradient_tiles(
        core,
        space_lefts,
        attend_rights,
        None,
        [(NORMED, part) for part in range(3)] + [(MIXED, 3)],
        batch,
        feed_sum.mark,
    )
    small_away, small_own = small_tiles(core, feed_sums + attend_sums, batch)
    attend_sum = Reduction(place, [*away, small_away], [*own, small_own])
    attend_sum.cores(own[:1])
    time_sum.last(attend_sum.mark)
    feed_sum.chips(time_sum.mark)
    attend_sum.chips(feed_sum.mark)
    feed_sum.last(attend_sum.mark)
    attend_sum.last(feed_sum.mark)

    return (
        outcome.reshape(frames.shape),
        delta.reshape(frames.shape),
        *collected(feed_sum, attend_sum, rows),
        *collected(time_sum, time_sum, rows),
    )


def collected(feed, attend, rows):
    feed_layout, feed_shapes = widen_places(rows, 0)
    attend_layout, attend_shapes = entry_places(rows, 4 * rows if feed is attend else 0)
    small_layout, small_shapes = small_places(rows, attend.rows - SMALL_ROWS)
    if feed is attend:
        made = feed.unpack(
            feed_layout + attend_layout + small_layout, feed_shapes + attend_shapes + small_shapes
        )
    else:
        made = feed.unpack(feed_layout, feed_shapes)
        made += attend.unpack(attend_layout + small_layout, attend_shapes + small_shapes)
    widen, narrow, entry, leave = made[:4]
    gain, offset, bias, weigh, shift, nudge, lift = [a.reshape(-1) for a in made[4:]]
    return gain, offset, entry, leave, bias, weigh, shift, widen, lift, narrow, nudge


def solution(mesh):
    rows = P("batch", None, "win", None, None, None)
    one, two = P("batch"), P("batch", None)
    grads = (one, one, two, two, one, one, one, two, one, two, one)
    return jax.shard_map(
        local,
        mesh=mesh,
        in_specs=(rows, *([P()] * 22), rows, P("batch", None)),
        out_specs=(rows, rows, *grads, *grads),
        check_vma=False,
    )
```

time: 1110 us -> 415 us (0.37); the launches traced: 1090 us -> 414 us
  matrix products: 356 us -> 0 us
  waiting for transfers between devices: 345 us -> 87.1 us
  Pallas kernels: 0 us -> 212 us
  local copies, waits for them, and re-layouts: 210 us -> 54.9 us
  other arithmetic: 107 us -> 1.69 us
  blocking collectives: 41.3 us -> 0 us
  starting transfers between devices: 18.4 us -> 56.2 us
  between operations: 16.8 us -> 1.53 us
    dot_general x36 -> x0, matrix products: 356 us -> none  [the longest x8 88.5 us: transposed_product(): lax.dot_general(incoming, weight, (((1,), (1,)), ((), ())), preferred_ele...]
    reduce_scatter x8 -> x0, waiting for transfers between devices: 303 us -> none  [the longest x1 71 us: local(): lax.psum_scatter(space_changes[7].astype(jnp.bfloat16), 'batch', scatter_...]
    pallas_call x0 -> x21, Pallas kernels: none -> 212 us  [run(): pl.pallas_call(inner, out_shape=[jax.ShapeDtypeStruct(shape, kind) for sh...]
    ppermute x0 -> x58, waiting for transfers between devices: none -> 87.1 us  [the longest x55 72.4 us: swap(): return lax.ppermute(value, axis, [(i, i ^ mask) for i in range(size)])]
    reshape x9 -> x2, local copies, waits for them, and re-layouts: 80.4 us -> 0.78 us  [small_tiles(): sums[:6, 0].reshape(6, batch, D // batch).swapaxes(0, 1).reshape(batch, -1)]
    convert_element_type x32 -> x0, other arithmetic: 69.9 us -> none  [the longest x2 17.8 us: attend_backward(): return stacked.reshape(-1, 3 * HEADS * HDIM).astype(HALF)]
    convert_element_type x6 -> x0, local copies, waits for them, and re-layouts: 65.2 us -> none  [the longest x3 48.6 us: attend_backward(): return stacked.reshape(-1, 3 * HEADS * HDIM).astype(HALF)]
    ppermute x0 -> x58, starting transfers between devices: none -> 56.2 us  [the longest x55 53.4 us: swap(): return lax.ppermute(value, axis, [(i, i ^ mask) for i in range(size)])]
  transfers between devices with their start and end apart: 13 -> 58, of which waited for: 7 -> 23; matrix products, arithmetic and copies ran while one was open for 34% -> 3% of each run, Pallas kernels for 0% -> 19%
where the time goes in v1:
time: 415 us; the launch traced here: 414 us
  Pallas kernels  212 us (51%)
  waiting for transfers between devices  87.1 us (21%)
  starting transfers between devices  56.2 us (14%)
  local copies, waits for them, and re-layouts  54.9 us (13%)
    pallas_call x21, Pallas kernels, run(): pl.pallas_call(inner, out_shape=[jax.ShapeDtypeStruct(shape, kind) for sh...  212 us
    ppermute x55, waiting for transfers between devices, swap(): return lax.ppermute(value, axis, [(i, i ^ mask) for i in range(size)])  72.4 us
    ppermute x55, starting transfers between devices, swap(): return lax.ppermute(value, axis, [(i, i ^ mask) for i in range(size)])  53.4 us
    unnamed x182, local copies, waits for them, and re-layouts  45.6 us
    ppermute x3, waiting for transfers between devices, move(): return lax.ppermute(value, ('batch', 'win'), pairs)  14.7 us
  transfers between devices with their start and end apart: 58, of which 23 were waited for; matrix products, arithmetic and copies ran while one was open for 3% of the time, Pallas kernels for 19%

profile of v1, /device:TPU:0, one launch (start us, length us, event | category | flops | bytes accessed | tf_op | source)
XLA Modules:
  0.0 413.6 jit_solution(16774517718323191483)
XLA Ops:
  0.8 1.6 copy-done.3
  2.4 1.4 copy-done.7
  4.8 1.6 copy-done.11
  6.4 1.6 copy-done.12
  12.8 20.9 %space_forward.2 = (bf16[2,2,64,512]{3,2,1,0:T(8,128)(2,1)S(1)}, bf16[2,2,64,512]{3,2,1,0:T(8,128)(2,1)}, bf16[2,2,64,512]{3,2,1,0:T(8,128)(2,1)}, bf16[2,2,64,5...) custom-call(s32[5]{0:T(128)S(1)} %stack.23.refs_0_, ...), custom_call_target="tpu_custom_call" | custom-call | flops 6442450944 | bytes 23068672 | tf_op jit(solution)/shard_map/space_forward/pallas_call | solution.py:154
  33.8 21.1 %space_forward.3 = (bf16[2,2,64,512]{3,2,1,0:T(8,128)(2,1)S(1)}, bf16[2,2,64,512]{3,2,1,0:T(8,128)(2,1)}, bf16[2,2,64,512]{3,2,1,0:T(8,128)(2,1)S(1)}, bf16[2,2,...) custom-call(s32[5]{0:T(128)S(1)} %stack.23.refs_0_, ...), custom_call_target="tpu_custom_call", output_to_operand_aliasing={{8}: (14, {}), {9}: (15, {}), {10}: (16, {}), {11}: (17, {}... | custom-call | flops 6442450944 | bytes 23068672 | tf_op jit(solution)/shard_map/space_forward/pallas_call | solution.py:154
  60.4 2.9 collective-permute-start.1
  63.5 2.0 collective-permute-start.4
  67.0 3.7 collective-permute-done.1
  70.8 2.1 collective-permute-start.10
  72.8 3.1 collective-permute-done.2
  76.0 1.9 collective-permute-start.11
  77.9 4.1 collective-permute-done.4
  82.0 2.1 collective-permute-start.13
  84.1 3.1 collective-permute-done.5
  87.2 1.9 collective-permute-start.14
  89.2 1.6 copy-done.37
  94.1 31.1 %time_block.2 = (bf16[2,128,512]{2,1,0:T(8,128)(2,1)S(1)}, bf16[2,128,512]{2,1,0:T(8,128)(2,1)S(1)}, bf16[2,128,512]{2,1,0:T(8,128)(2,1)S(1)}, bf16[2,128,512]{2...) custom-call(s32[5]{0:T(128)S(1)} %stack.23.refs_0_, ...), custom_call_target="tpu_custom_call" | custom-call | flops 12884901888 | bytes 27262976 | tf_op jit(solution)/shard_map/time_block/pallas_call | solution.py:154
  130.2 30.1 %time_block.3 = (bf16[2,128,512]{2,1,0:T(8,128)(2,1)S(1)}, bf16[2,128,512]{2,1,0:T(8,128)(2,1)S(1)}, bf16[2,128,512]{2,1,0:T(8,128)(2,1)S(1)}, bf16[2,128,512]{2...) custom-call(s32[5]{0:T(128)S(1)} %stack.23.refs_0_, ...), custom_call_target="tpu_custom_call", output_to_operand_aliasing={{8}: (21, {}), {9}: (22, {})} | custom-call | flops 12884901888 | bytes 27262976 | tf_op jit(solution)/shard_map/time_block/pallas_call | solution.py:154
  160.4 25.0 %gradient_tiles.3 = (bf16[2,8,64,512]{3,2,1,0:T(8,128)(2,1)S(1)}, bf16[2,8,64,512]{3,2,1,0:T(8,128)(2,1)S(1)}, bf16[4,8,64,512]{3,2,1,0:T(8,128)(2,1)}, bf16[4,8,64,512]{3,2,1,0:T(8,128)(2,1)S(1)}) custom-call(s32[1]{0:T(128)} %bitcast.4.refs_0_, s32[12]{0:T(128)S(1)} %pad_add_fusion.refs_1_, s32[12]{0:T(128)S(1)} %pad.22.refs_2_, ...), custom_call_target="tpu_custom_call" | custom-call | flops 12884901888 | bytes 50331648 | tf_op jit(solution)/shard_map/gradient_tiles/pallas_call | solution.py:154
  190.4 2.2 collective-permute-done.15.refs_9_
  193.5 4.2 %collective-permute-done.16.refs_10_ = bf16[2,2,64,512]{3,2,1,0:T(8,128)(2,1)} collective-permute-done((bf16[2,2,64,512]{3,2,1,0:T(8,128)(2,1)}, bf16[2,2,64,512]{3,2,1,0:T(8,128)(2,1)}, u32[]{:S(2)}, u32[]{:S(2)}) %collective-permute-start.16) | collective-permute-done | bytes 262176 | tf_op jit(solution)/shard_map/ppermute | solution.py:608
  197.7 3.7 collective-permute-done.17.refs_11_
  201.4 1.7 collective-permute-start.18
  203.2 5.8 %collective-permute-done.22.refs_18_ = bf16[2,2,64,512]{3,2,1,0:T(8,128)(2,1)} collective-permute-done((bf16[2,2,64,512]{3,2,1,0:T(8,128)(2,1)}, bf16[2,2,64,512]{3,2,1,0:T(8,128)(2,1)}, u32[]{:S(2)}, u32[]{:S(2)}) %collective-permute-start.22) | collective-permute-done | bytes 262176 | tf_op jit(solution)/shard_map/ppermute | solution.py:608
  209.8 2.9 collective-permute-done.23.refs_19_
  212.6 1.7 collective-permute-start.6
  214.4 5.8 %collective-permute-done.19.refs_14_ = bf16[2,2,64,512]{3,2,1,0:T(8,128)(2,1)} collective-permute-done((bf16[2,2,64,512]{3,2,1,0:T(8,128)(2,1)}, bf16[2,2,64,512]{3,2,1,0:T(8,128)(2,1)}, u32[]{:S(2)}, u32[]{:S(2)}) %collective-permute-start.19) | collective-permute-done | bytes 262176 | tf_op jit(solution)/shard_map/ppermute | solution.py:608
  220.2 3.7 collective-permute-done.20.refs_15_
  223.9 1.7 collective-permute-start.24
  226.1 5.4 %collective-permute-done.7.refs_6_ = bf16[2,2,64,512]{3,2,1,0:T(8,128)(2,1)} collective-permute-done((bf16[2,2,64,512]{3,2,1,0:T(8,128)(2,1)}, bf16[2,2,64,512]{3,2,1,0:T(8,128)(2,1)}, u32[]{:S(2)}, u32[]{:S(2)}) %collective-permute-start.7) | collective-permute-done | bytes 262176 | tf_op jit(solution)/shard_map/ppermute | solution.py:608
  231.4 3.7 collective-permute-done.8.refs_7_
  235.1 1.6 copy-done.14
  240.5 19.6 %feed_back.1 = (bf16[2,16,64,512]{3,2,1,0:T(8,128)(2,1)}, bf16[5,2048,512]{2,1,0:T(8,128)(2,1)}, f32[2048,512]{1,0:T(8,128)S(1)}, f32[10,1,512]{2,1,0:T(1,128)S(1)}) custom-call(s32[5]{0:T(128)S(1)} %stack.23.refs_0_, f32[1,512]{1,0:T(1,128)S(1)} %bitcast.123, bf16[512,2048]{1,0:T(8,128)(2,1)S(1)} %copy-done.13, bf16[2048,512]{1,0:T(8,128)(2,1)S(1)} %copy-done.14, ...), custom_call_target="tpu_custom_call" | custom-call | flops 8589934592 | bytes 35651584 | tf_op jit(solution)/shard_map/feed_back/pallas_call | solution.py:154
  260.2 5.2 %sum_cores.3 = (bf16[4,400,256]{2,1,0:T(8,128)(2,1)S(1)}, bf16[4,400,256]{2,1,0:T(8,128)(2,1)}, bf16[4,400,256]{2,1,0:T(8,128)(2,1)}, bf16[4,400,256]{2,1,0:T(8,128)(2,1)}) custom-call(s32[5]{0:T(128)S(1)} %stack.23.refs_0_, bf16[2,4,2,64,512]{4,3,2,1,0:T(8,128)(2,1)S(1)} %bitcast.107, bf16[4,4,2,64,512]{4,3,2,1,0:T(8,128)(2,1)S(1)} %bitcast.105, ...), custom_call_target="tpu_custom_call" | custom-call | tf_op jit(solution)/shard_map/sum_cores/pallas_call | solution.py:154
  265.5 16.6 %gradient_tiles.4 = (bf16[2,8,64,512]{3,2,1,0:T(8,128)(2,1)}, bf16[2,8,64,512]{3,2,1,0:T(8,128)(2,1)S(1)}, bf16[2,8,64,512]{3,2,1,0:T(8,128)(2,1)}, bf16[2,8,64,512]{3,2,1,0:T(8,128)(2,1)S(1)}) custom-call(s32[1]{0:T(128)} %bitcast.4.refs_0_, s32[8]{0:T(128)S(1)} %pad_add_fusion.1.refs_1_, s32[8]{0:T(128)S(1)} %pad.23.refs_2_, ...), custom_call_target="tpu_custom_call" | custom-call | flops 8589934592 | bytes 33554432 | tf_op jit(solution)/shard_map/gradient_tiles/pallas_call | solution.py:154
  283.9 1.5 collective-permute-start.29
  288.0 2.2 copy-done.1
  290.2 1.6 copy-done.6
  294.2 18.8 %attention_back.1 = (bf16[2,16,64,512]{3,2,1,0:T(8,128)(2,1)}, bf16[4,2048,512]{2,1,0:T(8,128)(2,1)}, f32[10,1,512]{2,1,0:T(1,128)S(1)}) custom-call(s32[5]{0:T(128)S(1)} %stack.23.refs_0_, bf16[2,16,64,512]{3,2,1,0:T(8,128)(2,1)S(1)} %bitcast.99, f32[1,512]{1,0:T(1,128)S(1)} %bitcast.112, bf16[512,1536]{1,0:T(8,128)(2,1)S(1)} %copy-done.8, ...), custom_call_target="tpu_custom_call" | custom-call | flops 4294967296 | bytes 25165824 | tf_op jit(solution)/shard_map/attention_back/pallas_call | solution.py:154
  313.1 10.5 %collective-permute-done.31.refs_4_ = bf16[4,400,256]{2,1,0:T(8,128)(2,1)} collective-permute-done((bf16[4,400,256]{2,1,0:T(8,128)(2,1)}, bf16[4,400,256]{2,1,0:T(8,128)(2,1)}, u32[]{:S(2)}, u32[]{:S(2)}) %collective-permute-start.31) | collective-permute-done | bytes 819232 | tf_op jit(solution)/shard_map/ppermute | solution.py:620
  323.6 1.6 copy-done.15
  325.2 2.8 sum_chips.3
  328.1 2.6 sum_cores.4
  330.7 8.7 %gradient_tiles.5 = (bf16[2,8,64,512]{3,2,1,0:T(8,128)(2,1)}, bf16[2,8,64,512]{3,2,1,0:T(8,128)(2,1)S(1)}) custom-call(s32[1]{0:T(128)} %bitcast.4.refs_0_, s32[4]{0:T(128)S(1)} %gather_fusion.4, s32[4]{0:T(128)S(1)} %gather_fusion.3, bf16[7,2048,512]{2,1,0:T(8,128)(2,1)} %get-tuple-element.183.refs_3_, bf16[4,2048,512]{2,1,0:T(8,128)(2,1)S(1)} %copy-done.2, ...), custom_call_target="tpu_custom_call" | custom-call | flops 4294967296 | bytes 16777216 | tf_op jit(solution)/shard_map/gradient_tiles/pallas_call | solution.py:154
  341.0 1.6 collective-permute-start.40
  342.6 1.5 collective-permute-start.37
  350.2 2.6 collective-permute-start.41
  357.5 9.6 %collective-permute-done.41.refs_2_ = bf16[400,256]{1,0:T(8,128)(2,1)} collective-permute-done((bf16[400,256]{1,0:T(8,128)(2,1)}, bf16[400,256]{1,0:T(8,128)(2,1)}, u32[]{:S(2)}, u32[]{:S(2)}) %collective-permute-start.41) | collective-permute-done | bytes 204832 | tf_op jit(solution)/shard_map/ppermute | solution.py:608
  367.1 1.5 collective-permute-start.34
  371.8 2.1 collective-permute-done.39.refs_4_
  373.9 2.0 sum_chips.4
  375.9 2.4 collective-permute-start.46
  378.2 1.7 collective-permute-done.34.refs_2_
  380.0 3.9 collective-permute-start.47
  383.9 2.1 collective-permute-done.36.refs_4_
  387.7 5.5 %collective-permute-done.47.refs_2_ = bf16[256,256]{1,0:T(8,128)(2,1)S(1)} collective-permute-done((bf16[256,256]{1,0:T(8,128)(2,1)S(1)}, bf16[256,256]{1,0:T(8,128)(2,1)S(1)}, u32[]{:S(2)}, u32[]{:S(2)}) %collective-permute-start.47) | collective-permute-done | bytes 131104 | tf_op jit(solution)/shard_map/ppermute | solution.py:608
  393.2 3.0 collective-permute-start.44
  396.2 2.4 collective-permute-start.45
  399.0 4.2 %collective-permute-start.53 = (bf16[256,256]{1,0:T(8,128)(2,1)S(1)}, bf16[256,256]{1,0:T(8,128)(2,1)S(1)}, u32[]{:S(2)}, u32[]{:S(2)}) collective-permute-start(bf16[256,256]{1,0:T(8,128)(2,1)S(1)} %sum_last.4.refs_4_.refs_1_), channel_id=1, source_target_pairs={{0,2},{1,3},{2,0},{3,1},{4,6},{5,7},{6,4},{7,5},{8,10},{9,11},{10,... | collective-permute-start | bytes 393224 | tf_op jit(solution)/shard_map/ppermute | solution.py:608
  403.5 2.0 collective-permute-start.50
  405.5 1.8 unpack.5
  407.4 2.2 collective-permute-done.54.refs_4_
  409.6 1.6 unpack.4
  (297 shorter events, 59.5 us)
Async XLA Ops:
  0.8 327.3 %copy-start.24 = (s32[5]{0:T(128)}, s32[5]{0:T(128)S(1)}, u32[]{:S(2)}) copy-start(s32[5]{0:T(128)S(1)} %stack.23.refs_0_) | copy-start | bytes 64
  33.7 55.4 %copy-start.36 = (bf16[512,2048]{1,0:T(8,128)(2,1)S(1)}, bf16[512,2048]{1,0:T(8,128)(2,1)}, u32[]{:S(2)}) copy-start(bf16[512,2048]{1,0:T(8,128)(2,1)} %refs_17_.3) | copy-start | bytes 6291460
  33.7 55.4 %copy-start.42 = (bf16[512,512]{1,0:T(8,128)(2,1)S(1)}, bf16[512,512]{1,0:T(8,128)(2,1)}, u32[]{:S(2)}) copy-start(bf16[512,512]{1,0:T(8,128)(2,1)} %refs_13_.3) | copy-start | bytes 1572868
  33.7 55.4 %copy-start.67 = (f32[2048]{0:T(1024)S(1)}, f32[2048]{0:T(1024)}, u32[]{:S(2)}) copy-start(f32[2048]{0:T(1024)} %param.55) | copy-start | bytes 24580
  59.9 3.6 collective-permute-start.9
  60.3 5.1 %collective-permute-start = (bf16[2,2,64,512]{3,2,1,0:T(8,128)(2,1)}, bf16[2,2,64,512]{3,2,1,0:T(8,128)(2,1)}, u32[]{:S(2)}, u32[]{:S(2)}) collective-permute-start(bf16[2,2,64,512]{3,2,1,0:T(8,128)(2,1)} %get-tuple-element.136), channel_id=1, source_target_pairs={{0,1},{1,0},{2,3},{3,2},{4,5},{5,4},{6,7},{7,6},{8,9},{9,8},{10,11... | collective-permute-start | bytes 786440 | tf_op jit(solution)/shard_map/ppermute | solution.py:608
  60.4 10.4 %collective-permute-start.1 = (bf16[2,2,64,512]{3,2,1,0:T(8,128)(2,1)}, bf16[2,2,64,512]{3,2,1,0:T(8,128)(2,1)}, u32[]{:S(2)}, u32[]{:S(2)}) collective-permute-start(bf16[2,2,64,512]{3,2,1,0:T(8,128)(2,1)} %get-tuple-element.137), channel_id=1, source_target_pairs={{0,2},{1,3},{2,0},{3,1},{4,6},{5,7},{6,4},{7,5},{8,10},{9,11},{10,... | collective-permute-start | bytes 786440 | tf_op jit(solution)/shard_map/ppermute | solution.py:608
  63.3 12.6 %collective-permute-start.2 = (bf16[2,2,64,512]{3,2,1,0:T(8,128)(2,1)}, bf16[2,2,64,512]{3,2,1,0:T(8,128)(2,1)}, u32[]{:S(2)}, u32[]{:S(2)}) collective-permute-start(bf16[2,2,64,512]{3,2,1,0:T(8,128)(2,1)} %get-tuple-element.138), channel_id=1, source_target_pairs={{0,3},{1,2},{2,1},{3,0},{4,7},{5,6},{6,5},{7,4},{8,11},{9,10},{10,... | collective-permute-start | bytes 786440 | tf_op jit(solution)/shard_map/ppermute | solution.py:608
  63.3 14.5 %collective-permute-start.3 = (bf16[2,2,64,512]{3,2,1,0:T(8,128)(2,1)}, bf16[2,2,64,512]{3,2,1,0:T(8,128)(2,1)}, u32[]{:S(2)}, u32[]{:S(2)}) collective-permute-start(bf16[2,2,64,512]{3,2,1,0:T(8,128)(2,1)} %get-tuple-element.140), channel_id=1, source_target_pairs={{0,1},{1,0},{2,3},{3,2},{4,5},{5,4},{6,7},{7,6},{8,9},{9,8},{10,11... | collective-permute-start | bytes 786440 | tf_op jit(solution)/shard_map/ppermute | solution.py:608
  63.5 18.5 %collective-permute-start.4 = (bf16[2,2,64,512]{3,2,1,0:T(8,128)(2,1)}, bf16[2,2,64,512]{3,2,1,0:T(8,128)(2,1)}, u32[]{:S(2)}, u32[]{:S(2)}) collective-permute-start(bf16[2,2,64,512]{3,2,1,0:T(8,128)(2,1)} %copy-done.59), channel_id=1, source_target_pairs={{0,2},{1,3},{2,0},{3,1},{4,6},{5,7},{6,4},{7,5},{8,10},{9,11},{10,... | collective-permute-start | bytes 786440 | tf_op jit(solution)/shard_map/ppermute | solution.py:608
  65.5 21.7 %collective-permute-start.5 = (bf16[2,2,64,512]{3,2,1,0:T(8,128)(2,1)}, bf16[2,2,64,512]{3,2,1,0:T(8,128)(2,1)}, u32[]{:S(2)}, u32[]{:S(2)}) collective-permute-start(bf16[2,2,64,512]{3,2,1,0:T(8,128)(2,1)} %copy-done.57), channel_id=1, source_target_pairs={{0,3},{1,2},{2,1},{3,0},{4,7},{5,6},{6,5},{7,4},{8,11},{9,10},{10,... | collective-permute-start | bytes 786440 | tf_op jit(solution)/shard_map/ppermute | solution.py:608
  70.8 59.3 %collective-permute-start.10 = (bf16[2,2,64,512]{3,2,1,0:T(8,128)(2,1)}, bf16[2,2,64,512]{3,2,1,0:T(8,128)(2,1)S(1)}, u32[]{:S(2)}, u32[]{:S(2)}) collective-permute-start(bf16[2,2,64,512]{3,2,1,0:T(8,128)(2,1)} %copy-done.56), channel_id=1, source_target_pairs={{0,2},{1,3},{2,0},{3,1},{4,6},{5,7},{6,4},{7,5},{8,10},{9,11},{10,... | collective-permute-start | bytes 786440 | tf_op jit(solution)/shard_map/ppermute | solution.py:608
  76.0 54.1 %collective-permute-start.11 = (bf16[2,2,64,512]{3,2,1,0:T(8,128)(2,1)}, bf16[2,2,64,512]{3,2,1,0:T(8,128)(2,1)S(1)}, u32[]{:S(2)}, u32[]{:S(2)}) collective-permute-start(bf16[2,2,64,512]{3,2,1,0:T(8,128)(2,1)} %copy-done.55), channel_id=1, source_target_pairs={{0,3},{1,2},{2,1},{3,0},{4,7},{5,6},{6,5},{7,4},{8,11},{9,10},{10,... | collective-permute-start | bytes 786440 | tf_op jit(solution)/shard_map/ppermute | solution.py:608
  77.9 52.2 %collective-permute-start.12 = (bf16[2,2,64,512]{3,2,1,0:T(8,128)(2,1)}, bf16[2,2,64,512]{3,2,1,0:T(8,128)(2,1)S(1)}, u32[]{:S(2)}, u32[]{:S(2)}) collective-permute-start(bf16[2,2,64,512]{3,2,1,0:T(8,128)(2,1)} %copy-done.54), channel_id=1, source_target_pairs={{0,1},{1,0},{2,3},{3,2},{4,5},{5,4},{6,7},{7,6},{8,9},{9,8},{10,11... | collective-permute-start | bytes 786440 | tf_op jit(solution)/shard_map/ppermute | solution.py:608
  82.0 48.1 %collective-permute-start.13 = (bf16[2,2,64,512]{3,2,1,0:T(8,128)(2,1)}, bf16[2,2,64,512]{3,2,1,0:T(8,128)(2,1)S(1)}, u32[]{:S(2)}, u32[]{:S(2)}) collective-permute-start(bf16[2,2,64,512]{3,2,1,0:T(8,128)(2,1)} %copy-done.53), channel_id=1, source_target_pairs={{0,2},{1,3},{2,0},{3,1},{4,6},{5,7},{6,4},{7,5},{8,10},{9,11},{10,... | collective-permute-start | bytes 786440 | tf_op jit(solution)/shard_map/ppermute | solution.py:608
  87.2 42.9 %collective-permute-start.14 = (bf16[2,2,64,512]{3,2,1,0:T(8,128)(2,1)}, bf16[2,2,64,512]{3,2,1,0:T(8,128)(2,1)S(1)}, u32[]{:S(2)}, u32[]{:S(2)}) collective-permute-start(bf16[2,2,64,512]{3,2,1,0:T(8,128)(2,1)} %copy-done.52), channel_id=1, source_target_pairs={{0,3},{1,2},{2,1},{3,0},{4,7},{5,6},{6,5},{7,4},{8,11},{9,10},{10,... | collective-permute-start | bytes 786440 | tf_op jit(solution)/shard_map/ppermute | solution.py:608
  160.4 74.7 %copy-start.13 = (bf16[512,2048]{1,0:T(8,128)(2,1)S(1)}, bf16[512,2048]{1,0:T(8,128)(2,1)}, u32[]{:S(2)}) copy-start(bf16[512,2048]{1,0:T(8,128)(2,1)} %refs_2_.1) | copy-start | bytes 6291460
  160.4 74.7 %copy-start.35 = (f32[512]{0:T(512)S(1)}, f32[512]{0:T(512)}, u32[]{:S(2)}) copy-start(f32[512]{0:T(512)} %param.41) | copy-start | bytes 6148
  187.7 72.5 %collective-permute-start.25 = (bf16[4,4,2,64,512]{4,3,2,1,0:T(8,128)(2,1)}, bf16[4,4,2,64,512]{4,3,2,1,0:T(8,128)(2,1)}, u32[]{:S(2)}, u32[]{:S(2)}) collective-permute-start(bf16[4,4,2,64,512]{4,3,2,1,0:T(8,128)(2,1)} %bitcast.65), channel_id=1, source_target_pairs={{0,1},{1,0},{2,3},{3,2},{4,5},{5,4},{6,7},{7,6},{8,9},{9,8},{10,11... | collective-permute-start | bytes 6291464 | tf_op jit(solution)/shard_map/ppermute | solution.py:608
  187.7 4.9 %collective-permute-start.15 = (bf16[2,2,64,512]{3,2,1,0:T(8,128)(2,1)}, bf16[2,2,64,512]{3,2,1,0:T(8,128)(2,1)}, u32[]{:S(2)}, u32[]{:S(2)}) collective-permute-start(bf16[2,2,64,512]{3,2,1,0:T(8,128)(2,1)} %bitcast.42), channel_id=1, source_target_pairs={{0,1},{1,0},{2,3},{3,2},{4,5},{5,4},{6,7},{7,6},{8,9},{9,8},{10,11... | collective-permute-start | bytes 786440 | tf_op jit(solution)/shard_map/ppermute | solution.py:608
  188.2 9.5 %collective-permute-start.16 = (bf16[2,2,64,512]{3,2,1,0:T(8,128)(2,1)}, bf16[2,2,64,512]{3,2,1,0:T(8,128)(2,1)}, u32[]{:S(2)}, u32[]{:S(2)}) collective-permute-start(bf16[2,2,64,512]{3,2,1,0:T(8,128)(2,1)} %bitcast.140), channel_id=1, source_target_pairs={{0,2},{1,3},{2,0},{3,1},{4,6},{5,7},{6,4},{7,5},{8,10},{9,11},{10,... | collective-permute-start | bytes 786440 | tf_op jit(solution)/shard_map/ppermute | solution.py:608
  188.3 13.1 %collective-permute-start.17 = (bf16[2,2,64,512]{3,2,1,0:T(8,128)(2,1)}, bf16[2,2,64,512]{3,2,1,0:T(8,128)(2,1)}, u32[]{:S(2)}, u32[]{:S(2)}) collective-permute-start(bf16[2,2,64,512]{3,2,1,0:T(8,128)(2,1)} %bitcast.138), channel_id=1, source_target_pairs={{0,3},{1,2},{2,1},{3,0},{4,7},{5,6},{6,5},{7,4},{8,11},{9,10},{10,... | collective-permute-start | bytes 786440 | tf_op jit(solution)/shard_map/ppermute | solution.py:608
  189.6 13.6 %collective-permute-start.21 = (bf16[2,2,64,512]{3,2,1,0:T(8,128)(2,1)}, bf16[2,2,64,512]{3,2,1,0:T(8,128)(2,1)}, u32[]{:S(2)}, u32[]{:S(2)}) collective-permute-start(bf16[2,2,64,512]{3,2,1,0:T(8,128)(2,1)} %bitcast.136), channel_id=1, source_target_pairs={{0,1},{1,0},{2,3},{3,2},{4,5},{5,4},{6,7},{7,6},{8,9},{9,8},{10,11... | collective-permute-start | bytes 786440 | tf_op jit(solution)/shard_map/ppermute | solution.py:608
  192.6 16.4 %collective-permute-start.22 = (bf16[2,2,64,512]{3,2,1,0:T(8,128)(2,1)}, bf16[2,2,64,512]{3,2,1,0:T(8,128)(2,1)}, u32[]{:S(2)}, u32[]{:S(2)}) collective-permute-start(bf16[2,2,64,512]{3,2,1,0:T(8,128)(2,1)} %bitcast.134), channel_id=1, source_target_pairs={{0,2},{1,3},{2,0},{3,1},{4,6},{5,7},{6,4},{7,5},{8,10},{9,11},{10,... | collective-permute-start | bytes 786440 | tf_op jit(solution)/shard_map/ppermute | solution.py:608
  197.7 14.9 %collective-permute-start.23 = (bf16[2,2,64,512]{3,2,1,0:T(8,128)(2,1)}, bf16[2,2,64,512]{3,2,1,0:T(8,128)(2,1)}, u32[]{:S(2)}, u32[]{:S(2)}) collective-permute-start(bf16[2,2,64,512]{3,2,1,0:T(8,128)(2,1)} %bitcast.133), channel_id=1, source_target_pairs={{0,3},{1,2},{2,1},{3,0},{4,7},{5,6},{6,5},{7,4},{8,11},{9,10},{10,... | collective-permute-start | bytes 786440 | tf_op jit(solution)/shard_map/ppermute | solution.py:608
  201.4 13.0 %collective-permute-start.18 = (bf16[2,2,64,512]{3,2,1,0:T(8,128)(2,1)}, bf16[2,2,64,512]{3,2,1,0:T(8,128)(2,1)}, u32[]{:S(2)}, u32[]{:S(2)}) collective-permute-start(bf16[2,2,64,512]{3,2,1,0:T(8,128)(2,1)} %bitcast.132), channel_id=1, source_target_pairs={{0,1},{1,0},{2,3},{3,2},{4,5},{5,4},{6,7},{7,6},{8,9},{9,8},{10,11... | collective-permute-start | bytes 786440 | tf_op jit(solution)/shard_map/ppermute | solution.py:608
  203.2 17.0 %collective-permute-start.19 = (bf16[2,2,64,512]{3,2,1,0:T(8,128)(2,1)}, bf16[2,2,64,512]{3,2,1,0:T(8,128)(2,1)}, u32[]{:S(2)}, u32[]{:S(2)}) collective-permute-start(bf16[2,2,64,512]{3,2,1,0:T(8,128)(2,1)} %bitcast.129), channel_id=1, source_target_pairs={{0,2},{1,3},{2,0},{3,1},{4,6},{5,7},{6,4},{7,5},{8,10},{9,11},{10,... | collective-permute-start | bytes 786440 | tf_op jit(solution)/shard_map/ppermute | solution.py:608
  208.9 14.9 %collective-permute-start.20 = (bf16[2,2,64,512]{3,2,1,0:T(8,128)(2,1)}, bf16[2,2,64,512]{3,2,1,0:T(8,128)(2,1)}, u32[]{:S(2)}, u32[]{:S(2)}) collective-permute-start(bf16[2,2,64,512]{3,2,1,0:T(8,128)(2,1)} %bitcast.128), channel_id=1, source_target_pairs={{0,3},{1,2},{2,1},{3,0},{4,7},{5,6},{6,5},{7,4},{8,11},{9,10},{10,... | collective-permute-start | bytes 786440 | tf_op jit(solution)/shard_map/ppermute | solution.py:608
  212.6 13.3 %collective-permute-start.6 = (bf16[2,2,64,512]{3,2,1,0:T(8,128)(2,1)}, bf16[2,2,64,512]{3,2,1,0:T(8,128)(2,1)}, u32[]{:S(2)}, u32[]{:S(2)}) collective-permute-start(bf16[2,2,64,512]{3,2,1,0:T(8,128)(2,1)} %bitcast.127), channel_id=1, source_target_pairs={{0,1},{1,0},{2,3},{3,2},{4,5},{5,4},{6,7},{7,6},{8,9},{9,8},{10,11... | collective-permute-start | bytes 786440 | tf_op jit(solution)/shard_map/ppermute | solution.py:608
  214.4 17.0 %collective-permute-start.7 = (bf16[2,2,64,512]{3,2,1,0:T(8,128)(2,1)}, bf16[2,2,64,512]{3,2,1,0:T(8,128)(2,1)}, u32[]{:S(2)}, u32[]{:S(2)}) collective-permute-start(bf16[2,2,64,512]{3,2,1,0:T(8,128)(2,1)} %bitcast.126), channel_id=1, source_target_pairs={{0,2},{1,3},{2,0},{3,1},{4,6},{5,7},{6,4},{7,5},{8,10},{9,11},{10,... | collective-permute-start | bytes 786440 | tf_op jit(solution)/shard_map/ppermute | solution.py:608
  220.2 14.9 %collective-permute-start.8 = (bf16[2,2,64,512]{3,2,1,0:T(8,128)(2,1)}, bf16[2,2,64,512]{3,2,1,0:T(8,128)(2,1)}, u32[]{:S(2)}, u32[]{:S(2)}) collective-permute-start(bf16[2,2,64,512]{3,2,1,0:T(8,128)(2,1)} %bitcast.125), channel_id=1, source_target_pairs={{0,3},{1,2},{2,1},{3,0},{4,7},{5,6},{6,5},{7,4},{8,11},{9,10},{10,... | collective-permute-start | bytes 786440 | tf_op jit(solution)/shard_map/ppermute | solution.py:608
  223.9 36.3 %collective-permute-start.24 = (bf16[2,4,2,64,512]{4,3,2,1,0:T(8,128)(2,1)}, bf16[2,4,2,64,512]{4,3,2,1,0:T(8,128)(2,1)}, u32[]{:S(2)}, u32[]{:S(2)}) collective-permute-start(bf16[2,4,2,64,512]{4,3,2,1,0:T(8,128)(2,1)} %bitcast.124), channel_id=1, source_target_pairs={{0,1},{1,0},{2,3},{3,2},{4,5},{5,4},{6,7},{7,6},{8,9},{9,8},{10,11... | collective-permute-start | bytes 3145736 | tf_op jit(solution)/shard_map/ppermute | solution.py:608
  226.0 34.2 %collective-permute-start.26 = (bf16[1,4,2,16,512]{4,3,2,1,0:T(8,128)(2,1)S(1)}, bf16[1,4,2,16,512]{4,3,2,1,0:T(8,128)(2,1)S(1)}, u32[]{:S(2)}, u32[]{:S(2)}) collective-permute-start(bf16[1,4,2,16,512]{4,3,2,1,0:T(8,128)(2,1)S(1)} %broadcast_in_dim.19), channel_id=1, source_target_pairs={{0,1},{1,0},{2,3},{3,2},{4,5},{5,4},{6,7},{7,6},{8,9},{9,8},{10,11... | collective-permute-start | bytes 393224 | tf_op jit(solution)/shard_map/ppermute | solution.py:608
  283.1 45.0 %collective-permute-start.27 = (bf16[2,4,2,64,512]{4,3,2,1,0:T(8,128)(2,1)}, bf16[2,4,2,64,512]{4,3,2,1,0:T(8,128)(2,1)}, u32[]{:S(2)}, u32[]{:S(2)}) collective-permute-start(bf16[2,4,2,64,512]{4,3,2,1,0:T(8,128)(2,1)} %bitcast.70), channel_id=1, source_target_pairs={{0,1},{1,0},{2,3},{3,2},{4,5},{5,4},{6,7},{7,6},{8,9},{9,8},{10,11... | collective-permute-start | bytes 3145736 | tf_op jit(solution)/shard_map/ppermute | solution.py:608
  283.9 44.2 %collective-permute-start.28 = (bf16[2,4,2,64,512]{4,3,2,1,0:T(8,128)(2,1)}, bf16[2,4,2,64,512]{4,3,2,1,0:T(8,128)(2,1)}, u32[]{:S(2)}, u32[]{:S(2)}) collective-permute-start(bf16[2,4,2,64,512]{4,3,2,1,0:T(8,128)(2,1)} %bitcast.71), channel_id=1, source_target_pairs={{0,1},{1,0},{2,3},{3,2},{4,5},{5,4},{6,7},{7,6},{8,9},{9,8},{10,11... | collective-permute-start | bytes 3145736 | tf_op jit(solution)/shard_map/ppermute | solution.py:608
  283.9 29.2 %collective-permute-start.29 = (bf16[4,400,256]{2,1,0:T(8,128)(2,1)}, bf16[4,400,256]{2,1,0:T(8,128)(2,1)}, u32[]{:S(2)}, u32[]{:S(2)}) collective-permute-start(bf16[4,400,256]{2,1,0:T(8,128)(2,1)} %get-tuple-element.197), channel_id=1, source_target_pairs={{0,4},{4,0},{8,12},{12,8},{16,20},{20,16},{24,28},{28,24},{1,5},{5... | collective-permute-start | bytes 2457608 | tf_op jit(solution)/shard_map/ppermute | solution.py:608
  285.4 27.7 %collective-permute-start.30 = (bf16[4,400,256]{2,1,0:T(8,128)(2,1)}, bf16[4,400,256]{2,1,0:T(8,128)(2,1)}, u32[]{:S(2)}, u32[]{:S(2)}) collective-permute-start(bf16[4,400,256]{2,1,0:T(8,128)(2,1)} %get-tuple-element.198), channel_id=1, source_target_pairs={{0,2},{1,3},{2,0},{3,1},{4,6},{5,7},{6,4},{7,5},{8,10},{9,11},{10,... | collective-permute-start | bytes 2457608 | tf_op jit(solution)/shard_map/ppermute | solution.py:608
  286.0 37.6 %collective-permute-start.31 = (bf16[4,400,256]{2,1,0:T(8,128)(2,1)}, bf16[4,400,256]{2,1,0:T(8,128)(2,1)}, u32[]{:S(2)}, u32[]{:S(2)}) collective-permute-start(bf16[4,400,256]{2,1,0:T(8,128)(2,1)} %get-tuple-element.199), channel_id=1, source_target_pairs={{0,6},{1,7},{2,4},{3,5},{4,2},{5,3},{6,0},{7,1},{8,14},{9,15},{10,... | collective-permute-start | bytes 2457608 | tf_op jit(solution)/shard_map/ppermute | solution.py:620
  339.4 13.4 %collective-permute-start.32 = (bf16[2,4,2,64,512]{4,3,2,1,0:T(8,128)(2,1)}, bf16[2,4,2,64,512]{4,3,2,1,0:T(8,128)(2,1)S(1)}, u32[]{:S(2)}, u32[]{:S(2)}) collective-permute-start(bf16[2,4,2,64,512]{4,3,2,1,0:T(8,128)(2,1)} %bitcast.74), channel_id=1, source_target_pairs={{0,1},{1,0},{2,3},{3,2},{4,5},{5,4},{6,7},{7,6},{8,9},{9,8},{10,11... | collective-permute-start | bytes 3145736 | tf_op jit(solution)/shard_map/ppermute | solution.py:608
  341.0 9.2 %collective-permute-start.40 = (bf16[400,256]{1,0:T(8,128)(2,1)}, bf16[400,256]{1,0:T(8,128)(2,1)S(1)}, u32[]{:S(2)}, u32[]{:S(2)}) collective-permute-start(bf16[400,256]{1,0:T(8,128)(2,1)} %copy-done.66), channel_id=1, source_target_pairs={{0,8},{4,12},{8,0},{12,4},{16,24},{20,28},{24,16},{28,20},{1,9},{5... | collective-permute-start | bytes 614408 | tf_op jit(solution)/shard_map/ppermute | solution.py:608
  342.6 27.2 %collective-permute-start.37 = (bf16[4,256,256]{2,1,0:T(8,128)(2,1)}, bf16[4,256,256]{2,1,0:T(8,128)(2,1)S(1)}, u32[]{:S(2)}, u32[]{:S(2)}) collective-permute-start(bf16[4,256,256]{2,1,0:T(8,128)(2,1)} %copy-done.45), channel_id=1, source_target_pairs={{0,4},{4,0},{8,12},{12,8},{16,20},{20,16},{24,28},{28,24},{1,5},{5... | collective-permute-start | bytes 1572872 | tf_op jit(solution)/shard_map/ppermute | solution.py:608
  347.5 1.4 collective-permute-start.33
  347.5 24.2 %collective-permute-start.38 = (bf16[4,256,256]{2,1,0:T(8,128)(2,1)}, bf16[4,256,256]{2,1,0:T(8,128)(2,1)}, u32[]{:S(2)}, u32[]{:S(2)}) collective-permute-start(bf16[4,256,256]{2,1,0:T(8,128)(2,1)} %copy-done.44), channel_id=1, source_target_pairs={{0,2},{1,3},{2,0},{3,1},{4,6},{5,7},{6,4},{7,5},{8,10},{9,11},{10,... | collective-permute-start | bytes 1572872 | tf_op jit(solution)/shard_map/ppermute | solution.py:608
  349.5 24.3 %collective-permute-start.39 = (bf16[4,256,256]{2,1,0:T(8,128)(2,1)}, bf16[4,256,256]{2,1,0:T(8,128)(2,1)}, u32[]{:S(2)}, u32[]{:S(2)}) collective-permute-start(bf16[4,256,256]{2,1,0:T(8,128)(2,1)} %copy-done.43), channel_id=1, source_target_pairs={{0,6},{1,7},{2,4},{3,5},{4,2},{5,3},{6,0},{7,1},{8,14},{9,15},{10,... | collective-permute-start | bytes 1572872 | tf_op jit(solution)/shard_map/ppermute | solution.py:620
  350.2 16.8 %collective-permute-start.41 = (bf16[400,256]{1,0:T(8,128)(2,1)}, bf16[400,256]{1,0:T(8,128)(2,1)}, u32[]{:S(2)}, u32[]{:S(2)}) collective-permute-start(bf16[400,256]{1,0:T(8,128)(2,1)} %copy-done.65), channel_id=1, source_target_pairs={{0,16},{4,20},{8,24},{12,28},{16,0},{20,4},{24,8},{28,12},{1,17},{... | collective-permute-start | bytes 614408 | tf_op jit(solution)/shard_map/ppermute | solution.py:608
  352.8 15.8 %collective-permute-start.42 = (bf16[400,256]{1,0:T(8,128)(2,1)}, bf16[400,256]{1,0:T(8,128)(2,1)}, u32[]{:S(2)}, u32[]{:S(2)}) collective-permute-start(bf16[400,256]{1,0:T(8,128)(2,1)} %copy-done.64), channel_id=1, source_target_pairs={{0,24},{4,28},{8,16},{12,20},{16,8},{20,12},{24,0},{28,4},{1,25},{... | collective-permute-start | bytes 614408 | tf_op jit(solution)/shard_map/ppermute | solution.py:608
  367.1 12.9 %collective-permute-start.34 = (bf16[4,144,256]{2,1,0:T(8,128)(2,1)S(1)}, bf16[4,144,256]{2,1,0:T(8,128)(2,1)S(1)}, u32[]{:S(2)}, u32[]{:S(2)}) collective-permute-start(bf16[4,144,256]{2,1,0:T(8,128)(2,1)S(1)} %get-tuple-element.207), channel_id=1, source_target_pairs={{0,4},{4,0},{8,12},{12,8},{16,20},{20,16},{24,28},{28,24},{1,5},{5... | collective-permute-start | bytes 884744 | tf_op jit(solution)/shard_map/ppermute | solution.py:608
  368.6 15.3 %collective-permute-start.35 = (bf16[4,144,256]{2,1,0:T(8,128)(2,1)S(1)}, bf16[4,144,256]{2,1,0:T(8,128)(2,1)S(1)}, u32[]{:S(2)}, u32[]{:S(2)}) collective-permute-start(bf16[4,144,256]{2,1,0:T(8,128)(2,1)S(1)} %get-tuple-element.208), channel_id=1, source_target_pairs={{0,2},{1,3},{2,0},{3,1},{4,6},{5,7},{6,4},{7,5},{8,10},{9,11},{10,... | collective-permute-start | bytes 884744 | tf_op jit(solution)/shard_map/ppermute | solution.py:608
  369.9 16.1 %collective-permute-start.36 = (bf16[4,144,256]{2,1,0:T(8,128)(2,1)S(1)}, bf16[4,144,256]{2,1,0:T(8,128)(2,1)S(1)}, u32[]{:S(2)}, u32[]{:S(2)}) collective-permute-start(bf16[4,144,256]{2,1,0:T(8,128)(2,1)S(1)} %get-tuple-element.209), channel_id=1, source_target_pairs={{0,6},{1,7},{2,4},{3,5},{4,2},{5,3},{6,0},{7,1},{8,14},{9,15},{10,... | collective-permute-start | bytes 884744 | tf_op jit(solution)/shard_map/ppermute | solution.py:620
  371.7 24.5 %collective-permute-start.55 = (bf16[400,256]{1,0:T(8,128)(2,1)S(1)}, bf16[400,256]{1,0:T(8,128)(2,1)S(1)}, u32[]{:S(2)}, u32[]{:S(2)}) collective-permute-start(bf16[400,256]{1,0:T(8,128)(2,1)S(1)} %sum_last.3.refs_5_.refs_1_), channel_id=1, source_target_pairs={{0,1},{1,0},{2,3},{3,2},{4,5},{5,4},{6,7},{7,6},{8,9},{9,8},{10,11... | collective-permute-start | bytes 614408 | tf_op jit(solution)/shard_map/ppermute | solution.py:608
  375.9 11.4 %collective-permute-start.46 = (bf16[256,256]{1,0:T(8,128)(2,1)S(1)}, bf16[256,256]{1,0:T(8,128)(2,1)S(1)}, u32[]{:S(2)}, u32[]{:S(2)}) collective-permute-start(bf16[256,256]{1,0:T(8,128)(2,1)S(1)} %get-tuple-element.221), channel_id=1, source_target_pairs={{0,8},{4,12},{8,0},{12,4},{16,24},{20,28},{24,16},{28,20},{1,9},{5... | collective-permute-start | bytes 393224 | tf_op jit(solution)/shard_map/ppermute | solution.py:608
  380.0 13.2 %collective-permute-start.47 = (bf16[256,256]{1,0:T(8,128)(2,1)S(1)}, bf16[256,256]{1,0:T(8,128)(2,1)S(1)}, u32[]{:S(2)}, u32[]{:S(2)}) collective-permute-start(bf16[256,256]{1,0:T(8,128)(2,1)S(1)} %get-tuple-element.222), channel_id=1, source_target_pairs={{0,16},{4,20},{8,24},{12,28},{16,0},{20,4},{24,8},{28,12},{1,17},{... | collective-permute-start | bytes 393224 | tf_op jit(solution)/shard_map/ppermute | solution.py:608
  383.9 9.3 %collective-permute-start.48 = (bf16[256,256]{1,0:T(8,128)(2,1)S(1)}, bf16[256,256]{1,0:T(8,128)(2,1)S(1)}, u32[]{:S(2)}, u32[]{:S(2)}) collective-permute-start(bf16[256,256]{1,0:T(8,128)(2,1)S(1)} %get-tuple-element.223), channel_id=1, source_target_pairs={{0,24},{4,28},{8,16},{12,20},{16,8},{20,12},{24,0},{28,4},{1,25},{... | collective-permute-start | bytes 393224 | tf_op jit(solution)/shard_map/ppermute | solution.py:608
  385.9 17.4 %collective-permute-start.56 = (bf16[400,256]{1,0:T(8,128)(2,1)S(1)}, bf16[400,256]{1,0:T(8,128)(2,1)S(1)}, u32[]{:S(2)}, u32[]{:S(2)}) collective-permute-start(bf16[400,256]{1,0:T(8,128)(2,1)S(1)} %sum_last.3.refs_5_.refs_1_), channel_id=1, source_target_pairs={{0,2},{1,3},{2,0},{3,1},{4,6},{5,7},{6,4},{7,5},{8,10},{9,11},{10,... | collective-permute-start | bytes 614408 | tf_op jit(solution)/shard_map/ppermute | solution.py:608
  387.2 16.3 %collective-permute-start.57 = (bf16[400,256]{1,0:T(8,128)(2,1)S(1)}, bf16[400,256]{1,0:T(8,128)(2,1)S(1)}, u32[]{:S(2)}, u32[]{:S(2)}) collective-permute-start(bf16[400,256]{1,0:T(8,128)(2,1)S(1)} %sum_last.3.refs_5_.refs_1_), channel_id=1, source_target_pairs={{0,3},{1,2},{2,1},{3,0},{4,7},{5,6},{6,5},{7,4},{8,11},{9,10},{10,... | collective-permute-start | bytes 614408 | tf_op jit(solution)/shard_map/ppermute | solution.py:608
  393.2 5.5 %collective-permute-start.43 = (bf16[144,256]{1,0:T(8,128)(2,1)S(1)}, bf16[144,256]{1,0:T(8,128)(2,1)S(1)}, u32[]{:S(2)}, u32[]{:S(2)}) collective-permute-start(bf16[144,256]{1,0:T(8,128)(2,1)S(1)} %get-tuple-element.218), channel_id=1, source_target_pairs={{0,8},{4,12},{8,0},{12,4},{16,24},{20,28},{24,16},{28,20},{1,9},{5... | collective-permute-start | bytes 221192 | tf_op jit(solution)/shard_map/ppermute | solution.py:608
  393.2 5.8 %collective-permute-start.44 = (bf16[144,256]{1,0:T(8,128)(2,1)S(1)}, bf16[144,256]{1,0:T(8,128)(2,1)S(1)}, u32[]{:S(2)}, u32[]{:S(2)}) collective-permute-start(bf16[144,256]{1,0:T(8,128)(2,1)S(1)} %get-tuple-element.219), channel_id=1, source_target_pairs={{0,16},{4,20},{8,24},{12,28},{16,0},{20,4},{24,8},{28,12},{1,17},{... | collective-permute-start | bytes 221192 | tf_op jit(solution)/shard_map/ppermute | solution.py:608
  396.2 7.0 %collective-permute-start.45 = (bf16[144,256]{1,0:T(8,128)(2,1)S(1)}, bf16[144,256]{1,0:T(8,128)(2,1)S(1)}, u32[]{:S(2)}, u32[]{:S(2)}) collective-permute-start(bf16[144,256]{1,0:T(8,128)(2,1)S(1)} %get-tuple-element.220), channel_id=1, source_target_pairs={{0,24},{4,28},{8,16},{12,20},{16,8},{20,12},{24,0},{28,4},{1,25},{... | collective-permute-start | bytes 221192 | tf_op jit(solution)/shard_map/ppermute | solution.py:608
  398.7 6.8 %collective-permute-start.52 = (bf16[256,256]{1,0:T(8,128)(2,1)S(1)}, bf16[256,256]{1,0:T(8,128)(2,1)S(1)}, u32[]{:S(2)}, u32[]{:S(2)}) collective-permute-start(bf16[256,256]{1,0:T(8,128)(2,1)S(1)} %sum_last.4.refs_4_.refs_1_), channel_id=1, source_target_pairs={{0,1},{1,0},{2,3},{3,2},{4,5},{5,4},{6,7},{7,6},{8,9},{9,8},{10,11... | collective-permute-start | bytes 393224 | tf_op jit(solution)/shard_map/ppermute | solution.py:608
  399.0 8.4 %collective-permute-start.53 = (bf16[256,256]{1,0:T(8,128)(2,1)S(1)}, bf16[256,256]{1,0:T(8,128)(2,1)S(1)}, u32[]{:S(2)}, u32[]{:S(2)}) collective-permute-start(bf16[256,256]{1,0:T(8,128)(2,1)S(1)} %sum_last.4.refs_4_.refs_1_), channel_id=1, source_target_pairs={{0,2},{1,3},{2,0},{3,1},{4,6},{5,7},{6,4},{7,5},{8,10},{9,11},{10,... | collective-permute-start | bytes 393224 | tf_op jit(solution)/shard_map/ppermute | solution.py:608
  403.3 6.3 %collective-permute-start.54 = (bf16[256,256]{1,0:T(8,128)(2,1)S(1)}, bf16[256,256]{1,0:T(8,128)(2,1)S(1)}, u32[]{:S(2)}, u32[]{:S(2)}) collective-permute-start(bf16[256,256]{1,0:T(8,128)(2,1)S(1)} %sum_last.4.refs_4_.refs_1_), channel_id=1, source_target_pairs={{0,3},{1,2},{2,1},{3,0},{4,7},{5,6},{6,5},{7,4},{8,11},{9,10},{10,... | collective-permute-start | bytes 393224 | tf_op jit(solution)/shard_map/ppermute | solution.py:608
  403.3 7.9 %collective-permute-start.49 = (bf16[144,256]{1,0:T(8,128)(2,1)S(1)}, bf16[144,256]{1,0:T(8,128)(2,1)S(1)}, u32[]{:S(2)}, u32[]{:S(2)}) collective-permute-start(bf16[144,256]{1,0:T(8,128)(2,1)S(1)} %sum_last.5.refs_1_), channel_id=1, source_target_pairs={{0,1},{1,0},{2,3},{3,2},{4,5},{5,4},{6,7},{7,6},{8,9},{9,8},{10,11... | collective-permute-start | bytes 221192 | tf_op jit(solution)/shard_map/ppermute | solution.py:608
  403.5 7.7 %collective-permute-start.50 = (bf16[144,256]{1,0:T(8,128)(2,1)S(1)}, bf16[144,256]{1,0:T(8,128)(2,1)S(1)}, u32[]{:S(2)}, u32[]{:S(2)}) collective-permute-start(bf16[144,256]{1,0:T(8,128)(2,1)S(1)} %sum_last.5.refs_1_), channel_id=1, source_target_pairs={{0,2},{1,3},{2,0},{3,1},{4,6},{5,7},{6,4},{7,5},{8,10},{9,11},{10,... | collective-permute-start | bytes 221192 | tf_op jit(solution)/shard_map/ppermute | solution.py:608
  405.5 6.6 %collective-permute-start.51 = (bf16[144,256]{1,0:T(8,128)(2,1)S(1)}, bf16[144,256]{1,0:T(8,128)(2,1)S(1)}, u32[]{:S(2)}, u32[]{:S(2)}) collective-permute-start(bf16[144,256]{1,0:T(8,128)(2,1)S(1)} %sum_last.5.refs_1_), channel_id=1, source_target_pairs={{0,3},{1,2},{2,1},{3,0},{4,7},{5,6},{6,5},{7,4},{8,11},{9,10},{10,... | collective-permute-start | bytes 221192 | tf_op jit(solution)/shard_map/ppermute | solution.py:608
  (85 other events, 1142.4 us)

commit v2 on v1

--- a/solution.py
+++ b/solution.py
@@ -21,12 +21,15 @@
 HALF = jnp.bfloat16
 HALVES = 2
 UNITS = 16
-VMEM = 40 << 20
+VMEM = 62 << 20
+SLOWER = 4
 
 NORMED, MIXED, SECOND, ACTIVE = 0, 1, 2, 3
 LEFTS = 3 + CHUNKS
 TRIPLE_BACK, ATTEND_BACK, HIDDEN_BACK, BRANCH_BACK = 0, 3, 4, 4 + CHUNKS
 RIGHTS = 5 + CHUNKS
+INNER, COTANGENT = 0, 1
+BACK, RESULT = 0, 1
 GAIN, OFFSET, BIAS, WEIGH, SHIFT, NUDGE, LIFT = 0, 1, 2, 3, 4, 5, 6
 SUMS = 6 + CHUNKS
 
@@ -163,7 +166,7 @@
         ),
         input_output_aliases={first + at: out for at, out in enumerate(aliases)},
         compiler_params=pltpu.CompilerParams(vmem_limit_bytes=VMEM),
-        cost_estimate=pl.CostEstimate(flops=flops, bytes_accessed=moved, transcendentals=0),
+        cost_estimate=pl.CostEstimate(flops=flops * SLOWER, bytes_accessed=moved * SLOWER, transcendentals=0),
         name=name,
     )(*scalars, *[array for array, _ in ins], *extra)
 
@@ -182,8 +185,8 @@
 
 def space_forward_body(place, rows_in, cotangent, *refs, window, pieces):
     gain, offset, entry, leave, bias, weigh, shift, widen, lift, narrow, nudge = refs[:11]
-    inners, cuts = refs[11 : 11 + pieces], refs[11 + pieces : 11 + 2 * pieces]
-    lefts, triple, weights, middles, slopes = refs[11 + 2 * pieces :]
+    sent = refs[11 : 11 + pieces]
+    lefts, triple, weights, middles, slopes = refs[11 + pieces :]
     step = pl.program_id(0)
     shape = rows_in.shape
     rows = rows_in[...].reshape(-1, D).astype(FLOAT)
@@ -211,8 +214,8 @@
 
         @pl.when(step == piece)
         def _(piece=piece):
-            inners[piece][...] = inner
-            cuts[piece][...] = cotangent[...]
+            sent[piece][INNER] = inner
+            sent[piece][COTANGENT] = cotangent[...]
 
 
 def space_forward(place, frames, cotangent, params, half, pieces, before):
@@ -224,7 +227,8 @@
     cut = pl.BlockSpec(block, lambda i, place: (0, (place[0] ^ i) * HALVES + half, 0, 0))
     at = lambda i, place: half * pieces + i
     attended = (rows // window, PAIRS, window, 2 * window)
-    outs = [(block, HALF, pl.BlockSpec(block, lambda i, place: (0, 0, 0, 0)))] * (2 * pieces)
+    both = (2, *block)
+    outs = [(both, HALF, pl.BlockSpec(both, lambda i, place: (0,) * 5))] * pieces
     outs += [
         ((LEFTS, count, D), HALF, slab_spec(LEFTS, rows, at)),
         ((count, 3 * D), HALF, row_spec(rows, 3 * D, at)),
@@ -243,26 +247,26 @@
         [place],
         [(frames, cut), (cotangent, cut)] + plain(params),
         outs,
-        aliases={2 * pieces + number: array for number, array in enumerate(before)},
+        aliases={pieces + number: array for number, array in enumerate(before)},
         flops=2 * rows * pieces * D * (4 * D + 2 * FF),
         moved=rows * pieces * (8 * D + 2 * LEFTS * D + 10 * D + 4 * D + 2 * FF),
     )
-    return made[:pieces], made[pieces : 2 * pieces], made[2 * pieces :]
-
-
-def by_position(refs, frames_of, positions):
-    parts = [ref[frame].astype(FLOAT) for ref in refs for frame in range(frames_of)]
+    return made[:pieces], made[pieces:]
+
+
+def by_position(refs, which, frames_of, positions):
+    parts = [ref[which, frame].astype(FLOAT) for ref in refs for frame in range(frames_of)]
     return jnp.concatenate(
         [part[start : start + 8] for start in range(0, positions, 8) for part in parts], axis=0
     )
 
 
-def by_frame(values, refs, frames_of, positions):
+def by_frame(values, refs, which, frames_of, positions):
     total = len(refs) * frames_of
     for at, ref in enumerate(refs):
         for frame in range(frames_of):
             number = at * frames_of + frame
-            ref[frame] = jnp.concatenate(
+            ref[which, frame] = jnp.concatenate(
                 [
                     values[(group * total + number) * 8 : (group * total + number) * 8 + 8]
                     for group in range(positions // 8)
@@ -291,16 +295,14 @@
 
 
 def time_body(place, lengths, *refs, pieces):
-    inners, cotangents = refs[:pieces], refs[pieces : 2 * pieces]
-    gain, offset, entry, leave, bias, weigh, shift, widen, lift, narrow, nudge = refs[
-        2 * pieces : 2 * pieces + 11
-    ]
+    came = refs[:pieces]
+    gain, offset, entry, leave, bias, weigh, shift, widen, lift, narrow, nudge = refs[pieces : pieces + 11]
+    sent = refs[pieces + 11 : 2 * pieces + 11]
     refs = refs[2 * pieces + 11 :]
-    results, backs = refs[:pieces], refs[pieces : 2 * pieces]
-    lefts, rights, sums, triple, weights, mixed_back, mask = refs[2 * pieces :]
-    frames_of, positions, _ = inners[0].shape
+    lefts, rights, sums, triple, weights, mixed_back, mask = refs
+    _, frames_of, positions, _ = came[0].shape
     window = 8 * pieces * frames_of
-    rows = by_position(inners, frames_of, positions)
+    rows = by_position(came, INNER, frames_of, positions)
     blocks = rows.shape[0] // window
 
     @pl.when(pl.program_id(0) == 0)
@@ -317,7 +319,7 @@
     unit_two, inverse_two = unit_of(middle)
     second = (unit_two * weigh[...] + shift[...]).astype(HALF)
     lefts[SECOND] = second
-    upstream = by_position(cotangents, frames_of, positions)
+    upstream = by_position(came, COTANGENT, frames_of, positions)
     branch_back = upstream.astype(HALF)
     rights[BRANCH_BACK] = branch_back
     sums[NUDGE] += column_sum(upstream)
@@ -334,7 +336,7 @@
         sums[LIFT + chunk] += column_sum(hidden_back)
         total = total + dot(active, narrow[at, :])
         second_back = second_back + dot_right(hidden_low, widen[:, at])
-    by_frame(total, results, frames_of, positions)
+    by_frame(total, sent, RESULT, frames_of, positions)
     sums[WEIGH] += column_sum(second_back * unit_two)
     sums[SHIFT] += column_sum(second_back)
     middle_back = upstream + norm_back(second_back * weigh[...], unit_two, inverse_two)
@@ -355,23 +357,23 @@
     sums[GAIN] += column_sum(normed_back * unit)
     sums[OFFSET] += column_sum(normed_back)
     rows_back = middle_back + norm_back(normed_back * gain[...], unit, inverse)
-    by_frame(rows_back, backs, frames_of, positions)
-
-
-def time_block(place, lengths, inners, cotangents, params, half, before, step_rows=256):
-    pieces = len(inners)
-    per_group, each, window, _ = inners[0].shape
+    by_frame(rows_back, sent, BACK, frames_of, positions)
+
+
+def time_block(place, lengths, came, params, half, before, step_rows=256):
+    pieces = len(came)
+    _, per_group, each, window, _ = came[0].shape
     positions = each * window
-    flat = (per_group, positions, D)
+    flat = (2, per_group, positions, D)
     frames = per_group * pieces
     batch = min(max(step_rows // frames, 16), positions)
     rows = batch * frames
     steps = positions // batch
     count = positions * frames
     attended = 8 * frames
-    spec = pl.BlockSpec((per_group, batch, D), lambda i, *_: (0, i, 0))
+    spec = pl.BlockSpec((2, per_group, batch, D), lambda i, *_: (0, 0, i, 0))
     at = lambda i, *_: half * steps + i
-    outs = [(flat, HALF, spec)] * (2 * pieces)
+    outs = [(flat, HALF, spec)] * pieces
     outs += [
         ((LEFTS, HALVES * count, D), HALF, slab_spec(LEFTS, rows, at)),
         ((RIGHTS, HALVES * count, D), HALF, slab_spec(RIGHTS, rows, at)),
@@ -382,7 +384,7 @@
         "time_block",
         (steps,),
         [place, lengths],
-        [(array.reshape(flat), spec) for array in (*inners, *cotangents)] + plain(params),
+        [(array.reshape(flat), spec) for array in came] + plain(params),
         outs,
         scratch=[
             pltpu.VMEM((rows, 3 * D), HALF),
@@ -390,20 +392,19 @@
             pltpu.VMEM((rows, D), HALF),
             pltpu.VMEM((attended, 2 * attended), FLOAT),
         ],
-        aliases={2 * pieces + number: array for number, array in enumerate(before)},
+        aliases={pieces + number: array for number, array in enumerate(before)},
         flops=4 * count * D * (4 * D + 2 * FF),
         moved=count * 2 * D * (4 + LEFTS + RIGHTS) + 2 * D * (4 * D + 2 * FF),
     )
-    shape = (per_group, each, window, D)
-    results = [array.reshape(shape) for array in made[:pieces]]
-    backs = [array.reshape(shape) for array in made[pieces : 2 * pieces]]
-    return results, backs, made[2 * pieces : 2 * pieces + 2], made[2 * pieces + 2]
+    shape = (2, per_group, each, window, D)
+    sent = [array.reshape(shape) for array in made[:pieces]]
+    return sent, made[pieces : pieces + 2], made[pieces + 2]
 
 
 def feed_back_body(place, *refs, pieces):
     weigh, widen, narrow = refs[:3]
-    backs, results = refs[3 : 3 + pieces], refs[3 + pieces : 3 + 2 * pieces]
-    middles, slopes, outcome, rights, middles_back, sums, upstream_low = refs[3 + 2 * pieces :]
+    came = refs[3 : 3 + pieces]
+    middles, slopes, outcome, rights, middles_back, sums, upstream_low = refs[3 + pieces :]
     step = pl.program_id(0)
 
     @pl.when(step == 0)
@@ -414,8 +415,8 @@
 
         @pl.when(step == piece)
         def _(piece=piece):
-            upstream_low[...] = backs[piece][...].reshape(-1, D)
-            outcome[...] = results[piece][...]
+            upstream_low[...] = came[piece][BACK].reshape(-1, D)
+            outcome[...] = came[piece][RESULT]
 
     branch_back = upstream_low[...]
     rights[4] = branch_back
@@ -437,16 +438,16 @@
     sums[BIAS] += column_sum(middle_back)
 
 
-def feed_back(place, shape, params, backs, results, middles, slopes, after):
-    pieces = len(backs)
+def feed_back(place, shape, params, came, middles, slopes, after):
+    pieces = len(came)
     per_group, windows, window, _ = shape
-    block = backs[0].shape
+    block = came[0].shape[1:]
     rows = per_group * block[1] * window
     count = rows * pieces
     across = pieces // HALVES
     cut = pl.BlockSpec(block, lambda i, place: (0, (place[0] ^ (i % across)) * HALVES + i // across, 0, 0))
     at = lambda i, place: i
-    ins = plain([params[5], params[7], params[9]]) + plain(backs) + plain(results)
+    ins = plain([params[5], params[7], params[9]]) + plain(came)
     ins += [(middles, row_spec(rows, D, at)), (slopes, row_spec(rows, FF, at))]
     return run(
         functools.partial(feed_back_body, pieces=pieces),
@@ -528,7 +529,7 @@
     )
 
 
-def gradient_body(core, left_at, right_at, left, right, *outs, narrows, sent):
+def gradient_body(core, left_at, right_at, left, right, *outs, narrows, starts):
     step = pl.program_id(0)
     value = dot_left(left[0], right[0]).astype(HALF)
     if narrows:
@@ -545,60 +546,174 @@
                     own[sub, shard] = jnp.where(core[0] == 0, one, two)
                     away[sub, shard] = jnp.where(core[0] == 0, two, one)
 
-    if sent:
-        away, own = outs
-
-        @pl.when((step >= narrows) & (step < narrows + sent))
-        def _():
-            away[0] = value.reshape(away.shape[1:])
-
-        @pl.when(step >= narrows + sent)
-        def _():
-            own[0] = value.reshape(own.shape[1:])
-
-
-def gradient_tiles(core, lefts, rights, narrow, tiles, batch, after=()):
-    sent = len(tiles) // 2
+    for out, (start, size) in zip(outs, starts):
+
+        @pl.when((step >= start) & (step < start + size))
+        def _(out=out):
+            out[0] = value.reshape(out.shape[1:])
+
+
+def gradient_tiles(core, lefts, rights, narrow, groups, batch, after=()):
     narrows = 0 if narrow is None else CHUNKS
-    order = [jnp.arange(sent) + sent * (1 - core), jnp.arange(sent) + sent * core]
-    order = jnp.concatenate(order).astype(jnp.int32)
-    tables = []
-    for which in range(2):
-        table = jnp.array([tile[which] for tile in tiles], jnp.int32)[order]
-        first = [ACTIVE + i if which == 0 else narrow for i in range(narrows)]
-        tables.append(jnp.concatenate([jnp.array(first, jnp.int32), table]))
+    lists = [[ACTIVE + i for i in range(narrows)], [narrow] * narrows]
+    tables = [[jnp.array(a, jnp.int32)] for a in lists]
     count = lefts.shape[1]
     block = (1, count, CHUNK)
     rows = D // batch
-    outs = []
+    outs, starts, start = [], [], narrows
     if narrows:
         shards = batch // CHUNKS
         spec = pl.BlockSpec(
             (2, shards, rows, CHUNK), lambda i, *_: (0, jnp.minimum(i, narrows - 1), 0, 0)
         )
         outs += [((2, batch, rows, CHUNK), HALF, spec)] * 2
-    if sent:
-        for start in (narrows, narrows + sent):
-            spec = pl.BlockSpec(
-                (1, batch, rows, CHUNK),
-                lambda i, *_, start=start: (jnp.clip(i - start, 0, sent - 1), 0, 0, 0),
-            )
-            outs.append(((sent, batch, rows, CHUNK), HALF, spec))
-    made = run(
-        functools.partial(gradient_body, narrows=narrows, sent=sent),
+    for tiles, which in groups:
+        size = len(tiles) // 2
+        for side in range(2):
+            halves = [jnp.array([t[side] for t in tiles[h * size : (h + 1) * size]], jnp.int32) for h in range(2)]
+            tables[side].append(jnp.where(which == 0, halves[0], halves[1]))
+        spec = pl.BlockSpec(
+            (1, batch, rows, CHUNK),
+            lambda i, *_, start=start, size=size: (jnp.clip(i - start, 0, size - 1), 0, 0, 0),
+        )
+        outs.append(((size, batch, rows, CHUNK), HALF, spec))
+        starts.append((start, size))
+        start += size
+    return run(
+        functools.partial(gradient_body, narrows=narrows, starts=starts),
         "gradient_tiles",
-        (narrows + len(tiles),),
-        [core.reshape(1), *tables],
+        (start,),
+        [core.reshape(1), *[jnp.concatenate(table) for table in tables]],
         [
             (lefts, pl.BlockSpec(block, lambda i, core, left, right: (left[i], 0, 0))),
             (rights, pl.BlockSpec(block, lambda i, core, left, right: (right[i], 0, 0))),
         ],
         outs,
         after=after,
-        flops=2 * count * CHUNK * CHUNK * (narrows + len(tiles)),
-        moved=4 * count * CHUNK * (narrows + len(tiles)),
-    )
-    return made[::2], made[1::2]
+        flops=2 * count * CHUNK * CHUNK * start,
+        moved=4 * count * CHUNK * start,
+    )
+
+
+def scatter_body(left_at, right_at, left, right, out, buffer, sems, *, narrows, units):
+    step = pl.program_id(0)
+    steps = pl.num_programs(0)
+    slot = step % 2
+    batch, win, _, rows, width = out.shape
+
+    def copies(number, at, narrow):
+        made = []
+        for half in range(2):
+            x = pl.ds(half * width, width)
+            if narrow:
+                shards = batch // narrows
+                source = buffer.at[at].reshape(shards, 4, rows, CHUNK)
+                for sub in range(4):
+                    unit = sub * 2 + half
+                    made.append(
+                        pltpu.make_async_copy(
+                            source.at[:, sub, :, x],
+                            out.at[pl.ds(number * shards, shards), unit // units, unit % units],
+                            sems.at[at, sub * 2 + half],
+                        )
+                    )
+            else:
+                unit = 8 + (number - narrows) * 2 + half
+                made.append(
+                    pltpu.make_async_copy(
+                        buffer.at[at].reshape(batch, rows, CHUNK).at[:, :, x],
+                        out.at[:, unit // units, unit % units],
+                        sems.at[at, half],
+                    )
+                )
+        return made
+
+    def each(number, at, act):
+        @pl.when(number < narrows)
+        def _():
+            for copy in copies(number, at, True):
+                act(copy)
+
+        @pl.when(number >= narrows)
+        def _():
+            for copy in copies(number, at, False):
+                act(copy)
+
+    @pl.when(step >= 2)
+    def _():
+        each(step - 2, slot, lambda copy: copy.wait())
+
+    buffer[slot] = dot_left(left[0], right[0]).astype(HALF)
+    each(step, slot, lambda copy: copy.start())
+
+    @pl.when(step == steps - 1)
+    def _():
+        each(step - 1, 1 - slot, lambda copy: copy.wait())
+        each(step, slot, lambda copy: copy.wait())
+
+
+def scattered_tiles(lefts, rights, narrow, tiles, batch, win, after):
+    units = 2 * (CHUNKS + len(tiles)) // win
+    rows, width = D // batch, CHUNK // 2
+    count = lefts.shape[1]
+    block = (1, count, CHUNK)
+    left_at = jnp.array([ACTIVE + i for i in range(CHUNKS)] + [t[0] for t in tiles], jnp.int32)
+    right_at = jnp.array([narrow] * CHUNKS + [t[1] for t in tiles], jnp.int32)
+    steps = CHUNKS + len(tiles)
+    (out,) = run(
+        functools.partial(scatter_body, narrows=CHUNKS, units=units),
+        "scattered_tiles",
+        (steps,),
+        [left_at, right_at],
+        [
+            (lefts, pl.BlockSpec(block, lambda i, left, right: (left[i], 0, 0))),
+            (rights, pl.BlockSpec(block, lambda i, left, right: (right[i], 0, 0))),
+        ],
+        [((batch, win, units, rows, width), HALF, pl.BlockSpec(memory_space=pl.ANY))],
+        scratch=[pltpu.VMEM((2, CHUNK, CHUNK), HALF), pltpu.SemaphoreType.DMA((2, 8))],
+        after=after,
+        flops=2 * count * CHUNK * CHUNK * steps,
+        moved=4 * count * CHUNK * steps,
+    )
+    return out.reshape(batch * win, units * rows, width)
+
+
+def spread_body(place, *refs, pieces, layout):
+    ins, outs, held = refs[:pieces], refs[pieces:-1], refs[-1]
+    for piece, ref in enumerate(ins):
+        held[place[0] ^ piece] = ref[...].astype(FLOAT)
+    units = held.shape[1]
+    rows, width = held.shape[2:]
+    for out, places in zip(outs, layout):
+        for unit, row, column in places:
+            out[row * rows : (row + 1) * rows, column * width : (column + 1) * width] = held[
+                unit // units, unit % units
+            ]
+
+
+def spread_units(place, total, win, rows, after=()):
+    units = total.shape[0] // rows
+    width = total.shape[1]
+    pieces = [swap(total, "win", number).reshape(units, rows, width) for number in range(win)]
+    spot = lambda tile, row, column: [(8 + tile * 2 + half, row, column * 2 + half) for half in range(2)]
+    narrow = [(sub * 2 + half, sub, half) for sub in range(4) for half in range(2)]
+    layout = [
+        sum([spot(chunk, 0, chunk) for chunk in range(CHUNKS)], []),
+        narrow,
+        sum([spot(CHUNKS + part, 0, part) for part in range(3)], []),
+        spot(CHUNKS + 3, 0, 0),
+    ]
+    shapes = [(rows, FF), (4 * rows, D), (rows, 3 * D), (rows, D)]
+    return run(
+        functools.partial(spread_body, pieces=win, layout=layout),
+        "spread_units",
+        (1,),
+        [place],
+        plain(pieces),
+        [(s, FLOAT, whole(s)) for s in shapes],
+        scratch=[pltpu.VMEM((win, units, rows, width), FLOAT)],
+        after=after,
+    )
 
 
 def swap(value, axis, mask):
@@ -718,7 +833,7 @@
         self.mark = [total]
         self.pieces = [swap(total, "win", number) for number in range(self.win)]
 
-    def unpack(self, layout, shapes):
+    def unpack(self, layout, shapes, after=()):
         return run(
             functools.partial(
                 unpack_body, pieces=self.win, across=self.across, layout=layout
@@ -729,6 +844,7 @@
             plain(self.pieces),
             [(s, FLOAT, whole(s)) for s in shapes],
             scratch=[pltpu.VMEM((2, self.rows, CHUNK), FLOAT)],
+            after=after,
         )
 
 
@@ -736,21 +852,21 @@
 
 
 def small_tiles(core, sums, batch):
-    vectors = sums[:6, 0].reshape(6, batch, D // batch).swapaxes(0, 1).reshape(batch, -1)
-    lifts = sums[LIFT:, 0].reshape(batch, FF // batch)
-    both = [jnp.pad(a, ((0, 0), (0, CHUNK - a.shape[1]))).astype(HALF) for a in (vectors, lifts)]
-    both = [jnp.broadcast_to(a[None, :, None], (1, batch, SMALL_ROWS, CHUNK)) for a in both]
-    own = jnp.where(core == 0, both[0], both[1])
-    away = jnp.where(core == 0, both[1], both[0])
-    return away, own
+    blocks = len(sums)
+    sums = jnp.stack(sums)[:, :, 0]
+    vectors = sums[:, :6].reshape(blocks, 6, batch, -1).transpose(2, 0, 1, 3).reshape(batch, blocks, -1)
+    lifts = sums[:, LIFT:].reshape(blocks, batch, -1).swapaxes(0, 1)
+    pad = lambda a: jnp.pad(a, ((0, 0), (0, SMALL_ROWS - blocks), (0, CHUNK - a.shape[2])))
+    both = [pad(a).astype(HALF)[None] for a in (vectors, lifts)]
+    return jnp.where(core == 0, both[1], both[0]), jnp.where(core == 0, both[0], both[1])
 
 
 ENTRY_TILES = [(NORMED, TRIPLE_BACK + part) for part in range(3)] + [(MIXED, ATTEND_BACK)]
 WIDEN_TILES = [(SECOND, HIDDEN_BACK + chunk) for chunk in range(CHUNKS)]
-TIME_TILES = WIDEN_TILES[:2] + ENTRY_TILES[:2] + WIDEN_TILES[2:] + ENTRY_TILES[2:]
-
-
-def entry_places(rows, start):
+TIME_TILES = WIDEN_TILES + ENTRY_TILES
+
+
+def attend_places(rows, start):
     spot = lambda tile: (tile // 2, start + tile % 2 * rows, rows, 0, CHUNK)
     return [
         [(*spot(part), 0, part * CHUNK) for part in range(3)],
@@ -758,7 +874,7 @@
     ], [(rows, 3 * D), (rows, D)]
 
 
-def widen_places(rows, start):
+def feed_places(rows, start):
     narrows = [(sub // 2, start + sub % 2 * rows, rows, 0, CHUNK, sub * rows, 0) for sub in range(4)]
     start += 2 * rows
     widens = [
@@ -768,9 +884,12 @@
 
 
 def small_places(rows, start):
-    layout = [[(0, start, 1, number * rows, rows, 0, 0)] for number in range(6)]
-    layout.append([(1, start, 1, 0, 4 * rows, 0, 0)])
-    return layout, [(1, rows)] * 6 + [(1, 4 * rows)]
+    layout, shapes = [], []
+    for block in range(2):
+        layout += [[(0, start + block, 1, number * rows, rows, 0, 0)] for number in range(6)]
+        layout.append([(1, start + block, 1, 0, 4 * rows, 0, 0)])
+        shapes += [(1, rows)] * 6 + [(1, 4 * rows)]
+    return layout, shapes
 
 
 def local(*args):
@@ -786,87 +905,67 @@
     rows_in, cotangent = frames.reshape(shape), cotangent.reshape(shape)
     rows = D // batch
 
-    kept, inners, cotangents = [], [], []
+    kept, came = [], []
     for half in range(HALVES):
-        inner, cut, kept = space_forward(place, rows_in, cotangent, space, half, win, kept)
-        inners.append(exchange(inner))
-        cotangents.append(exchange(cut))
-    space_lefts, triple, weights, middles, slopes = kept
-    results, backs, slabs, time_sums = [], [], [], []
+        sent, kept = space_forward(place, rows_in, cotangent, space, half, win, kept)
+        came.append(exchange(sent))
+    lefts, triple, weights, middles, slopes = kept
+    backs, slabs, time_sums = [], [], []
     for half in range(HALVES):
-        result, back, slabs, sums = time_block(
-            place, video_frames, inners[half], cotangents[half], time, half, slabs
-        )
-        backs += exchange(back)
-        results += exchange(result)
+        sent, slabs, sums = time_block(place, video_frames, came[half], time, half, slabs)
+        backs += exchange(sent)
         time_sums.append(sums)
-    time_lefts, time_rights = slabs
-
-    away, own = gradient_tiles(
-        core, time_lefts, time_rights, BRANCH_BACK, TIME_TILES, batch
-    )
-    mark = own[:1]
-    small_away, small_own = small_tiles(core, sum(time_sums), batch)
-    time_sum = Reduction(place, [*away, small_away], [*own, small_own])
+
+    time_tiles = scattered_tiles(*slabs, BRANCH_BACK, TIME_TILES, batch, win, backs[1:win])
+    time_total = lax.psum_scatter(time_tiles, ("batch", "win"), scatter_dimension=0, tiled=True)[0]
     outcome, feed_rights, middles_back, feed_sums = feed_back(
-        place, shape, space, backs, results, middles, slopes, mark
-    )
-    time_sum.cores([middles_back])
-    away, own = gradient_tiles(
-        core,
-        space_lefts,
-        feed_rights,
-        CHUNKS,
-        [(SECOND, chunk) for chunk in range(CHUNKS)],
-        batch,
-        time_sum.mark,
-    )
-    feed_sum = Reduction(place, away, own)
+        place, shape, space, backs, middles, slopes, [time_tiles]
+    )
+    feed_tiles = [(SECOND, chunk) for chunk in range(CHUNKS)]
+    narrow_away, narrow_own, away = gradient_tiles(
+        core, lefts, feed_rights, CHUNKS, [(feed_tiles, 1 - core)], batch
+    )
+    (own,) = gradient_tiles(core, lefts, feed_rights, None, [(feed_tiles, core)], batch, [away])
+    feed_sum = Reduction(place, [narrow_away, away], [narrow_own, own])
+    feed_sum.cores()
     delta, attend_rights, attend_sums = attention_back(
-        place, rows_in, space, triple, weights, middles_back, 2 * win, own[:1]
-    )
-    time_sum.chips([delta])
-    feed_sum.cores(time_sum.mark)
-    away, own = gradient_tiles(
-        core,
-        space_lefts,
-        attend_rights,
-        None,
-        [(NORMED, part) for part in range(3)] + [(MIXED, 3)],
-        batch,
-        feed_sum.mark,
-    )
-    small_away, small_own = small_tiles(core, feed_sums + attend_sums, batch)
-    attend_sum = Reduction(place, [*away, small_away], [*own, small_own])
-    attend_sum.cores(own[:1])
-    time_sum.last(attend_sum.mark)
-    feed_sum.chips(time_sum.mark)
+        place, rows_in, space, triple, weights, middles_back, 2 * win, feed_sum.mark
+    )
+    attend_tiles = [(NORMED, part) for part in range(3)] + [(MIXED, 3)]
+    (away,) = gradient_tiles(
+        core, lefts, attend_rights, None, [(attend_tiles, 1 - core)], batch
+    )
+    feed_sum.chips([away])
+    (own,) = gradient_tiles(
+        core, lefts, attend_rights, None, [(attend_tiles, core)], batch, feed_sum.mark
+    )
+    small_away, small_own = small_tiles(core, [feed_sums + attend_sums, sum(time_sums)], batch)
+    attend_sum = Reduction(place, [away, small_away], [own, small_own])
+    attend_sum.cores()
+    feed_sum.last(attend_sum.mark)
     attend_sum.chips(feed_sum.mark)
-    feed_sum.last(attend_sum.mark)
-    attend_sum.last(feed_sum.mark)
+    feed_layout, feed_shapes = feed_places(rows, 0)
+    feed_grads = feed_sum.unpack(feed_layout, feed_shapes, attend_sum.mark)
+    attend_sum.last(feed_grads[:1])
+    time_grads = spread_units(place, time_total, win, rows, attend_sum.mark)
+    attend_layout, attend_shapes = attend_places(rows, 0)
+    small_layout, small_shapes = small_places(rows, 2 * rows)
+    attend_grads = attend_sum.unpack(
+        attend_layout + small_layout, attend_shapes + small_shapes, time_grads[:1]
+    )
+    smalls = [a.reshape(-1) for a in attend_grads[2:]]
+
+    def collected(grads, smalls):
+        widen, narrow, entry, leave = grads
+        gain, offset, bias, weigh, shift, nudge, lift = smalls
+        return gain, offset, entry, leave, bias, weigh, shift, widen, lift, narrow, nudge
 
     return (
         outcome.reshape(frames.shape),
         delta.reshape(frames.shape),
-        *collected(feed_sum, attend_sum, rows),
-        *collected(time_sum, time_sum, rows),
-    )
-
-
-def collected(feed, attend, rows):
-    feed_layout, feed_shapes = widen_places(rows, 0)
-    attend_layout, attend_shapes = entry_places(rows, 4 * rows if feed is attend else 0)
-    small_layout, small_shapes = small_places(rows, attend.rows - SMALL_ROWS)
-    if feed is attend:
-        made = feed.unpack(
-            feed_layout + attend_layout + small_layout, feed_shapes + attend_shapes + small_shapes
-        )
-    else:
-        made = feed.unpack(feed_layout, feed_shapes)
-        made += attend.unpack(attend_layout + small_layout, attend_shapes + small_shapes)
-    widen, narrow, entry, leave = made[:4]
-    gain, offset, bias, weigh, shift, nudge, lift = [a.reshape(-1) for a in made[4:]]
-    return gain, offset, entry, leave, bias, weigh, shift, widen, lift, narrow, nudge
+        *collected([*feed_grads, *attend_grads[:2]], smalls[:7]),
+        *collected(time_grads, smalls[7:]),
+    )
 
 
 def solution(mesh):

time: 415 us -> 321 us (0.77)
  waiting for transfers between devices: 87.1 us -> 24 us
  local copies, waits for them, and re-layouts: 54.9 us -> 11.2 us
  Pallas kernels: 212 us -> 236 us
  starting transfers between devices: 56.2 us -> 32.6 us
  between operations: 1.53 us -> 14.4 us
    ppermute x55 -> x35, waiting for transfers between devices: 72.4 us -> 11.9 us  [swap(): return lax.ppermute(value, axis, [(i, i ^ mask) for i in range(size)])]
    unnamed x182 -> x68, local copies, waits for them, and re-layouts: 45.6 us -> 8.43 us
    pallas_call x21 -> x20, Pallas kernels: 212 us -> 236 us  [run(): pl.pallas_call(inner, out_shape=[jax.ShapeDtypeStruct(shape, kind) for sh...]
    ppermute x55 -> x35, starting transfers between devices: 53.4 us -> 30.9 us  [swap(): return lax.ppermute(value, axis, [(i, i ^ mask) for i in range(size)])]
    ppermute x3 -> x2, waiting for transfers between devices: 14.7 us -> 6.44 us  [move(): return lax.ppermute(value, ('batch', 'win'), pairs)]
    reduce_scatter x0 -> x1, waiting for transfers between devices: none -> 5.65 us  [local(): lax.psum_scatter(time_tiles, ('batch', 'win'), scatter_dimension=0, tiled...]
  transfers between devices with their start and end apart: 58 -> 38, of which waited for: 23 -> 6; matrix products, arithmetic and copies ran while one was open for 3% -> 1% of each run, Pallas kernels for 19% -> 66%
where the time goes in v2:
time: 321 us; the launch traced here: 320 us
  Pallas kernels  236 us (74%)
  starting transfers between devices  32.6 us (10%)
  waiting for transfers between devices  24 us (7%)
  between operations  14.4 us (4%)
  local copies, waits for them, and re-layouts  11.2 us (3%)
    pallas_call x20, Pallas kernels, run(): pl.pallas_call(inner, out_shape=[jax.ShapeDtypeStruct(shape, kind) for sh...  236 us
    ppermute x35, starting transfers between devices, swap(): return lax.ppermute(value, axis, [(i, i ^ mask) for i in range(size)])  30.9 us
    ppermute x35, waiting for transfers between devices, swap(): return lax.ppermute(value, axis, [(i, i ^ mask) for i in range(size)])  11.9 us
    unnamed x68, local copies, waits for them, and re-layouts  8.43 us
    ppermute x2, waiting for transfers between devices, move(): return lax.ppermute(value, ('batch', 'win'), pairs)  6.44 us
  transfers between devices with their start and end apart: 38, of which 6 were waited for; matrix products, arithmetic and copies ran while one was open for 1% of the time, Pallas kernels for 66%

profile of v2, /device:TPU:0, one launch (start us, length us, event | category | flops | bytes accessed | tf_op | source)
XLA Modules:
  0.0 320.2 jit_solution(4518621118765935664)
XLA Ops:
  7.3 0.7 stack.32.refs_0_
  7.9 22.8 %space_forward.2 = (bf16[2,2,2,64,512]{4,3,2,1,0:T(8,128)(2,1)}, bf16[2,2,2,64,512]{4,3,2,1,0:T(8,128)(2,1)}, bf16[2,2,2,64,512]{4,3,2,1,0:T(8,128)(2,1)}, bf16[...) custom-call(s32[5]{0:T(128)} %stack.32.refs_0_, ...), custom_call_target="tpu_custom_call" | custom-call | flops 25769803776 | bytes 92274688 | tf_op jit(solution)/shard_map/space_forward/pallas_call | solution.py:157
  30.7 0.5 collective-permute-start
  31.2 2.6 collective-permute-start.1
  33.9 22.8 %space_forward.3 = (bf16[2,2,2,64,512]{4,3,2,1,0:T(8,128)(2,1)}, bf16[2,2,2,64,512]{4,3,2,1,0:T(8,128)(2,1)}, bf16[2,2,2,64,512]{4,3,2,1,0:T(8,128)(2,1)}, bf16[...) custom-call(s32[5]{0:T(128)} %stack.32.refs_0_, ...), custom_call_target="tpu_custom_call", output_to_operand_aliasing={{4}: (14, {}), {5}: (15, {}), {6}: (16, {}), {7}: (17, {}),... | custom-call | flops 25769803776 | bytes 92274688 | tf_op jit(solution)/shard_map/space_forward/pallas_call | solution.py:157
  56.9 1.9 collective-permute-start.7
  58.8 0.5 iota_select_fusion
  59.3 0.5 copy-done.26
  59.8 0.6 pad.13.refs_2_
  60.4 0.5 iota_select_fusion.2.refs_1_
  60.9 0.8 copy-done.32
  61.7 32.8 %time_block.2 = (bf16[2,2,128,512]{3,2,1,0:T(8,128)(2,1)}, bf16[2,2,128,512]{3,2,1,0:T(8,128)(2,1)}, bf16[2,2,128,512]{3,2,1,0:T(8,128)(2,1)}, bf16[2,2,128,512]...) custom-call(s32[5]{0:T(128)} %stack.32.refs_0_, ...), custom_call_target="tpu_custom_call" | custom-call | flops 51539607552 | bytes 109051904 | tf_op jit(solution)/shard_map/time_block/pallas_call | solution.py:157
  94.6 1.4 collective-permute-start.4
  95.9 0.8 copy-done.31
  96.7 0.5 collective-permute-start.5
  97.2 32.6 %time_block.3 = (bf16[2,2,128,512]{3,2,1,0:T(8,128)(2,1)}, bf16[2,2,128,512]{3,2,1,0:T(8,128)(2,1)}, bf16[2,2,128,512]{3,2,1,0:T(8,128)(2,1)}, bf16[2,2,128,512]...) custom-call(s32[5]{0:T(128)} %stack.32.refs_0_, ...), custom_call_target="tpu_custom_call", output_to_operand_aliasing={{4}: (17, {}), {5}: (18, {})} | custom-call | flops 51539607552 | bytes 109051904 | tf_op jit(solution)/shard_map/time_block/pallas_call | solution.py:157
  129.8 1.0 collective-permute-start.10
  130.8 0.8 collective-permute-start.11
  133.0 24.3 %scattered_tiles.1 = bf16[8,4,6,64,256]{4,3,2,1,0:T(8,128)(2,1)} custom-call(s32[12]{0:T(128)} %constant.73.clone.refs_0_, s32[12]{0:T(128)} %constant.74.clone.refs_1_, bf16[7,2048,512]{2,1,0:T(8,128)(2,1)} %get-tuple-element.129.refs_2_, bf16[9,2048,512]{2,1,0:T(8,128)(2,1)} %get-tuple-element.130.refs_3_, bf16[2,2,2,64,512]{4,3,2,1,0:T(8,128)(2,1)} %copy-done.28, ...), custom_call_target="tpu_custom_call" | custom-call | flops 51539607552 | bytes 201326592 | tf_op jit(solution)/shard_map/scattered_tiles/pallas_call | solution.py:157
  157.4 22.0 %feed_back.1 = (bf16[2,16,64,512]{3,2,1,0:T(8,128)(2,1)}, bf16[5,2048,512]{2,1,0:T(8,128)(2,1)}, f32[2048,512]{1,0:T(8,128)}, f32[10,1,512]{2,1,0:T(1,128)}) custom-call(s32[5]{0:T(128)} %stack.32.refs_0_, f32[1,512]{1,0:T(1,128)} %bitcast.144, bf16[512,2048]{1,0:T(8,128)(2,1)} %refs_2_.1, bf16[2048,512]{1,0:T(8,128)(2,1)} %refs_3_.2, ...), custom_call_target="tpu_custom_call" | custom-call | flops 34359738368 | bytes 142606336 | tf_op jit(solution)/shard_map/feed_back/pallas_call | solution.py:157
  179.4 14.0 %gradient_tiles.4 = (bf16[2,8,64,512]{3,2,1,0:T(8,128)(2,1)}, bf16[2,8,64,512]{3,2,1,0:T(8,128)(2,1)}, bf16[2,8,64,512]{3,2,1,0:T(8,128)(2,1)}) custom-call(s32[1]{0:T(128)} %bitcast.4.refs_0_, s32[6]{0:T(128)} %constant.87.refs_1_, s32[6]{0:T(128)} %pad.13.refs_2_, bf16[7,2048,512]{2,1,0:T(8,128)(2,1)} %get-tuple-element.135.refs_3_, ...), custom_call_target="tpu_custom_call" | custom-call | flops 25769803776 | bytes 100663296 | tf_op jit(solution)/shard_map/gradient_tiles/pallas_call | solution.py:157
  193.9 0.5 iota_select_fusion.3.refs_1_
  194.4 0.5 broadcast.19.refs_1_
  194.9 6.5 %gradient_tiles.5 = bf16[2,8,64,512]{3,2,1,0:T(8,128)(2,1)} custom-call(s32[1]{0:T(128)} %bitcast.4.refs_0_, s32[2]{0:T(128)} %broadcast.19.refs_1_, s32[2]{0:T(128)} %get-tuple-element.258.refs_2_, bf16[7,2048,512]{2,1,0:T(8,128)(2,1)} %get-tuple-element.135.refs_3_, bf16[5,2048,512]{2,1,0:T(8,128)(2,1)} %get-tuple-element.136.refs_4_, ...), custom_call_target="tpu_custom_call" | custom-call | flops 8589934592 | bytes 33554432 | tf_op jit(solution)/shard_map/gradient_tiles/pallas_call | solution.py:157
  201.5 1.0 copy-done
  202.4 4.5 %sum_cores.2 = (bf16[4,256,256]{2,1,0:T(8,128)(2,1)}, bf16[4,256,256]{2,1,0:T(8,128)(2,1)}, bf16[4,256,256]{2,1,0:T(8,128)(2,1)}, bf16[4,256,256]{2,1,0:T(8,128)(2,1)}) custom-call(s32[5]{0:T(128)} %stack.32.refs_0_, bf16[2,4,2,64,512]{4,3,2,1,0:T(8,128)(2,1)} %bitcast.86, bf16[2,4,2,64,512]{4,3,2,1,0:T(8,128)(2,1)} %bitcast.87, ...), custom_call_target="tpu_custom_call" | custom-call | tf_op jit(solution)/shard_map/sum_cores/pallas_call | solution.py:157
  207.0 1.5 collective-permute-start.14
  208.4 0.9 collective-permute-start.15
  209.4 1.1 collective-permute-start.16
  210.5 19.7 %attention_back.1 = (bf16[2,16,64,512]{3,2,1,0:T(8,128)(2,1)}, bf16[4,2048,512]{2,1,0:T(8,128)(2,1)}, f32[10,1,512]{2,1,0:T(1,128)}) custom-call(s32[5]{0:T(128)} %stack.32.refs_0_, bf16[2,16,64,512]{3,2,1,0:T(8,128)(2,1)} %bitcast.107, f32[1,512]{1,0:T(1,128)} %bitcast.147, bf16[512,1536]{1,0:T(8,128)(2,1)} %refs_3_.3, bf16[512,512]{1,0:T(8,128)(2,1)} %refs_4_.1, ...), custom_call_target="tpu_custom_call" | custom-call | flops 17179869184 | bytes 100663296 | tf_op jit(solution)/shard_map/attention_back/pallas_call | solution.py:157
  230.1 6.5 %gradient_tiles.6.refs_5_ = bf16[2,8,64,512]{3,2,1,0:T(8,128)(2,1)} custom-call(s32[1]{0:T(128)} %bitcast.4.refs_0_, s32[2]{0:T(128)} %iota_select_fusion.2.refs_1_, s32[2]{0:T(128)} %copy-done.26, bf16[7,2048,512]{2,1,0:T(8,128)(2,1)} %get-tuple-element.135.refs_3_, bf16[4,2048,512]{2,1,0:T(8,128)(2,1)} %get-tuple-element.142.refs_4_), custom_call_target="tpu_custom_call" | custom-call | flops 8589934592 | bytes 33554432 | tf_op jit(solution)/shard_map/gradient_tiles/pallas_call | solution.py:157
  237.2 0.6 collective-permute-start.18
  237.7 0.7 copy.89
  238.4 6.4 %collective-permute-done.16.refs_4_ = bf16[4,256,256]{2,1,0:T(8,128)(2,1)} collective-permute-done((bf16[4,256,256]{2,1,0:T(8,128)(2,1)}, bf16[4,256,256]{2,1,0:T(8,128)(2,1)}, u32[]{:S(2)}, u32[]{:S(2)}) %collective-permute-start.16) | collective-permute-done | bytes 524320 | tf_op jit(solution)/shard_map/ppermute | solution.py:735
  244.9 3.2 sum_chips.2
  248.0 1.6 collective-permute-start.22
  249.7 6.5 %gradient_tiles.7 = bf16[2,8,64,512]{3,2,1,0:T(8,128)(2,1)} custom-call(s32[1]{0:T(128)} %bitcast.4.refs_0_, s32[2]{0:T(128)} %iota_select_fusion.3.refs_1_, s32[2]{0:T(128)} %get-tuple-element.258.refs_2_, bf16[7,2048,512]{2,1,0:T(8,128)(2,1)} %get-tuple-element.135.refs_3_, bf16[4,2048,512]{2,1,0:T(8,128)(2,1)} %get-tuple-element.142.refs_4_, ...), custom_call_target="tpu_custom_call" | custom-call | flops 8589934592 | bytes 33554432 | tf_op jit(solution)/shard_map/gradient_tiles/pallas_call | solution.py:157
  256.2 0.6 copy-done.9
  257.2 3.5 %sum_cores.3 = (bf16[4,144,256]{2,1,0:T(8,128)(2,1)}, bf16[4,144,256]{2,1,0:T(8,128)(2,1)}, bf16[4,144,256]{2,1,0:T(8,128)(2,1)}, bf16[4,144,256]{2,1,0:T(8,128)(2,1)}) custom-call(s32[5]{0:T(128)} %stack.32.refs_0_, bf16[2,4,2,64,512]{4,3,2,1,0:T(8,128)(2,1)} %bitcast.88, bf16[1,4,2,16,512]{4,3,2,1,0:T(8,128)(2,1)} %bitcast.90, ...), custom_call_target="tpu_custom_call" | custom-call | tf_op jit(solution)/shard_map/sum_cores/pallas_call | solution.py:157
  260.7 1.6 collective-permute-start.19
  262.4 1.3 collective-permute-start.20
  263.7 0.5 collective-permute-start.21
  264.2 2.6 collective-permute-start.23
  266.8 0.5 collective-permute-start.24
  267.4 9.6 %collective-permute-done.23.refs_2_ = bf16[256,256]{1,0:T(8,128)(2,1)S(1)} collective-permute-done((bf16[256,256]{1,0:T(8,128)(2,1)}, bf16[256,256]{1,0:T(8,128)(2,1)S(1)}, u32[]{:S(2)}, u32[]{:S(2)}) %collective-permute-start.23) | collective-permute-done | bytes 131104 | tf_op jit(solution)/shard_map/ppermute | solution.py:723
  277.0 0.6 copy-done.14
  277.7 1.8 sum_last.2.refs_5_.refs_1_
  279.7 1.7 collective-permute-start.30
  281.4 5.6 %reduce-scatter.2.cloned.1.call-done = bf16[1,384,256]{2,1,0:T(8,128)(2,1)} async-done(((bf16[32,384,256]{2,1,0:T(8,128)(2,1)}), bf16[1,384,256]{2,1,0:T(8,128)(2,1)}) %reduce-scatter.2.cloned.1.call-update) | async-done | bytes 196624 | tf_op jit(solution)/shard_map/reduce_scatter | solution.py:920
  287.1 0.7 copy-done.5
  287.8 2.7 sum_chips.3
  290.9 1.4 collective-permute-start.35
  292.4 2.4 collective-permute-start.26
  294.8 0.5 collective-permute-done.25.refs_1_
  295.3 2.2 collective-permute-start.27
  297.5 2.8 unpack.2
  300.4 1.4 collective-permute-done.26.refs_2_
  301.8 0.6 copy-done.17
  302.4 1.7 sum_last.3.refs_5_.refs_1_
  304.1 1.2 collective-permute-start.32
  305.3 0.6 collective-permute-start.33
  306.0 0.6 copy-done.7
  306.7 3.1 spread_units.1
  310.8 2.5 unpack.3
  (121 shorter events, 5.2 us)
Async XLA Ops:
  7.2 279.8 %reduce-scatter.2.cloned.1.call-start = ((), (), s32[]{:S(2)}) async-start(), calls=%async_computation.1 | async-start | bytes 6488064 | tf_op jit(solution)/shard_map/reduce_scatter | solution.py:920
  30.7 30.2 %collective-permute-start = (bf16[2,2,2,64,512]{4,3,2,1,0:T(8,128)(2,1)}, bf16[2,2,2,64,512]{4,3,2,1,0:T(8,128)(2,1)S(1)}, u32[]{:S(2)}, u32[]{:S(2)}) collective-permute-start(bf16[2,2,2,64,512]{4,3,2,1,0:T(8,128)(2,1)} %get-tuple-element.105), channel_id=1, source_target_pairs={{0,1},{1,0},{2,3},{3,2},{4,5},{5,4},{6,7},{7,6},{8,9},{9,8},{10,11... | collective-permute-start | bytes 1572872 | tf_op jit(solution)/shard_map/ppermute | solution.py:723
  31.2 29.7 %collective-permute-start.1 = (bf16[2,2,2,64,512]{4,3,2,1,0:T(8,128)(2,1)}, bf16[2,2,2,64,512]{4,3,2,1,0:T(8,128)(2,1)}, u32[]{:S(2)}, u32[]{:S(2)}) collective-permute-start(bf16[2,2,2,64,512]{4,3,2,1,0:T(8,128)(2,1)} %get-tuple-element.106), channel_id=1, source_target_pairs={{0,2},{1,3},{2,0},{3,1},{4,6},{5,7},{6,4},{7,5},{8,10},{9,11},{10,... | collective-permute-start | bytes 1572872 | tf_op jit(solution)/shard_map/ppermute | solution.py:723
  33.8 27.1 %collective-permute-start.2 = (bf16[2,2,2,64,512]{4,3,2,1,0:T(8,128)(2,1)}, bf16[2,2,2,64,512]{4,3,2,1,0:T(8,128)(2,1)}, u32[]{:S(2)}, u32[]{:S(2)}) collective-permute-start(bf16[2,2,2,64,512]{4,3,2,1,0:T(8,128)(2,1)} %get-tuple-element.107), channel_id=1, source_target_pairs={{0,3},{1,2},{2,1},{3,0},{4,7},{5,6},{6,5},{7,4},{8,11},{9,10},{10,... | collective-permute-start | bytes 1572872 | tf_op jit(solution)/shard_map/ppermute | solution.py:723
  33.9 24.9 %copy-start.27 = (s32[2]{0:T(128)S(1)}, s32[2]{0:T(128)}, u32[]{:S(2)}) copy-start(s32[2]{0:T(128)} %constant.78.clone) | copy-start | bytes 28
  56.6 39.3 %collective-permute-start.6 = (bf16[2,2,2,64,512]{4,3,2,1,0:T(8,128)(2,1)}, bf16[2,2,2,64,512]{4,3,2,1,0:T(8,128)(2,1)S(1)}, u32[]{:S(2)}, u32[]{:S(2)}) collective-permute-start(bf16[2,2,2,64,512]{4,3,2,1,0:T(8,128)(2,1)} %get-tuple-element.118), channel_id=1, source_target_pairs={{0,1},{1,0},{2,3},{3,2},{4,5},{5,4},{6,7},{7,6},{8,9},{9,8},{10,11... | collective-permute-start | bytes 1572872 | tf_op jit(solution)/shard_map/ppermute | solution.py:723
  56.9 40.4 %collective-permute-start.7 = (bf16[2,2,2,64,512]{4,3,2,1,0:T(8,128)(2,1)}, bf16[2,2,2,64,512]{4,3,2,1,0:T(8,128)(2,1)}, u32[]{:S(2)}, u32[]{:S(2)}) collective-permute-start(bf16[2,2,2,64,512]{4,3,2,1,0:T(8,128)(2,1)} %get-tuple-element.119), channel_id=1, source_target_pairs={{0,2},{1,3},{2,0},{3,1},{4,6},{5,7},{6,4},{7,5},{8,10},{9,11},{10,... | collective-permute-start | bytes 1572872 | tf_op jit(solution)/shard_map/ppermute | solution.py:723
  60.9 0.8 copy-start.32
  60.9 36.3 %collective-permute-start.8 = (bf16[2,2,2,64,512]{4,3,2,1,0:T(8,128)(2,1)}, bf16[2,2,2,64,512]{4,3,2,1,0:T(8,128)(2,1)}, u32[]{:S(2)}, u32[]{:S(2)}) collective-permute-start(bf16[2,2,2,64,512]{4,3,2,1,0:T(8,128)(2,1)} %get-tuple-element.120), channel_id=1, source_target_pairs={{0,3},{1,2},{2,1},{3,0},{4,7},{5,6},{6,5},{7,4},{8,11},{9,10},{10,... | collective-permute-start | bytes 1572872 | tf_op jit(solution)/shard_map/ppermute | solution.py:723
  94.5 37.1 %collective-permute-start.3 = (bf16[2,2,2,64,512]{4,3,2,1,0:T(8,128)(2,1)}, bf16[2,2,2,64,512]{4,3,2,1,0:T(8,128)(2,1)S(1)}, u32[]{:S(2)}, u32[]{:S(2)}) collective-permute-start(bf16[2,2,2,64,512]{4,3,2,1,0:T(8,128)(2,1)} %bitcast.114), channel_id=1, source_target_pairs={{0,1},{1,0},{2,3},{3,2},{4,5},{5,4},{6,7},{7,6},{8,9},{9,8},{10,11... | collective-permute-start | bytes 1572872 | tf_op jit(solution)/shard_map/ppermute | solution.py:723
  94.6 37.5 %collective-permute-start.4 = (bf16[2,2,2,64,512]{4,3,2,1,0:T(8,128)(2,1)}, bf16[2,2,2,64,512]{4,3,2,1,0:T(8,128)(2,1)S(1)}, u32[]{:S(2)}, u32[]{:S(2)}) collective-permute-start(bf16[2,2,2,64,512]{4,3,2,1,0:T(8,128)(2,1)} %bitcast.113), channel_id=1, source_target_pairs={{0,2},{1,3},{2,0},{3,1},{4,6},{5,7},{6,4},{7,5},{8,10},{9,11},{10,... | collective-permute-start | bytes 1572872 | tf_op jit(solution)/shard_map/ppermute | solution.py:723
  95.9 0.8 copy-start.31
  96.7 35.3 %collective-permute-start.5 = (bf16[2,2,2,64,512]{4,3,2,1,0:T(8,128)(2,1)}, bf16[2,2,2,64,512]{4,3,2,1,0:T(8,128)(2,1)S(1)}, u32[]{:S(2)}, u32[]{:S(2)}) collective-permute-start(bf16[2,2,2,64,512]{4,3,2,1,0:T(8,128)(2,1)} %bitcast.112), channel_id=1, source_target_pairs={{0,3},{1,2},{2,1},{3,0},{4,7},{5,6},{6,5},{7,4},{8,11},{9,10},{10,... | collective-permute-start | bytes 1572872 | tf_op jit(solution)/shard_map/ppermute | solution.py:723
  129.8 27.5 %collective-permute-start.10 = (bf16[2,2,2,64,512]{4,3,2,1,0:T(8,128)(2,1)}, bf16[2,2,2,64,512]{4,3,2,1,0:T(8,128)(2,1)}, u32[]{:S(2)}, u32[]{:S(2)}) collective-permute-start(bf16[2,2,2,64,512]{4,3,2,1,0:T(8,128)(2,1)} %bitcast.117), channel_id=1, source_target_pairs={{0,2},{1,3},{2,0},{3,1},{4,6},{5,7},{6,4},{7,5},{8,10},{9,11},{10,... | collective-permute-start | bytes 1572872 | tf_op jit(solution)/shard_map/ppermute | solution.py:723
  130.8 26.5 %collective-permute-start.11 = (bf16[2,2,2,64,512]{4,3,2,1,0:T(8,128)(2,1)}, bf16[2,2,2,64,512]{4,3,2,1,0:T(8,128)(2,1)}, u32[]{:S(2)}, u32[]{:S(2)}) collective-permute-start(bf16[2,2,2,64,512]{4,3,2,1,0:T(8,128)(2,1)} %bitcast.116), channel_id=1, source_target_pairs={{0,3},{1,2},{2,1},{3,0},{4,7},{5,6},{6,5},{7,4},{8,11},{9,10},{10,... | collective-permute-start | bytes 1572872 | tf_op jit(solution)/shard_map/ppermute | solution.py:723
  131.6 0.8 copy-start.28
  131.6 25.8 %collective-permute-start.9 = (bf16[2,2,2,64,512]{4,3,2,1,0:T(8,128)(2,1)}, bf16[2,2,2,64,512]{4,3,2,1,0:T(8,128)(2,1)}, u32[]{:S(2)}, u32[]{:S(2)}) collective-permute-start(bf16[2,2,2,64,512]{4,3,2,1,0:T(8,128)(2,1)} %bitcast.115), channel_id=1, source_target_pairs={{0,1},{1,0},{2,3},{3,2},{4,5},{5,4},{6,7},{7,6},{8,9},{9,8},{10,11... | collective-permute-start | bytes 1572872 | tf_op jit(solution)/shard_map/ppermute | solution.py:723
  132.0 0.8 copy-start.29
  132.1 1.0 copy-start.30
  179.4 15.0 %copy-start.22 = (f32[10,1,512]{2,1,0:T(1,128)S(1)}, f32[10,1,512]{2,1,0:T(1,128)}, u32[]{:S(2)}) copy-start(f32[10,1,512]{2,1,0:T(1,128)} %get-tuple-element.149) | copy-start | bytes 61444
  179.4 15.0 %copy-start.23 = (f32[10,1,512]{2,1,0:T(1,128)S(1)}, f32[10,1,512]{2,1,0:T(1,128)}, u32[]{:S(2)}) copy-start(f32[10,1,512]{2,1,0:T(1,128)} %get-tuple-element.150) | copy-start | bytes 61444
  193.4 8.1 %collective-permute-start.12 = (bf16[2,4,2,64,512]{4,3,2,1,0:T(8,128)(2,1)}, bf16[2,4,2,64,512]{4,3,2,1,0:T(8,128)(2,1)S(1)}, u32[]{:S(2)}, u32[]{:S(2)}) collective-permute-start(bf16[2,4,2,64,512]{4,3,2,1,0:T(8,128)(2,1)} %bitcast.109), channel_id=1, source_target_pairs={{0,1},{1,0},{2,3},{3,2},{4,5},{5,4},{6,7},{7,6},{8,9},{9,8},{10,11... | collective-permute-start | bytes 3145736 | tf_op jit(solution)/shard_map/ppermute | solution.py:723
  193.5 7.9 %collective-permute-start.13 = (bf16[2,4,2,64,512]{4,3,2,1,0:T(8,128)(2,1)}, bf16[2,4,2,64,512]{4,3,2,1,0:T(8,128)(2,1)}, u32[]{:S(2)}, u32[]{:S(2)}) collective-permute-start(bf16[2,4,2,64,512]{4,3,2,1,0:T(8,128)(2,1)} %bitcast.108), channel_id=1, source_target_pairs={{0,1},{1,0},{2,3},{3,2},{4,5},{5,4},{6,7},{7,6},{8,9},{9,8},{10,11... | collective-permute-start | bytes 3145736 | tf_op jit(solution)/shard_map/ppermute | solution.py:723
  201.4 1.0 copy-start
  207.0 31.5 %collective-permute-start.14 = (bf16[4,256,256]{2,1,0:T(8,128)(2,1)}, bf16[4,256,256]{2,1,0:T(8,128)(2,1)S(1)}, u32[]{:S(2)}, u32[]{:S(2)}) collective-permute-start(bf16[4,256,256]{2,1,0:T(8,128)(2,1)} %get-tuple-element.143), channel_id=1, source_target_pairs={{0,4},{4,0},{8,12},{12,8},{16,20},{20,16},{24,28},{28,24},{1,5},{5... | collective-permute-start | bytes 1572872 | tf_op jit(solution)/shard_map/ppermute | solution.py:723
  208.4 30.0 %collective-permute-start.15 = (bf16[4,256,256]{2,1,0:T(8,128)(2,1)}, bf16[4,256,256]{2,1,0:T(8,128)(2,1)}, u32[]{:S(2)}, u32[]{:S(2)}) collective-permute-start(bf16[4,256,256]{2,1,0:T(8,128)(2,1)} %get-tuple-element.144), channel_id=1, source_target_pairs={{0,2},{1,3},{2,0},{3,1},{4,6},{5,7},{6,4},{7,5},{8,10},{9,11},{10,... | collective-permute-start | bytes 1572872 | tf_op jit(solution)/shard_map/ppermute | solution.py:723
  209.4 35.5 %collective-permute-start.16 = (bf16[4,256,256]{2,1,0:T(8,128)(2,1)}, bf16[4,256,256]{2,1,0:T(8,128)(2,1)}, u32[]{:S(2)}, u32[]{:S(2)}) collective-permute-start(bf16[4,256,256]{2,1,0:T(8,128)(2,1)} %get-tuple-element.145), channel_id=1, source_target_pairs={{0,6},{1,7},{2,4},{3,5},{4,2},{5,3},{6,0},{7,1},{8,14},{9,15},{10,... | collective-permute-start | bytes 1572872 | tf_op jit(solution)/shard_map/ppermute | solution.py:735
  230.1 6.6 %copy-start.24 = (f32[10,1,512]{2,1,0:T(1,128)S(1)}, f32[10,1,512]{2,1,0:T(1,128)}, u32[]{:S(2)}) copy-start(f32[10,1,512]{2,1,0:T(1,128)} %get-tuple-element.147) | copy-start | bytes 61444
  230.1 6.6 %copy-start.25 = (f32[10,1,512]{2,1,0:T(1,128)S(1)}, f32[10,1,512]{2,1,0:T(1,128)}, u32[]{:S(2)}) copy-start(f32[10,1,512]{2,1,0:T(1,128)} %get-tuple-element.148) | copy-start | bytes 61444
  236.7 19.5 %collective-permute-start.17 = (bf16[2,4,2,64,512]{4,3,2,1,0:T(8,128)(2,1)}, bf16[2,4,2,64,512]{4,3,2,1,0:T(8,128)(2,1)S(1)}, u32[]{:S(2)}, u32[]{:S(2)}) collective-permute-start(bf16[2,4,2,64,512]{4,3,2,1,0:T(8,128)(2,1)} %bitcast.89), channel_id=1, source_target_pairs={{0,1},{1,0},{2,3},{3,2},{4,5},{5,4},{6,7},{7,6},{8,9},{9,8},{10,11... | collective-permute-start | bytes 3145736 | tf_op jit(solution)/shard_map/ppermute | solution.py:723
  237.2 19.0 %collective-permute-start.18 = (bf16[1,4,2,16,512]{4,3,2,1,0:T(8,128)(2,1)S(1)}, bf16[1,4,2,16,512]{4,3,2,1,0:T(8,128)(2,1)S(1)}, u32[]{:S(2)}, u32[]{:S(2)}) collective-permute-start(bf16[1,4,2,16,512]{4,3,2,1,0:T(8,128)(2,1)S(1)} %bitcast.98), channel_id=1, source_target_pairs={{0,1},{1,0},{2,3},{3,2},{4,5},{5,4},{6,7},{7,6},{8,9},{9,8},{10,11... | collective-permute-start | bytes 393224 | tf_op jit(solution)/shard_map/ppermute | solution.py:723
  238.4 6.4 %copy-start.2 = (bf16[4,256,256]{2,1,0:T(8,128)(2,1)}, bf16[4,256,256]{2,1,0:T(8,128)(2,1)S(1)}, u32[]{:S(2)}) copy-start(bf16[4,256,256]{2,1,0:T(8,128)(2,1)S(1)} %collective-permute-done.14.refs_2_) | copy-start | bytes 1572868
  248.0 18.8 %collective-permute-start.22 = (bf16[256,256]{1,0:T(8,128)(2,1)}, bf16[256,256]{1,0:T(8,128)(2,1)S(1)}, u32[]{:S(2)}, u32[]{:S(2)}) collective-permute-start(bf16[256,256]{1,0:T(8,128)(2,1)} %get-tuple-element.155), channel_id=1, source_target_pairs={{0,8},{4,12},{8,0},{12,4},{16,24},{20,28},{24,16},{28,20},{1,9},{5... | collective-permute-start | bytes 393224 | tf_op jit(solution)/shard_map/ppermute | solution.py:723
  249.7 17.2 %copy-start.33 = (bf16[256,256]{1,0:T(8,128)(2,1)S(1)}, bf16[256,256]{1,0:T(8,128)(2,1)}, u32[]{:S(2)}) copy-start(bf16[256,256]{1,0:T(8,128)(2,1)} %get-tuple-element.157) | copy-start | bytes 393220
  256.2 1.0 copy-start.1
  260.7 19.0 %collective-permute-start.19 = (bf16[4,144,256]{2,1,0:T(8,128)(2,1)}, bf16[4,144,256]{2,1,0:T(8,128)(2,1)S(1)}, u32[]{:S(2)}, u32[]{:S(2)}) collective-permute-start(bf16[4,144,256]{2,1,0:T(8,128)(2,1)} %get-tuple-element.152), channel_id=1, source_target_pairs={{0,4},{4,0},{8,12},{12,8},{16,20},{20,16},{24,28},{28,24},{1,5},{5... | collective-permute-start | bytes 884744 | tf_op jit(solution)/shard_map/ppermute | solution.py:723
  262.4 19.0 %collective-permute-start.20 = (bf16[4,144,256]{2,1,0:T(8,128)(2,1)}, bf16[4,144,256]{2,1,0:T(8,128)(2,1)S(1)}, u32[]{:S(2)}, u32[]{:S(2)}) collective-permute-start(bf16[4,144,256]{2,1,0:T(8,128)(2,1)} %get-tuple-element.153), channel_id=1, source_target_pairs={{0,2},{1,3},{2,0},{3,1},{4,6},{5,7},{6,4},{7,5},{8,10},{9,11},{10,... | collective-permute-start | bytes 884744 | tf_op jit(solution)/shard_map/ppermute | solution.py:723
  263.7 23.3 %collective-permute-start.21 = (bf16[4,144,256]{2,1,0:T(8,128)(2,1)}, bf16[4,144,256]{2,1,0:T(8,128)(2,1)S(1)}, u32[]{:S(2)}, u32[]{:S(2)}) collective-permute-start(bf16[4,144,256]{2,1,0:T(8,128)(2,1)} %get-tuple-element.154), channel_id=1, source_target_pairs={{0,6},{1,7},{2,4},{3,5},{4,2},{5,3},{6,0},{7,1},{8,14},{9,15},{10,... | collective-permute-start | bytes 884744 | tf_op jit(solution)/shard_map/ppermute | solution.py:735
  264.2 12.8 %collective-permute-start.23 = (bf16[256,256]{1,0:T(8,128)(2,1)}, bf16[256,256]{1,0:T(8,128)(2,1)S(1)}, u32[]{:S(2)}, u32[]{:S(2)}) collective-permute-start(bf16[256,256]{1,0:T(8,128)(2,1)} %get-tuple-element.156), channel_id=1, source_target_pairs={{0,16},{4,20},{8,24},{12,28},{16,0},{20,4},{24,8},{28,12},{1,17},{... | collective-permute-start | bytes 393224 | tf_op jit(solution)/shard_map/ppermute | solution.py:723
  266.8 10.2 %copy-start.13 = (bf16[256,256]{1,0:T(8,128)(2,1)}, bf16[256,256]{1,0:T(8,128)(2,1)S(1)}, u32[]{:S(2)}) copy-start(bf16[256,256]{1,0:T(8,128)(2,1)S(1)} %collective-permute-done.22.refs_1_) | copy-start | bytes 393220
  266.8 10.2 %collective-permute-start.24 = (bf16[256,256]{1,0:T(8,128)(2,1)S(1)}, bf16[256,256]{1,0:T(8,128)(2,1)S(1)}, u32[]{:S(2)}, u32[]{:S(2)}) collective-permute-start(bf16[256,256]{1,0:T(8,128)(2,1)S(1)} %copy-done.33), channel_id=1, source_target_pairs={{0,24},{4,28},{8,16},{12,20},{16,8},{20,12},{24,0},{28,4},{1,25},{... | collective-permute-start | bytes 393224 | tf_op jit(solution)/shard_map/ppermute | solution.py:723
  277.0 0.7 copy-start.15
  279.5 11.3 %collective-permute-start.28 = (bf16[256,256]{1,0:T(8,128)(2,1)}, bf16[256,256]{1,0:T(8,128)(2,1)S(1)}, u32[]{:S(2)}, u32[]{:S(2)}) collective-permute-start(bf16[256,256]{1,0:T(8,128)(2,1)} %sum_last.2.refs_5_.refs_1_), channel_id=1, source_target_pairs={{0,1},{1,0},{2,3},{3,2},{4,5},{5,4},{6,7},{7,6},{8,9},{9,8},{10,11... | collective-permute-start | bytes 393224 | tf_op jit(solution)/shard_map/ppermute | solution.py:723
  279.5 12.7 %collective-permute-start.29 = (bf16[256,256]{1,0:T(8,128)(2,1)}, bf16[256,256]{1,0:T(8,128)(2,1)S(1)}, u32[]{:S(2)}, u32[]{:S(2)}) collective-permute-start(bf16[256,256]{1,0:T(8,128)(2,1)} %sum_last.2.refs_5_.refs_1_), channel_id=1, source_target_pairs={{0,2},{1,3},{2,0},{3,1},{4,6},{5,7},{6,4},{7,5},{8,10},{9,11},{10,... | collective-permute-start | bytes 393224 | tf_op jit(solution)/shard_map/ppermute | solution.py:723
  279.7 7.3 %copy-start.3 = (bf16[4,144,256]{2,1,0:T(8,128)(2,1)}, bf16[4,144,256]{2,1,0:T(8,128)(2,1)S(1)}, u32[]{:S(2)}) copy-start(bf16[4,144,256]{2,1,0:T(8,128)(2,1)S(1)} %collective-permute-done.19.refs_2_) | copy-start | bytes 884740
  279.7 12.7 %collective-permute-start.30 = (bf16[256,256]{1,0:T(8,128)(2,1)}, bf16[256,256]{1,0:T(8,128)(2,1)S(1)}, u32[]{:S(2)}, u32[]{:S(2)}) collective-permute-start(bf16[256,256]{1,0:T(8,128)(2,1)} %sum_last.2.refs_5_.refs_1_), channel_id=1, source_target_pairs={{0,3},{1,2},{2,1},{3,0},{4,7},{5,6},{6,5},{7,4},{8,11},{9,10},{10,... | collective-permute-start | bytes 393224 | tf_op jit(solution)/shard_map/ppermute | solution.py:723
  281.4 5.7 %copy-start.4 = (bf16[4,144,256]{2,1,0:T(8,128)(2,1)}, bf16[4,144,256]{2,1,0:T(8,128)(2,1)S(1)}, u32[]{:S(2)}) copy-start(bf16[4,144,256]{2,1,0:T(8,128)(2,1)S(1)} %collective-permute-done.20.refs_3_) | copy-start | bytes 884740
  287.0 18.3 %collective-permute-start.34 = (bf16[384,256]{1,0:T(8,128)(2,1)}, bf16[384,256]{1,0:T(8,128)(2,1)S(1)}, u32[]{:S(2)}, u32[]{:S(2)}) collective-permute-start(bf16[384,256]{1,0:T(8,128)(2,1)} %bitcast.91), channel_id=1, source_target_pairs={{0,1},{1,0},{2,3},{3,2},{4,5},{5,4},{6,7},{7,6},{8,9},{9,8},{10,11... | collective-permute-start | bytes 589832 | tf_op jit(solution)/shard_map/ppermute | solution.py:723
  287.0 0.7 copy-start.5
  290.4 4.9 %collective-permute-start.25 = (bf16[144,256]{1,0:T(8,128)(2,1)}, bf16[144,256]{1,0:T(8,128)(2,1)S(1)}, u32[]{:S(2)}, u32[]{:S(2)}) collective-permute-start(bf16[144,256]{1,0:T(8,128)(2,1)} %get-tuple-element.159), channel_id=1, source_target_pairs={{0,8},{4,12},{8,0},{12,4},{16,24},{20,28},{24,16},{28,20},{1,9},{5... | collective-permute-start | bytes 221192 | tf_op jit(solution)/shard_map/ppermute | solution.py:723
  290.9 6.7 %copy-start.10 = (bf16[256,256]{1,0:T(8,128)(2,1)}, bf16[256,256]{1,0:T(8,128)(2,1)S(1)}, u32[]{:S(2)}) copy-start(bf16[256,256]{1,0:T(8,128)(2,1)S(1)} %collective-permute-done.28.refs_2_) | copy-start | bytes 393220
  290.9 15.1 %collective-permute-start.35 = (bf16[384,256]{1,0:T(8,128)(2,1)}, bf16[384,256]{1,0:T(8,128)(2,1)S(1)}, u32[]{:S(2)}, u32[]{:S(2)}) collective-permute-start(bf16[384,256]{1,0:T(8,128)(2,1)} %bitcast.92), channel_id=1, source_target_pairs={{0,2},{1,3},{2,0},{3,1},{4,6},{5,7},{6,4},{7,5},{8,10},{9,11},{10,... | collective-permute-start | bytes 589832 | tf_op jit(solution)/shard_map/ppermute | solution.py:723
  292.2 5.3 %copy-start.11 = (bf16[256,256]{1,0:T(8,128)(2,1)}, bf16[256,256]{1,0:T(8,128)(2,1)S(1)}, u32[]{:S(2)}) copy-start(bf16[256,256]{1,0:T(8,128)(2,1)S(1)} %collective-permute-done.29.refs_3_) | copy-start | bytes 393220
  292.2 13.7 %collective-permute-start.36 = (bf16[384,256]{1,0:T(8,128)(2,1)}, bf16[384,256]{1,0:T(8,128)(2,1)S(1)}, u32[]{:S(2)}, u32[]{:S(2)}) collective-permute-start(bf16[384,256]{1,0:T(8,128)(2,1)} %bitcast.93), channel_id=1, source_target_pairs={{0,3},{1,2},{2,1},{3,0},{4,7},{5,6},{6,5},{7,4},{8,11},{9,10},{10,... | collective-permute-start | bytes 589832 | tf_op jit(solution)/shard_map/ppermute | solution.py:723
  292.4 5.1 %copy-start.12 = (bf16[256,256]{1,0:T(8,128)(2,1)}, bf16[256,256]{1,0:T(8,128)(2,1)S(1)}, u32[]{:S(2)}) copy-start(bf16[256,256]{1,0:T(8,128)(2,1)S(1)} %collective-permute-done.30.refs_4_) | copy-start | bytes 393220
  292.4 9.3 %collective-permute-start.26 = (bf16[144,256]{1,0:T(8,128)(2,1)}, bf16[144,256]{1,0:T(8,128)(2,1)S(1)}, u32[]{:S(2)}, u32[]{:S(2)}) collective-permute-start(bf16[144,256]{1,0:T(8,128)(2,1)} %get-tuple-element.160), channel_id=1, source_target_pairs={{0,16},{4,20},{8,24},{12,28},{16,0},{20,4},{24,8},{28,12},{1,17},{... | collective-permute-start | bytes 221192 | tf_op jit(solution)/shard_map/ppermute | solution.py:723
  295.3 6.5 %copy-start.16 = (bf16[144,256]{1,0:T(8,128)(2,1)}, bf16[144,256]{1,0:T(8,128)(2,1)S(1)}, u32[]{:S(2)}) copy-start(bf16[144,256]{1,0:T(8,128)(2,1)S(1)} %collective-permute-done.25.refs_1_) | copy-start | bytes 221188
  295.3 6.4 %collective-permute-start.27 = (bf16[144,256]{1,0:T(8,128)(2,1)}, bf16[144,256]{1,0:T(8,128)(2,1)S(1)}, u32[]{:S(2)}, u32[]{:S(2)}) collective-permute-start(bf16[144,256]{1,0:T(8,128)(2,1)} %get-tuple-element.161), channel_id=1, source_target_pairs={{0,24},{4,28},{8,16},{12,20},{16,8},{20,12},{24,0},{28,4},{1,25},{... | collective-permute-start | bytes 221192 | tf_op jit(solution)/shard_map/ppermute | solution.py:723
  304.1 5.8 %collective-permute-start.31 = (bf16[144,256]{1,0:T(8,128)(2,1)}, bf16[144,256]{1,0:T(8,128)(2,1)S(1)}, u32[]{:S(2)}, u32[]{:S(2)}) collective-permute-start(bf16[144,256]{1,0:T(8,128)(2,1)} %sum_last.3.refs_5_.refs_1_), channel_id=1, source_target_pairs={{0,1},{1,0},{2,3},{3,2},{4,5},{5,4},{6,7},{7,6},{8,9},{9,8},{10,11... | collective-permute-start | bytes 221192 | tf_op jit(solution)/shard_map/ppermute | solution.py:723
  304.1 5.8 %collective-permute-start.32 = (bf16[144,256]{1,0:T(8,128)(2,1)}, bf16[144,256]{1,0:T(8,128)(2,1)S(1)}, u32[]{:S(2)}, u32[]{:S(2)}) collective-permute-start(bf16[144,256]{1,0:T(8,128)(2,1)} %sum_last.3.refs_5_.refs_1_), channel_id=1, source_target_pairs={{0,2},{1,3},{2,0},{3,1},{4,6},{5,7},{6,4},{7,5},{8,10},{9,11},{10,... | collective-permute-start | bytes 221192 | tf_op jit(solution)/shard_map/ppermute | solution.py:723
  305.3 0.7 copy-start.6
  305.3 4.8 %collective-permute-start.33 = (bf16[144,256]{1,0:T(8,128)(2,1)}, bf16[144,256]{1,0:T(8,128)(2,1)S(1)}, u32[]{:S(2)}, u32[]{:S(2)}) collective-permute-start(bf16[144,256]{1,0:T(8,128)(2,1)} %sum_last.3.refs_5_.refs_1_), channel_id=1, source_target_pairs={{0,3},{1,2},{2,1},{3,0},{4,7},{5,6},{6,5},{7,4},{8,11},{9,10},{10,... | collective-permute-start | bytes 221192 | tf_op jit(solution)/shard_map/ppermute | solution.py:723
  305.9 0.7 copy-start.7
  305.9 0.7 copy-start.8
  (8 other events, 5.0 us)
Sparse Core Ops, SparseCore 0:
  157.5 129.5 reduce-scatter.1

commit v3 on v2

v3 whole, which is shorter than its diff:
```python
import functools

import jax
import jax.numpy as jnp
from jax import lax
from jax.experimental import pallas as pl
from jax.experimental.pallas import tpu as pltpu
from jax.sharding import PartitionSpec as P

D = 512
HEADS = 8
HDIM = 64
FF = 2048
PAIR = 2 * HDIM
PAIRS = HEADS // 2
CHUNK = 512
CHUNKS = FF // CHUNK
EPS = 1e-05
NEGATIVE = -1e30
FLOAT = jnp.float32
HALF = jnp.bfloat16
HALVES = 2
UNITS = 16
VMEM = 62 << 20
SMALL_VMEM = 24 << 20
ARRIVED_FLOPS = 6 * 10**9
FIRST_FEED = 2
SMALL_FLOPS = 2 * 10**8
SLOWER = 4

NARROW, WIDEN, ENTRY, EXIT = 0, CHUNKS, 2 * CHUNKS, 2 * CHUNKS + 3
TILES = 2 * CHUNKS + 4
INNER, COTANGENT = 0, 1
BACK, RESULT = 0, 1
GAIN, OFFSET, BIAS, WEIGH, SHIFT, NUDGE, LIFT = 0, 1, 2, 3, 4, 5, 6
SUMS = 6 + CHUNKS


def dot(left, right):
    return lax.dot_general(left, right, (((1,), (0,)), ((), ())), preferred_element_type=FLOAT)


def dot_right(left, right):
    return lax.dot_general(left, right, (((1,), (1,)), ((), ())), preferred_element_type=FLOAT)


def dot_left(left, right):
    return lax.dot_general(left, right, (((0,), (0,)), ((), ())), preferred_element_type=FLOAT)


def unit_of(rows):
    centre = rows - jnp.mean(rows, axis=-1, keepdims=True)
    inverse = lax.rsqrt(jnp.mean(centre * centre, axis=-1, keepdims=True) + EPS)
    return centre * inverse, inverse


def norm_back(scaled, unit, inverse):
    return inverse * (
        scaled
        - jnp.mean(scaled, axis=-1, keepdims=True)
        - unit * jnp.mean(scaled * unit, axis=-1, keepdims=True)
    )


def gelu_pair(hidden):
    half = 0.5 * lax.erf(hidden * 0.7071067811865476) + 0.5
    bell = jnp.exp(hidden * hidden * -0.5) * 0.3989422804014327
    return hidden * half, half + hidden * bell


def gelu_of(hidden):
    return hidden * (0.5 * lax.erf(hidden * 0.7071067811865476) + 0.5)


def column_sum(values):
    return jnp.sum(values, axis=0, keepdims=True)


def first_head(rows):
    return lax.broadcasted_iota(jnp.int32, (rows, PAIR), 1) < HDIM


def spread(pair, first):
    zero = jnp.zeros_like(pair)
    return jnp.concatenate([jnp.where(first, pair, zero), jnp.where(first, zero, pair)], axis=0)


def gathered(both, first, rows):
    return jnp.where(first, both[:rows], both[rows:])


def attend_units(blocks):
    units = [(block, pair) for block in range(blocks) for pair in range(PAIRS)]
    return [units[start : start + UNITS] for start in range(0, len(units), UNITS)]


def columns(pair, part=0):
    start = part * D + pair * PAIR
    return slice(start, start + PAIR)


def attend_forward(triple, mixed, weights, blocks, rows, mask):
    first = first_head(rows)
    for units in attend_units(blocks):
        spans = [slice(block * rows, block * rows + rows) for block, _ in units]
        queries = [spread(triple[s, columns(p)], first) for s, (_, p) in zip(spans, units)]
        scores = [dot_right(triple[s, columns(p, 1)], q) for q, s, (_, p) in zip(queries, spans, units)]
        if mask is not None:
            scores = [score + mask for score in scores]
        powers = [
            jnp.exp((score - jnp.max(score, axis=0, keepdims=True)) * HDIM ** (-0.5)) for score in scores
        ]
        probs = [
            (power * (1.0 / jnp.sum(power, axis=0, keepdims=True))).astype(HALF) for power in powers
        ]
        both = [dot_left(prob, triple[s, columns(p, 2)]) for prob, s, (_, p) in zip(probs, spans, units)]
        for value, prob, s, (block, p) in zip(both, probs, spans, units):
            weights[block, p] = prob
            mixed[s, columns(p)] = gathered(value, first, rows).astype(HALF)


def attend_backward(triple, weights, mixed_back, put, blocks, rows):
    first = first_head(rows)
    scale = HDIM ** (-0.5)
    for units in attend_units(blocks):
        spans = [slice(block * rows, block * rows + rows) for block, _ in units]
        mixes = [spread(mixed_back[s, columns(p)], first) for s, (_, p) in zip(spans, units)]
        probs = [weights[block, p] for block, p in units]
        values_back = [dot(prob, mix) for prob, mix in zip(probs, mixes)]
        weights_back = [
            dot_right(triple[s, columns(p, 2)], mix) for mix, s, (_, p) in zip(mixes, spans, units)
        ]
        scores_back = []
        for prob, back in zip(probs, weights_back):
            wide = prob.astype(FLOAT)
            inside = back - jnp.sum(back * wide, axis=0, keepdims=True)
            scores_back.append((wide * inside * scale).astype(HALF))
        queries = [spread(triple[s, columns(p)], first) for s, (_, p) in zip(spans, units)]
        keys_back = [dot(score, query) for score, query in zip(scores_back, queries)]
        both = [
            dot_left(score, triple[s, columns(p, 1)])
            for score, s, (_, p) in zip(scores_back, spans, units)
        ]
        for key, value, pair, s, (_, p) in zip(keys_back, values_back, both, spans, units):
            put(s, p, 0, gathered(pair, first, rows).astype(HALF))
            put(s, p, 1, key.astype(HALF))
            put(s, p, 2, value.astype(HALF))


def whole(shape):
    return pl.BlockSpec(shape, lambda *_: (0,) * len(shape), pipeline_mode=pl.Buffered(1))


def run(body, name, grid, scalars, ins, outs, scratch=(), aliases=None, after=(), flops=0, moved=0, vmem=VMEM):
    aliases = aliases or {}
    anywhere = pl.BlockSpec(memory_space=pl.ANY)
    first = len(scalars) + len(ins)
    extra = [*aliases.values(), *after]

    def inner(*refs):
        body(*refs[:first], *refs[first + len(extra) :])

    return pl.pallas_call(
        inner,
        out_shape=[jax.ShapeDtypeStruct(shape, kind) for shape, kind, _ in outs],
        grid_spec=pltpu.PrefetchScalarGridSpec(
            num_scalar_prefetch=len(scalars),
            grid=grid,
            in_specs=[spec for _, spec in ins] + [anywhere] * len(extra),
            out_specs=[spec for _, _, spec in outs],
            scratch_shapes=list(scratch),
        ),
        input_output_aliases={first + at: out for at, out in enumerate(aliases)},
        compiler_params=pltpu.CompilerParams(vmem_limit_bytes=vmem),
        cost_estimate=pl.CostEstimate(flops=flops * SLOWER, bytes_accessed=moved * SLOWER, transcendentals=0),
        name=name,
    )(*scalars, *[array for array, _ in ins], *extra)


def plain(arrays):
    return [(array, whole(array.shape)) for array in arrays]


def slab_spec(slabs, rows, at):
    return pl.BlockSpec((slabs, rows, D), lambda *i: (0, at(*i), 0))


def row_spec(rows, width, at):
    return pl.BlockSpec((rows, width), lambda *i: (at(*i), 0))


def space_forward_body(place, rows_in, cotangent, *refs, window, pieces):
    gain, offset, entry, leave, bias, weigh, shift, widen, lift, narrow, nudge = refs[:11]
    sent = refs[11 : 11 + pieces]
    triple, weights, mixed, middles, hiddens = refs[11 + pieces :]
    step = pl.program_id(0)
    shape = rows_in.shape
    rows = rows_in[...].reshape(-1, D).astype(FLOAT)
    count = rows.shape[0]
    unit, _ = unit_of(rows)
    normed = (unit * gain[...] + offset[...]).astype(HALF)
    triple[...] = dot(normed, entry[...]).astype(HALF)
    attend_forward(triple, mixed, weights, count // window, window, None)
    middle = rows + dot(mixed[...], leave[...]) + bias[...]
    middles[...] = middle
    unit_two, _ = unit_of(middle)
    second = (unit_two * weigh[...] + shift[...]).astype(HALF)
    total = middle + nudge[...]
    for chunk in range(CHUNKS):
        at = slice(chunk * CHUNK, (chunk + 1) * CHUNK)
        hidden = dot(second, widen[:, at]) + lift[:, at]
        hiddens[:, at] = hidden.astype(HALF)
        total = total + dot(gelu_of(hidden).astype(HALF), narrow[at, :])
    inner = total.astype(HALF).reshape(shape)
    for piece in range(pieces):

        @pl.when(step == piece)
        def _(piece=piece):
            sent[piece][INNER] = inner
            sent[piece][COTANGENT] = cotangent[...]


def space_forward(place, frames, cotangent, params, half, pieces, before):
    per_group, windows, window, _ = frames.shape
    each = windows // pieces // HALVES
    block = (per_group, each, window, D)
    rows = per_group * each * window
    count = rows * pieces * HALVES
    cut = pl.BlockSpec(block, lambda i, place: (0, (place[0] ^ i) * HALVES + half, 0, 0))
    at = lambda i, place: half * pieces + i
    attended = (rows // window, PAIRS, window, 2 * window)
    both = (2, *block)
    outs = [(both, HALF, pl.BlockSpec(both, lambda i, place: (0,) * 5))] * pieces
    outs += [
        ((count, 3 * D), HALF, row_spec(rows, 3 * D, at)),
        (
            (count // window, *attended[1:]),
            HALF,
            pl.BlockSpec(attended, lambda i, place: (at(i, place), 0, 0, 0)),
        ),
        ((count, D), HALF, row_spec(rows, D, at)),
        ((count, D), FLOAT, row_spec(rows, D, at)),
        ((count, FF), HALF, row_spec(rows, FF, at)),
    ]
    made = run(
        functools.partial(space_forward_body, window=window, pieces=pieces),
        "space_forward",
        (pieces,),
        [place],
        [(frames, cut), (cotangent, cut)] + plain(params),
        outs,
        aliases={pieces + number: array for number, array in enumerate(before)},
        flops=2 * rows * pieces * D * (4 * D + 2 * FF),
        moved=rows * pieces * (8 * D + 12 * D + 2 * FF),
    )
    return made[:pieces], made[pieces:]


def by_position(refs, which, frames_of, positions):
    parts = [ref[which, frame].astype(FLOAT) for ref in refs for frame in range(frames_of)]
    return jnp.concatenate(
        [part[start : start + 8] for start in range(0, positions, 8) for part in parts], axis=0
    )


def by_frame(values, refs, which, frames_of, positions):
    total = len(refs) * frames_of
    for at, ref in enumerate(refs):
        for frame in range(frames_of):
            number = at * frames_of + frame
            ref[which, frame] = jnp.concatenate(
                [
                    values[(group * total + number) * 8 : (group * total + number) * 8 + 8]
                    for group in range(positions // 8)
                ],
                axis=0,
            ).astype(HALF)


def fill_mask(mask, place, lengths, per_group, pieces):
    window = mask.shape[0]
    key = lax.broadcasted_iota(jnp.int32, mask.shape, 0)
    query = lax.broadcasted_iota(jnp.int32, mask.shape, 1) % window
    frames = []
    for row in (query, key):
        number = row // 8
        frames.append((number % per_group) * pieces + ((number // per_group) ^ place[0]))
    videos = [jnp.zeros_like(frame) for frame in frames]
    entries = lengths.shape[1]
    end = 0
    for entry in range(entries):
        end = end + lengths[0, entry]
        videos = [v + (f >= end).astype(jnp.int32) for v, f in zip(videos, frames)]
    videos = [jnp.where(f < end, v, entries + f) for v, f in zip(videos, frames)]
    allowed = (videos[0] == videos[1]) & (frames[1] <= frames[0]) & (query % 8 == key % 8)
    mask[...] = jnp.where(allowed, 0.0, NEGATIVE)


def scatter_copies(tile, stage, out, sems):
    batch, _, units, rows, width = out.shape
    made = []
    for half in range(2):
        x = pl.ds(half * width, width)
        if tile < WIDEN:
            shards = batch // CHUNKS
            source = stage.at[tile].reshape(shards, 4, rows, CHUNK)
            for sub in range(4):
                unit = sub * 2 + half
                made.append((source.at[:, sub, :, x], out.at[pl.ds(tile * shards, shards), unit // units, unit % units]))
        else:
            unit = 8 + (tile - WIDEN) * 2 + half
            source = stage.at[tile].reshape(batch, rows, CHUNK)
            made.append((source.at[:, :, x], out.at[:, unit // units, unit % units]))
    return [
        pltpu.make_async_copy(source, target, sems.at[tile, number])
        for number, (source, target) in enumerate(made)
    ]


def time_body(place, lengths, *refs, pieces, last):
    came = refs[:pieces]
    gain, offset, entry, leave, bias, weigh, shift, widen, lift, narrow, nudge = refs[pieces : pieces + 11]
    refs = refs[pieces + 11 :]
    if last:
        partial, refs = refs[0], refs[1:]
    sent, refs = refs[:pieces], refs[pieces:]
    grads, sums, triple, weights, mixed, mixed_back, triple_back, mask, held, stage, sems = refs
    _, frames_of, positions, _ = came[0].shape
    window = 8 * pieces * frames_of
    rows = by_position(came, INNER, frames_of, positions)
    blocks = rows.shape[0] // window
    step = pl.program_id(0)

    @pl.when(step == 0)
    def _():
        sums[...] = jnp.zeros_like(sums)
        held[...] = jnp.zeros_like(held)
        fill_mask(mask, place, lengths, frames_of, pieces)
        if last:
            pltpu.make_async_copy(partial, stage, sems.at[0, 0]).start()

    unit, inverse = unit_of(rows)
    normed = (unit * gain[...] + offset[...]).astype(HALF)
    triple[...] = dot(normed, entry[...]).astype(HALF)
    attend_forward(triple, mixed, weights, blocks, window, mask[...])
    middle = rows + dot(mixed[...], leave[...]) + bias[...]
    unit_two, inverse_two = unit_of(middle)
    second = (unit_two * weigh[...] + shift[...]).astype(HALF)
    upstream = by_position(came, COTANGENT, frames_of, positions)
    branch_back = upstream.astype(HALF)
    sums[NUDGE] += column_sum(upstream)
    total = middle + nudge[...]
    second_back = jnp.zeros_like(middle)
    for chunk in range(CHUNKS):
        at = slice(chunk * CHUNK, (chunk + 1) * CHUNK)
        active, slope = gelu_pair(dot(second, widen[:, at]) + lift[:, at])
        active = active.astype(HALF)
        hidden_back = dot_right(branch_back, narrow[at, :]) * slope
        hidden_low = hidden_back.astype(HALF)
        sums[LIFT + chunk] += column_sum(hidden_back)
        total = total + dot(active, narrow[at, :])
        second_back = second_back + dot_right(hidden_low, widen[:, at])
        held[NARROW + chunk] += dot_left(active, branch_back)
        held[WIDEN + chunk] += dot_left(second, hidden_low)
    by_frame(total, sent, RESULT, frames_of, positions)
    sums[WEIGH] += column_sum(second_back * unit_two)
    sums[SHIFT] += column_sum(second_back)
    middle_back = upstream + norm_back(second_back * weigh[...], unit_two, inverse_two)
    attend_back = middle_back.astype(HALF)
    sums[BIAS] += column_sum(middle_back)
    mixed_back[...] = dot_right(attend_back, leave[...]).astype(HALF)
    held[EXIT] += dot_left(mixed[...], attend_back)

    def put(span, pair, part, value):
        triple_back[part, span, columns(pair)] = value

    attend_backward(triple, weights, mixed_back, put, blocks, window)
    normed_back = jnp.zeros_like(middle)
    for part in range(3):
        back = triple_back[part]
        normed_back = normed_back + dot_right(back, entry[:, part * D : (part + 1) * D])
        held[ENTRY + part] += dot_left(normed, back)
    sums[GAIN] += column_sum(normed_back * unit)
    sums[OFFSET] += column_sum(normed_back)
    rows_back = middle_back + norm_back(normed_back * gain[...], unit, inverse)
    by_frame(rows_back, sent, BACK, frames_of, positions)

    @pl.when(step == pl.num_programs(0) - 1)
    def _():
        if last:
            pltpu.make_async_copy(partial, stage, sems.at[0, 0]).wait()
        copies = []
        for tile in range(TILES):
            value = held[tile]
            if last:
                value = value + stage[tile].astype(FLOAT)
            stage[tile] = value.astype(HALF)
            if last:
                made = scatter_copies(tile, stage, grads, sems)
            else:
                made = [pltpu.make_async_copy(stage.at[tile], grads.at[tile], sems.at[tile, 0])]
            for copy in made:
                copy.start()
            copies += made
        for copy in copies:
            copy.wait()


def time_block(place, lengths, came, params, batch, partial=None, step_rows=512):
    pieces = len(came)
    _, per_group, each, window, _ = came[0].shape
    positions = each * window
    flat = (2, per_group, positions, D)
    frames = per_group * pieces
    together = min(max(step_rows // frames, 16), positions)
    rows = together * frames
    steps = positions // together
    count = positions * frames
    attended = 8 * frames
    last = partial is not None
    anywhere = pl.BlockSpec(memory_space=pl.ANY)
    spec = pl.BlockSpec((2, per_group, together, D), lambda i, *_: (0, 0, i, 0))
    grads = (batch, pieces, 2 * TILES // pieces, D // batch, CHUNK // 2) if last else (TILES, CHUNK, CHUNK)
    outs = [(flat, HALF, spec)] * pieces
    outs += [(grads, HALF, anywhere), ((SUMS, 1, D), FLOAT, whole((SUMS, 1, D)))]
    ins = [(array.reshape(flat), spec) for array in came] + plain(params)
    if last:
        ins.append((partial, anywhere))
    made = run(
        functools.partial(time_body, pieces=pieces, last=last),
        "time_block",
        (steps,),
        [place, lengths],
        ins,
        outs,
        scratch=[
            pltpu.VMEM((rows, 3 * D), HALF),
            pltpu.VMEM((rows // attended, PAIRS, attended, 2 * attended), HALF),
            pltpu.VMEM((rows, D), HALF),
            pltpu.VMEM((rows, D), HALF),
            pltpu.VMEM((3, rows, D), HALF),
            pltpu.VMEM((attended, 2 * attended), FLOAT),
            pltpu.VMEM((TILES, CHUNK, CHUNK), FLOAT),
            pltpu.VMEM((TILES, CHUNK, CHUNK), HALF),
            pltpu.SemaphoreType.DMA((TILES, 8)),
        ],
        flops=6 * count * D * (4 * D + 2 * FF),
        moved=count * 2 * D * 4 + 2 * D * (4 * D + 2 * FF),
    )
    shape = (2, per_group, each, window, D)
    sent = [array.reshape(shape) for array in made[:pieces]]
    return sent, made[pieces], made[pieces + 1]


def side_by_side(refs, index=slice(None)):
    return jnp.concatenate([ref[index] for ref in refs], axis=0)


def pick(core, away, own, tiles):
    size = len(tiles) // 2
    for number in range(size):
        one, two = tiles[number], tiles[size + number]
        own[number] = jnp.where(core == 0, one, two).reshape(own.shape[1:])
        away[number] = jnp.where(core == 0, two, one).reshape(away.shape[1:])


def feed_back_body(place, weigh, shift, widen, narrow, *refs, arrays, steps, last):
    came, refs = refs[:arrays], refs[arrays:]
    middles, hiddens, refs = refs[:2], refs[2:4], refs[4:]
    if last:
        partial, refs = refs[0], refs[1:]
    middles_back, refs = refs[0], refs[1:]
    if last:
        narrow_away, narrow_own, away, own, sums, arrived, held, sems, stage, stage_sem = refs
    else:
        tiles, sums, arrived, held, sems = refs
    step = pl.program_id(0)

    def coming(number):
        return [
            pltpu.make_async_copy(
                came[number * 2 + side].at[BACK], arrived.at[number % 2, side], sems.at[number % 2, side]
            )
            for side in range(2)
        ]

    @pl.when(step == 0)
    def _():
        for copy in coming(0):
            copy.start()
        if last:
            pltpu.make_async_copy(partial, stage, stage_sem).start()
        sums[...] = jnp.zeros_like(sums)
        held[...] = jnp.zeros_like(held)

    for number in range(steps):

        @pl.when(step == number)
        def _(number=number):
            for copy in coming(number):
                copy.wait()
            if number + 1 < steps:
                for copy in coming(number + 1):
                    copy.start()

    branch_back = arrived[step % 2].reshape(-1, D)
    upstream = branch_back.astype(FLOAT)
    unit_two, inverse_two = unit_of(side_by_side(middles))
    second = (unit_two * weigh[...] + shift[...]).astype(HALF)
    sums[NUDGE] += column_sum(upstream)
    second_back = jnp.zeros_like(upstream)
    for chunk in range(CHUNKS):
        at = slice(chunk * CHUNK, (chunk + 1) * CHUNK)
        active, slope = gelu_pair(side_by_side(hiddens, (slice(None), at)).astype(FLOAT))
        hidden_back = dot_right(branch_back, narrow[at, :]) * slope
        hidden_low = hidden_back.astype(HALF)
        sums[LIFT + chunk] += column_sum(hidden_back)
        second_back = second_back + dot_right(hidden_low, widen[:, at])
        held[NARROW + chunk] += dot_left(active.astype(HALF), branch_back)
        held[WIDEN + chunk] += dot_left(second, hidden_low)
    sums[WEIGH] += column_sum(second_back * unit_two)
    sums[SHIFT] += column_sum(second_back)
    middle_back = upstream + norm_back(second_back * weigh[...], unit_two, inverse_two)
    middles_back[...] = middle_back
    sums[BIAS] += column_sum(middle_back)

    @pl.when(step == steps - 1)
    def _():
        if not last:
            tiles[...] = held[...].astype(HALF)
            return
        pltpu.make_async_copy(partial, stage, stage_sem).wait()
        value = lambda tile: (held[tile] + stage[tile].astype(FLOAT)).astype(HALF)
        pick(place[4], away, own, [value(WIDEN + chunk) for chunk in range(CHUNKS)])
        _, batch, rows, _ = narrow_own.shape
        shards = batch // CHUNKS
        for chunk in range(CHUNKS):
            parts = value(NARROW + chunk).reshape(shards, 4, rows, CHUNK)
            at = pl.ds(chunk * shards, shards)
            pick(place[4], narrow_away.at[:, at], narrow_own.at[:, at], [parts[:, sub] for sub in range(4)])


def feed_back(place, params, came, middles, hiddens, batch, before=None, after=()):
    pieces = len(came[0])
    part = came[0][0].shape[1:]
    count = middles.shape[0]
    rows = count // (pieces * HALVES)
    last = before is not None
    pairs = [((0, 0), (1, 0)), ((0, 1), (1, 1))] + [((0, k), (0, k + 1)) for k in range(2, pieces, 2)]
    start = len(pairs) if last else 0
    if last:
        pairs = [((1, k), (1, k + 1)) for k in range(2, pieces, 2)]
    steps = len(pairs)
    numbers = [[half * pieces + piece for half, piece in side] for side in zip(*pairs)]
    tables = [jnp.array(side, jnp.int32) for side in numbers]
    block_of = lambda width, side: pl.BlockSpec((rows, width), lambda i, place, *tables: (tables[side][i], 0))
    ins = plain([params[5], params[6], params[7], params[9]])
    ins += [(came[half][piece], pl.BlockSpec(memory_space=pl.ANY)) for pair in pairs for half, piece in pair]
    ins += [(middles, block_of(D, side)) for side in range(2)]
    ins += [(hiddens, block_of(FF, side)) for side in range(2)]
    scratch = [
        pltpu.VMEM((2, 2, *part), HALF),
        pltpu.VMEM((2 * CHUNKS, CHUNK, CHUNK), FLOAT),
        pltpu.SemaphoreType.DMA((2, 2)),
    ]
    outs = [((count, D), FLOAT, row_spec(2 * rows, D, lambda i, *_: start + i))]
    aliases = {}
    if last:
        aliases = {0: before[0]}
        ins.append((before[1], pl.BlockSpec(memory_space=pl.ANY)))
        tiles = (2, batch, D // batch, CHUNK)
        outs += [(tiles, HALF, whole(tiles))] * 4
        scratch += [pltpu.VMEM((2 * CHUNKS, CHUNK, CHUNK), HALF), pltpu.SemaphoreType.DMA]
    else:
        tiles = (2 * CHUNKS, CHUNK, CHUNK)
        outs.append((tiles, HALF, whole(tiles)))
    outs.append(((SUMS, 1, D), FLOAT, whole((SUMS, 1, D))))
    body = functools.partial(feed_back_body, arrays=2 * steps, steps=steps, last=last)
    return run(
        lambda place, one, two, *refs: body(place, *refs),
        "feed_back",
        (steps,),
        [place, *tables],
        ins,
        outs,
        scratch=scratch,
        aliases=aliases,
        after=after,
        flops=16 * rows * steps * D * FF * (1 if last else FIRST_FEED),
        moved=2 * rows * steps * (10 * D + 2 * FF) + 8 * D * FF,
    )


def attention_back_body(place, rows_in, gain, offset, entry, leave, *refs, window, pieces):
    came, refs = refs[: HALVES * pieces], refs[HALVES * pieces :]
    triples, weights, mixes, middles_back = [refs[HALVES * k : HALVES * (k + 1)] for k in range(4)]
    delta, outcome, away, own, sums, mixed_back, triple_back, held, sems = refs[4 * HALVES :]
    step = pl.program_id(0)
    each = rows_in.shape[1] // HALVES

    def results(piece):
        return [
            pltpu.make_async_copy(
                came[half * pieces + piece].at[RESULT],
                outcome.at[:, pl.ds(half * each, each)],
                sems.at[half],
            )
            for half in range(HALVES)
        ]

    @pl.when(step == 0)
    def _():
        sums[...] = jnp.zeros_like(sums)
        held[...] = jnp.zeros_like(held)

    for piece in range(pieces):

        @pl.when(step == piece)
        def _(piece=piece):
            for copy in results(piece):
                copy.start()

    parts = [rows_in[:, half * each : (half + 1) * each].reshape(-1, D) for half in range(HALVES)]
    count = parts[0].shape[0]
    middle_back = side_by_side(middles_back)
    attend_back = middle_back.astype(HALF)
    mixed_back[...] = dot_right(attend_back, leave[...]).astype(HALF)
    held[3] += dot_left(side_by_side(mixes), attend_back)
    unit, inverse = unit_of(jnp.concatenate(parts, axis=0).astype(FLOAT))
    normed = (unit * gain[...] + offset[...]).astype(HALF)
    for half in range(HALVES):
        span = pl.ds(half * count, count)
        back = triple_back.at[:, span]

        def put(rows, pair, part, value, back=back):
            back[part, rows, columns(pair)] = value

        attend_backward(triples[half], weights[half], mixed_back.at[span], put, count // window, window)
    normed_back = jnp.zeros_like(middle_back)
    for part in range(3):
        back = triple_back[part]
        normed_back = normed_back + dot_right(back, entry[:, part * D : (part + 1) * D])
        held[part] += dot_left(normed, back)
    sums[GAIN] += column_sum(normed_back * unit)
    sums[OFFSET] += column_sum(normed_back)
    rows_back = (middle_back + norm_back(normed_back * gain[...], unit, inverse)).astype(HALF)
    for half in range(HALVES):
        delta[:, half * each : (half + 1) * each] = rows_back[half * count : (half + 1) * count].reshape(
            -1, each, window, D
        )

    @pl.when(step == pl.num_programs(0) - 1)
    def _():
        pick(place[4], away, own, [held[tile].astype(HALF) for tile in range(4)])

    for piece in range(pieces):

        @pl.when(step == piece)
        def _(piece=piece):
            for copy in results(piece):
                copy.wait()


def attention_back(place, frames, params, came, triple, weights, mixed, middles_back, batch, after):
    pieces = len(came[0])
    per_group, windows, window, _ = frames.shape
    block = (per_group, windows // pieces, window, D)
    rows = per_group * block[1] * window // HALVES
    cut = pl.BlockSpec(block, lambda i, place: (0, place[0] ^ i, 0, 0))
    attended = (rows // window, PAIRS, window, 2 * window)
    halves = range(HALVES)
    spread_out = lambda half: lambda i, place: jnp.where(i < 2, 2 * i + half, i + (pieces if half else 2))
    ins = [(frames, cut)] + plain(params[:4])
    ins += [(array, pl.BlockSpec(memory_space=pl.ANY)) for half in came for array in half]
    ins += [(triple, row_spec(rows, 3 * D, lambda i, place, h=h: h * pieces + i)) for h in halves]
    ins += [
        (weights, pl.BlockSpec(attended, lambda i, place, h=h: (h * pieces + i, 0, 0, 0))) for h in halves
    ]
    ins += [(mixed, row_spec(rows, D, lambda i, place, h=h: h * pieces + i)) for h in halves]
    ins += [(middles_back, row_spec(rows, D, spread_out(h))) for h in halves]
    tiles = (2, batch, D // batch, CHUNK)
    count = rows * pieces * HALVES
    return run(
        functools.partial(attention_back_body, window=window, pieces=pieces),
        "attention_back",
        (pieces,),
        [place],
        ins,
        [
            (frames.shape, HALF, cut),
            (frames.shape, HALF, cut),
            *[(tiles, HALF, whole(tiles))] * 2,
            ((SUMS, 1, D), FLOAT, whole((SUMS, 1, D))),
        ],
        scratch=[
            pltpu.VMEM((rows * HALVES, D), HALF),
            pltpu.VMEM((3, rows * HALVES, D), HALF),
            pltpu.VMEM((4, CHUNK, CHUNK), FLOAT),
            pltpu.SemaphoreType.DMA((HALVES,)),
        ],
        after=after,
        flops=16 * count * D * D,
        moved=count * D * 2 * (3 + 1 + 1 + 2 + 2 + 4),
    )


def swap(value, axis, mask):
    size = lax.axis_size(axis)
    if mask == 0:
        return value
    return lax.ppermute(value, axis, [(i, i ^ mask) for i in range(size)])


def move(value, batch_mask, win_mask):
    if batch_mask == 0:
        return swap(value, "win", win_mask)
    if win_mask == 0:
        return swap(value, "batch", batch_mask)
    batch, win = lax.axis_size("batch"), lax.axis_size("win")
    pairs = [
        (b * win + w, (b ^ batch_mask) * win + (w ^ win_mask)) for b in range(batch) for w in range(win)
    ]
    return lax.ppermute(value, ("batch", "win"), pairs)


def exchange(arrays):
    made = {k: swap(arrays[k], "win", k) for k in reversed(range(len(arrays)))}
    return [made[k] for k in range(len(arrays))]


def split_body(place, *refs, groups, across):
    own, got, outs = refs[:groups], refs[groups : 2 * groups], refs[2 * groups :]
    column, row = place[1], place[2]
    width = CHUNK // across
    at = 0
    for one, two in zip(own, got):
        rows = one.shape[3]
        for tile in range(one.shape[0]):
            for piece, out in enumerate(outs):
                y = row ^ (piece % 2)
                x = pl.ds(pl.multiple_of((column ^ (piece // 2)) * width, width), width)
                total = one[tile, :, y, :, x].astype(FLOAT) + two[tile, :, y, :, x].astype(FLOAT)
                out[:, at : at + rows] = total.astype(HALF)
            at += rows


def merge_body(place, *refs, inputs):
    ins, outs = refs[:inputs], refs[inputs:]
    for piece, out in enumerate(outs):
        z = place[3] ^ piece
        total = ins[0][z].astype(FLOAT)
        for ref in ins[1:]:
            total = total + ref[z].astype(FLOAT)
        out[...] = total.astype(HALF)


def last_body(*refs):
    ins, out = refs[:-1], refs[-1]
    total = ins[0][...].astype(FLOAT)
    for ref in ins[1:]:
        total = total + ref[...].astype(FLOAT)
    out[...] = total.astype(HALF)


def unpack_body(place, *refs, pieces, across, layout):
    ins, outs, held = refs[:pieces], refs[pieces:-1], refs[-1]
    width = CHUNK // across
    for piece, ref in enumerate(ins):
        x = pl.ds(pl.multiple_of((place[1] ^ (piece // 2)) * width, width), width)
        held[place[4] ^ (piece % 2), :, x] = ref[...].astype(FLOAT)
    for out, places in zip(outs, layout):
        for core, start, rows, left, wide, row, column in places:
            out[row : row + rows, column : column + wide] = held[
                core, start : start + rows, left : left + wide
            ]


def arrived_body(*refs):
    refs[-1][...] = jnp.zeros_like(refs[-1])


def arrived(arrays):
    shape = (8, 128)
    outs = [(shape, FLOAT, whole(shape))]
    return run(
        arrived_body, "arrived", (1,), [], [], outs, after=arrays, flops=ARRIVED_FLOPS, vmem=SMALL_VMEM
    )


class Reduction:
    def __init__(self, place, away, own):
        self.place = place
        self.batch, self.win = lax.axis_size("batch"), lax.axis_size("win")
        self.across, self.depth = self.win // 2, self.batch // 2
        cut = lambda a: a.reshape(-1, self.depth, 2, *a.shape[2:])
        self.own = [cut(a) for a in own]
        self.got = [swap(cut(a), "win", 1) for a in away]
        self.rows = sum(a.shape[0] * a.shape[3] for a in self.own)
        self.width = CHUNK // self.across

    def cores(self, after=()):
        shape = (self.depth, self.rows, self.width)
        pieces = run(
            functools.partial(split_body, groups=len(self.own), across=self.across),
            "sum_cores",
            (1,),
            [self.place],
            plain(self.own + self.got),
            [(shape, HALF, whole(shape))] * (2 * self.across),
            after=after,
            vmem=SMALL_VMEM,
            flops=SMALL_FLOPS,
        )
        self.mark = pieces[:1]
        self.pieces = [move(a, number % 2, 2 * (number // 2)) for number, a in enumerate(pieces)]

    def chips(self, after=(), flops=SMALL_FLOPS):
        shape = (self.rows, self.width)
        pieces = run(
            functools.partial(merge_body, inputs=len(self.pieces)),
            "sum_chips",
            (1,),
            [self.place],
            plain(self.pieces),
            [(shape, HALF, whole(shape))] * self.depth,
            after=after,
            vmem=SMALL_VMEM,
            flops=flops,
        )
        self.mark = pieces[:1]
        self.pieces = [swap(a, "batch", 2 * number) for number, a in enumerate(pieces)]

    def last(self, after=()):
        shape = (self.rows, self.width)
        outs = [(shape, HALF, whole(shape))]
        (total,) = run(last_body, "sum_last", (1,), [], plain(self.pieces), outs, after=after, vmem=SMALL_VMEM, flops=SMALL_FLOPS)
        self.mark = [total]
        self.pieces = [swap(total, "win", number) for number in range(self.win)]

    def unpack(self, layout, shapes, after=()):
        return run(
            functools.partial(
                unpack_body, pieces=self.win, across=self.across, layout=layout
            ),
            "unpack",
            (1,),
            [self.place],
            plain(self.pieces),
            [(s, FLOAT, whole(s)) for s in shapes],
            scratch=[pltpu.VMEM((2, self.rows, CHUNK), FLOAT)],
            after=after,
            vmem=SMALL_VMEM,
            flops=SMALL_FLOPS,
        )


def spread_body(place, *refs, pieces, layout):
    ins, outs, held = refs[:pieces], refs[pieces:-1], refs[-1]
    for piece, ref in enumerate(ins):
        held[place[0] ^ piece] = ref[...].astype(FLOAT)
    units = held.shape[1]
    rows, width = held.shape[2:]
    for out, places in zip(outs, layout):
        for unit, row, column in places:
            out[row * rows : (row + 1) * rows, column * width : (column + 1) * width] = held[
                unit // units, unit % units
            ]


def spread_units(place, total, win, rows, after=()):
    units = total.shape[0] // rows
    width = total.shape[1]
    pieces = [swap(total, "win", number).reshape(units, rows, width) for number in range(win)]
    spot = lambda tile, row, column: [(8 + tile * 2 + half, row, column * 2 + half) for half in range(2)]
    narrow = [(sub * 2 + half, sub, half) for sub in range(4) for half in range(2)]
    layout = [
        sum([spot(chunk, 0, chunk) for chunk in range(CHUNKS)], []),
        narrow,
        sum([spot(CHUNKS + part, 0, part) for part in range(3)], []),
        spot(CHUNKS + 3, 0, 0),
    ]
    shapes = [(rows, FF), (4 * rows, D), (rows, 3 * D), (rows, D)]
    return run(
        functools.partial(spread_body, pieces=win, layout=layout),
        "spread_units",
        (1,),
        [place],
        plain(pieces),
        [(s, FLOAT, whole(s)) for s in shapes],
        scratch=[pltpu.VMEM((win, units, rows, width), FLOAT)],
        after=after,
            vmem=SMALL_VMEM,
            flops=SMALL_FLOPS,
    )


SMALL_ROWS = 16


def small_tiles(core, sums, batch):
    blocks = len(sums)
    sums = jnp.stack(sums)[:, :, 0]
    vectors = sums[:, :6].reshape(blocks, 6, batch, -1).transpose(2, 0, 1, 3).reshape(batch, blocks, -1)
    lifts = sums[:, LIFT:].reshape(blocks, batch, -1).swapaxes(0, 1)
    pad = lambda a: jnp.pad(a, ((0, 0), (0, SMALL_ROWS - blocks), (0, CHUNK - a.shape[2])))
    both = [pad(a).astype(HALF)[None] for a in (vectors, lifts)]
    return jnp.where(core == 0, both[1], both[0]), jnp.where(core == 0, both[0], both[1])


def attend_places(rows, start):
    spot = lambda tile: (tile // 2, start + tile % 2 * rows, rows, 0, CHUNK)
    return [
        [(*spot(part), 0, part * CHUNK) for part in range(3)],
        [(*spot(3), 0, 0)],
    ], [(rows, 3 * D), (rows, D)]


def feed_places(rows, start):
    narrows = [(sub // 2, start + sub % 2 * rows, rows, 0, CHUNK, sub * rows, 0) for sub in range(4)]
    start += 2 * rows
    widens = [
        (chunk // 2, start + chunk % 2 * rows, rows, 0, CHUNK, 0, chunk * CHUNK) for chunk in range(CHUNKS)
    ]
    return [widens, narrows], [(rows, FF), (4 * rows, D)]


def small_places(rows, start):
    layout, shapes = [], []
    for block in range(2):
        layout += [[(0, start + block, 1, number * rows, rows, 0, 0)] for number in range(6)]
        layout.append([(1, start + block, 1, 0, 4 * rows, 0, 0)])
        shapes += [(1, rows)] * 6 + [(1, 4 * rows)]
    return layout, shapes


def local(*args):
    frames, cotangent, video_frames = args[0], args[23], args[24]
    space = [a.reshape(1, -1) if a.ndim == 1 else a for a in args[1:12]]
    time = [a.reshape(1, -1) if a.ndim == 1 else a for a in args[12:23]]
    batch, win = lax.axis_size("batch"), lax.axis_size("win")
    here, group = lax.axis_index("win"), lax.axis_index("batch")
    core = here % 2
    place = jnp.stack([here, here // 2, group % 2, group // 2, core]).astype(jnp.int32)
    _, per_group, _, windows, window, _ = frames.shape
    shape = (per_group, windows, window, D)
    rows_in, cotangent = frames.reshape(shape), cotangent.reshape(shape)
    rows = D // batch

    kept, came = [], []
    for half in range(HALVES):
        sent, kept = space_forward(place, rows_in, cotangent, space, half, win, kept)
        came.append(exchange(sent))
    triple, weights, mixed, middles, hiddens = kept
    backs, time_sums, tiles = [], [], None
    for half in range(HALVES):
        sent, tiles, sums = time_block(place, video_frames, came[half], time, batch, tiles)
        backs.append(exchange(sent))
        time_sums.append(sums)

    time_tiles = tiles.reshape(batch * win, -1, CHUNK // 2)
    time_total = lax.psum_scatter(time_tiles, ("batch", "win"), scatter_dimension=0, tiled=True)[0]
    mark = [*arrived(backs[0][1:]), tiles]
    *fed, first_sums = feed_back(place, space, backs, middles, hiddens, batch, after=mark)
    middles_back, narrow_away, narrow_own, away, own, feed_sums = feed_back(
        place, space, backs, middles, hiddens, batch, fed
    )
    feed_sum = Reduction(place, [narrow_away, away], [narrow_own, own])
    feed_sum.cores()
    delta, outcome, away, own, attend_sums = attention_back(
        place, rows_in, space, backs, triple, weights, mixed, middles_back, batch, feed_sum.mark
    )
    small_away, small_own = small_tiles(
        core, [first_sums + feed_sums + attend_sums, sum(time_sums)], batch
    )
    attend_sum = Reduction(place, [away, small_away], [own, small_own])
    feed_sum.chips([delta], 10 * SMALL_FLOPS)
    attend_sum.cores(feed_sum.mark)
    feed_sum.last(attend_sum.mark)
    attend_sum.chips(feed_sum.mark)
    feed_layout, feed_shapes = feed_places(rows, 0)
    feed_grads = feed_sum.unpack(feed_layout, feed_shapes, attend_sum.mark)
    attend_sum.last(feed_grads[:1])
    time_grads = spread_units(place, time_total, win, rows, attend_sum.mark)
    attend_layout, attend_shapes = attend_places(rows, 0)
    small_layout, small_shapes = small_places(rows, 2 * rows)
    attend_grads = attend_sum.unpack(
        attend_layout + small_layout, attend_shapes + small_shapes, time_grads[:1]
    )
    smalls = [a.reshape(-1) for a in attend_grads[2:]]

    def collected(grads, smalls):
        widen, narrow, entry, leave = grads
        gain, offset, bias, weigh, shift, nudge, lift = smalls
        return gain, offset, entry, leave, bias, weigh, shift, widen, lift, narrow, nudge

    return (
        outcome.reshape(frames.shape),
        delta.reshape(frames.shape),
        *collected([*feed_grads, *attend_grads[:2]], smalls[:7]),
        *collected(time_grads, smalls[7:]),
    )


def solution(mesh):
    rows = P("batch", None, "win", None, None, None)
    one, two = P("batch"), P("batch", None)
    grads = (one, one, two, two, one, one, one, two, one, two, one)
    return jax.shard_map(
        local,
        mesh=mesh,
        in_specs=(rows, *([P()] * 22), rows, P("batch", None)),
        out_specs=(rows, rows, *grads, *grads),
        check_vma=False,
    )
```

time: 321 us -> 297 us (0.925); the launches traced: 320 us -> 292 us
  Pallas kernels: 236 us -> 197 us
  waiting for transfers between devices: 24 us -> 30.7 us
  starting transfers between devices: 32.6 us -> 37 us
    pallas_call x20 -> x17, Pallas kernels: 236 us -> 197 us  [run(): pl.pallas_call(inner, out_shape=[jax.ShapeDtypeStruct(shape, kind) for sh...]
    ppermute x35, waiting for transfers between devices: 11.9 us -> 19.1 us  [swap(): return lax.ppermute(value, axis, [(i, i ^ mask) for i in range(size)])]
    ppermute x2, waiting for transfers between devices: 6.44 us -> 1.74 us  [move(): return lax.ppermute(value, ('batch', 'win'), pairs)]
    reduce_scatter x1, waiting for transfers between devices: 5.65 us -> 9.89 us  [local(): lax.psum_scatter(time_tiles, ('batch', 'win'), scatter_dimension=0, tiled...]
    ppermute x35, starting transfers between devices: 30.9 us -> 34.8 us  [swap(): return lax.ppermute(value, axis, [(i, i ^ mask) for i in range(size)])]
    unnamed x68 -> x46, local copies, waits for them, and re-layouts: 8.43 us -> 9.89 us
  transfers between devices with their start and end apart: 38 -> 38, of which waited for: 6 -> 10; matrix products, arithmetic and copies ran while one was open for 1% -> 1% of each run, Pallas kernels for 66% -> 60%
where the time goes in v3:
time: 297 us; the launch traced here: 292 us
  Pallas kernels  197 us (66%)
  starting transfers between devices  37 us (12%)
  waiting for transfers between devices  30.7 us (10%)
  between operations  14.7 us (5%)
  local copies, waits for them, and re-layouts  11.4 us (4%)
    pallas_call x17, Pallas kernels, run(): pl.pallas_call(inner, out_shape=[jax.ShapeDtypeStruct(shape, kind) for sh...  197 us
    ppermute x35, starting transfers between devices, swap(): return lax.ppermute(value, axis, [(i, i ^ mask) for i in range(size)])  34.8 us
    ppermute x35, waiting for transfers between devices, swap(): return lax.ppermute(value, axis, [(i, i ^ mask) for i in range(size)])  19.1 us
    unnamed x46, local copies, waits for them, and re-layouts  9.89 us
    reduce_scatter x1, waiting for transfers between devices, local(): lax.psum_scatter(time_tiles, ('batch', 'win'), scatter_dimension=0, tiled...  9.89 us
  transfers between devices with their start and end apart: 38, of which 10 were waited for; matrix products, arithmetic and copies ran while one was open for 1% of the time, Pallas kernels for 60%

profile of v3, /device:TPU:0, one launch (start us, length us, event | category | flops | bytes accessed | tf_op | source)
XLA Modules:
  0.0 291.8 jit_solution(1468502276086852192)
XLA Ops:
  7.3 0.6 stack.32.refs_0_
  7.9 20.5 %space_forward.2 = (bf16[2,2,2,64,512]{4,3,2,1,0:T(8,128)(2,1)}, bf16[2,2,2,64,512]{4,3,2,1,0:T(8,128)(2,1)}, bf16[2,2,2,64,512]{4,3,2,1,0:T(8,128)(2,1)}, bf16[...) custom-call(s32[5]{0:T(128)} %stack.32.refs_0_, ...), custom_call_target="tpu_custom_call" | custom-call | flops 25769803776 | bytes 58720256 | tf_op jit(solution)/shard_map/space_forward/pallas_call | solution.py:163
  28.3 0.5 collective-permute-start
  28.9 2.5 collective-permute-start.1
  31.5 20.6 %space_forward.3 = (bf16[2,2,2,64,512]{4,3,2,1,0:T(8,128)(2,1)}, bf16[2,2,2,64,512]{4,3,2,1,0:T(8,128)(2,1)}, bf16[2,2,2,64,512]{4,3,2,1,0:T(8,128)(2,1)}, bf16[...) custom-call(s32[5]{0:T(128)} %stack.32.refs_0_, ...), custom_call_target="tpu_custom_call", output_to_operand_aliasing={{4}: (14, {}), {5}: (15, {}), {6}: (16, {}), {7}: (17, {}),... | custom-call | flops 25769803776 | bytes 58720256 | tf_op jit(solution)/shard_map/space_forward/pallas_call | solution.py:163
  52.1 0.2 collective-permute-start.6
  52.3 2.0 collective-permute-start.7
  54.3 1.0 collective-permute-done.2
  55.2 38.9 %time_block.2 = (bf16[2,2,128,512]{3,2,1,0:T(8,128)(2,1)}, bf16[2,2,128,512]{3,2,1,0:T(8,128)(2,1)}, bf16[2,2,128,512]{3,2,1,0:T(8,128)(2,1)}, bf16[2,2,128,512]...) custom-call(s32[5]{0:T(128)} %stack.32.refs_0_, s32[1,8]{1,0:T(1,128)} %refs_1_.5, ...), custom_call_target="tpu_custom_call" | custom-call | flops 77309411328 | bytes 41943040 | tf_op jit(solution)/shard_map/time_block/pallas_call | solution.py:163
  94.3 1.8 collective-permute-start.4
  96.2 0.8 copy-done.20
  97.0 39.3 %time_block.3 = (bf16[2,2,128,512]{3,2,1,0:T(8,128)(2,1)}, bf16[2,2,128,512]{3,2,1,0:T(8,128)(2,1)}, bf16[2,2,128,512]{3,2,1,0:T(8,128)(2,1)}, bf16[2,2,128,512]...) custom-call(s32[5]{0:T(128)} %stack.32.refs_0_, s32[1,8]{1,0:T(1,128)} %refs_1_.5, ...), custom_call_target="tpu_custom_call" | custom-call | flops 77309411328 | bytes 41943040 | tf_op jit(solution)/shard_map/time_block/pallas_call | solution.py:163
  136.3 0.3 collective-permute-start.9
  136.7 1.8 collective-permute-start.10
  138.7 0.6 copy-done.4
  139.7 0.8 copy-done.19
  140.5 0.5 call_exported.0.refs_1_
  141.0 27.5 %feed_back.2 = (f32[2048,512]{1,0:T(8,128)}, bf16[8,512,512]{2,1,0:T(8,128)(2,1)}, f32[10,1,512]{2,1,0:T(1,128)}) custom-call(s32[5]{0:T(128)} %stack.32.refs_0_, s32[3]{0:T(128)} %call_exported.0.refs_1_, s32[3]{0:T(128)} %constant.56.clone.refs_2_, f32[1,512]{1,0:T(1,128)} %bitcast.140, f32[1,512]{1,0:T(1,128)} %bitcast.144, bf16[512,2048]{1,0:T(8,128)(2,1)} %refs_5_.8, ...), custom_call_target="tpu_custom_call" | custom-call | flops 103079215104 | bytes 90177536 | tf_op jit(solution)/shard_map/feed_back/pallas_call | solution.py:163
  168.6 14.2 %feed_back.3 = (f32[2048,512]{1,0:T(8,128)}, bf16[2,8,64,512]{3,2,1,0:T(8,128)(2,1)}, bf16[2,8,64,512]{3,2,1,0:T(8,128)(2,1)}, bf16[2,8,64,512]{3,2,1,0:T(8,128)...) custom-call(s32[5]{0:T(128)} %stack.32.refs_0_, ...), custom_call_target="tpu_custom_call", output_to_operand_aliasing={{0}: (14, {})} | custom-call | flops 17179869184 | bytes 52428800 | tf_op jit(solution)/shard_map/feed_back/pallas_call | solution.py:163
  182.8 0.3 collective-permute-start.12
  183.1 0.3 collective-permute-start.13
  183.4 2.3 collective-permute-done.12.refs_3_
  185.7 1.5 collective-permute-done.13.refs_4_
  187.2 1.2 copy-done
  188.5 1.5 copy-done.1
  190.0 1.9 sum_cores.2
  192.0 0.8 copy-done.7
  192.8 1.7 collective-permute-start.16
  194.5 1.5 collective-permute-start.17
  196.0 0.3 collective-permute-start.18
  196.3 25.7 %attention_back.1 = (bf16[2,16,64,512]{3,2,1,0:T(8,128)(2,1)}, bf16[2,16,64,512]{3,2,1,0:T(8,128)(2,1)}, bf16[2,8,64,512]{3,2,1,0:T(8,128)(2,1)}, bf16[2,8,64,512]{3,2,1,0:T(8,128)(2,1)}, f32[10,1,512]{2,1,0:T(1,128)}) custom-call(s32[5]{0:T(128)} %stack.32.refs_0_, bf16[2,16,64,512]{3,2,1,0:T(8,128)(2,1)} %bitcast.106, f32[1,512]{1,0:T(1,128)} %bitcast.148, ...), custom_call_target="tpu_custom_call" | custom-call | flops 34359738368 | bytes 109051904 | tf_op jit(solution)/shard_map/attention_back/pallas_call | solution.py:163
  222.1 0.8 add_bitcast_fusion.1
  223.4 0.5 collective-permute-start.15
  223.9 1.7 collective-permute-done.18.refs_4_
  225.7 1.6 copy-done.10
  227.3 2.0 sum_chips.2
  229.3 1.6 collective-permute-start.22
  230.8 0.8 sum_cores.3
  231.6 0.6 collective-permute-start.19
  232.3 1.0 collective-permute-start.20
  233.3 1.9 collective-permute-start.21
  235.2 2.4 collective-permute-start.23
  237.6 1.9 collective-permute-done.22.refs_1_
  239.5 3.6 %collective-permute-start.24 = (bf16[256,256]{1,0:T(8,128)(2,1)S(1)}, bf16[256,256]{1,0:T(8,128)(2,1)S(1)}, u32[]{:S(2)}, u32[]{:S(2)}) collective-permute-start(bf16[256,256]{1,0:T(8,128)(2,1)S(1)} %get-tuple-element.161), channel_id=1, source_target_pairs={{0,24},{4,28},{8,16},{12,20},{16,8},{20,12},{24,0},{28,4},{1,25},{... | collective-permute-start | bytes 393224 | tf_op jit(solution)/shard_map/ppermute | solution.py:711
  243.1 5.9 %collective-permute-done.23.refs_2_ = bf16[256,256]{1,0:T(8,128)(2,1)S(1)} collective-permute-done((bf16[256,256]{1,0:T(8,128)(2,1)S(1)}, bf16[256,256]{1,0:T(8,128)(2,1)S(1)}, u32[]{:S(2)}, u32[]{:S(2)}) %collective-permute-start.23) | collective-permute-done | bytes 131104 | tf_op jit(solution)/shard_map/ppermute | solution.py:711
  249.2 1.1 collective-permute-start.29
  250.3 0.8 collective-permute-start.30
  251.1 0.7 sum_chips.3
  251.8 2.6 collective-permute-start.25
  254.4 9.9 %reduce-scatter.2.cloned.1.call-done = bf16[1,384,256]{2,1,0:T(8,128)(2,1)} async-done(((bf16[32,384,256]{2,1,0:T(8,128)(2,1)}), bf16[1,384,256]{2,1,0:T(8,128)(2,1)}) %reduce-scatter.2.cloned.1.call-update) | async-done | bytes 196624 | tf_op jit(solution)/shard_map/reduce_scatter | solution.py:961
  264.3 1.2 collective-permute-start.35
  265.4 0.7 collective-permute-start.36
  266.1 1.1 collective-permute-start.26
  267.3 2.1 collective-permute-start.27
  269.4 1.6 unpack.2
  271.0 4.0 %collective-permute-done.26.refs_2_ = bf16[144,256]{1,0:T(8,128)(2,1)S(1)} collective-permute-done((bf16[144,256]{1,0:T(8,128)(2,1)S(1)}, bf16[144,256]{1,0:T(8,128)(2,1)S(1)}, u32[]{:S(2)}, u32[]{:S(2)}) %collective-permute-start.26) | collective-permute-done | bytes 73760 | tf_op jit(solution)/shard_map/ppermute | solution.py:711
  275.0 1.0 copy-done.12
  276.2 1.5 collective-permute-start.32
  277.7 0.3 collective-permute-start.33
  278.0 1.8 spread_units.1
  279.9 1.2 collective-permute-done.32.refs_3_
  281.0 1.2 collective-permute-done.33.refs_4_
  282.2 1.0 copy-done.13
  283.3 1.4 unpack.3
  (92 shorter events, 1.7 us)
Async XLA Ops:
  7.2 257.1 %reduce-scatter.2.cloned.1.call-start = ((), (), s32[]{:S(2)}) async-start(), calls=%async_computation.1 | async-start | bytes 6488064 | tf_op jit(solution)/shard_map/reduce_scatter | solution.py:961
  28.3 25.9 %collective-permute-start = (bf16[2,2,2,64,512]{4,3,2,1,0:T(8,128)(2,1)}, bf16[2,2,2,64,512]{4,3,2,1,0:T(8,128)(2,1)S(1)}, u32[]{:S(2)}, u32[]{:S(2)}) collective-permute-start(bf16[2,2,2,64,512]{4,3,2,1,0:T(8,128)(2,1)} %get-tuple-element.107), channel_id=1, source_target_pairs={{0,1},{1,0},{2,3},{3,2},{4,5},{5,4},{6,7},{7,6},{8,9},{9,8},{10,11... | collective-permute-start | bytes 1572872 | tf_op jit(solution)/shard_map/ppermute | solution.py:711
  28.9 25.4 %collective-permute-start.1 = (bf16[2,2,2,64,512]{4,3,2,1,0:T(8,128)(2,1)}, bf16[2,2,2,64,512]{4,3,2,1,0:T(8,128)(2,1)S(1)}, u32[]{:S(2)}, u32[]{:S(2)}) collective-permute-start(bf16[2,2,2,64,512]{4,3,2,1,0:T(8,128)(2,1)} %get-tuple-element.108), channel_id=1, source_target_pairs={{0,2},{1,3},{2,0},{3,1},{4,6},{5,7},{6,4},{7,5},{8,10},{9,11},{10,... | collective-permute-start | bytes 1572872 | tf_op jit(solution)/shard_map/ppermute | solution.py:711
  31.4 23.8 %collective-permute-start.2 = (bf16[2,2,2,64,512]{4,3,2,1,0:T(8,128)(2,1)}, bf16[2,2,2,64,512]{4,3,2,1,0:T(8,128)(2,1)}, u32[]{:S(2)}, u32[]{:S(2)}) collective-permute-start(bf16[2,2,2,64,512]{4,3,2,1,0:T(8,128)(2,1)} %get-tuple-element.109), channel_id=1, source_target_pairs={{0,3},{1,2},{2,1},{3,0},{4,7},{5,6},{6,5},{7,4},{8,11},{9,10},{10,... | collective-permute-start | bytes 1572872 | tf_op jit(solution)/shard_map/ppermute | solution.py:711
  52.1 44.1 %collective-permute-start.6 = (bf16[2,2,2,64,512]{4,3,2,1,0:T(8,128)(2,1)}, bf16[2,2,2,64,512]{4,3,2,1,0:T(8,128)(2,1)S(1)}, u32[]{:S(2)}, u32[]{:S(2)}) collective-permute-start(bf16[2,2,2,64,512]{4,3,2,1,0:T(8,128)(2,1)} %get-tuple-element.120), channel_id=1, source_target_pairs={{0,1},{1,0},{2,3},{3,2},{4,5},{5,4},{6,7},{7,6},{8,9},{9,8},{10,11... | collective-permute-start | bytes 1572872 | tf_op jit(solution)/shard_map/ppermute | solution.py:711
  52.3 44.7 %collective-permute-start.7 = (bf16[2,2,2,64,512]{4,3,2,1,0:T(8,128)(2,1)}, bf16[2,2,2,64,512]{4,3,2,1,0:T(8,128)(2,1)}, u32[]{:S(2)}, u32[]{:S(2)}) collective-permute-start(bf16[2,2,2,64,512]{4,3,2,1,0:T(8,128)(2,1)} %get-tuple-element.121), channel_id=1, source_target_pairs={{0,2},{1,3},{2,0},{3,1},{4,6},{5,7},{6,4},{7,5},{8,10},{9,11},{10,... | collective-permute-start | bytes 1572872 | tf_op jit(solution)/shard_map/ppermute | solution.py:711
  54.2 1.0 copy-start.21
  54.2 42.8 %collective-permute-start.8 = (bf16[2,2,2,64,512]{4,3,2,1,0:T(8,128)(2,1)}, bf16[2,2,2,64,512]{4,3,2,1,0:T(8,128)(2,1)}, u32[]{:S(2)}, u32[]{:S(2)}) collective-permute-start(bf16[2,2,2,64,512]{4,3,2,1,0:T(8,128)(2,1)} %get-tuple-element.122), channel_id=1, source_target_pairs={{0,3},{1,2},{2,1},{3,0},{4,7},{5,6},{6,5},{7,4},{8,11},{9,10},{10,... | collective-permute-start | bytes 1572872 | tf_op jit(solution)/shard_map/ppermute | solution.py:711
  54.2 1.0 copy-start.22
  94.2 44.4 %collective-permute-start.3 = (bf16[2,2,2,64,512]{4,3,2,1,0:T(8,128)(2,1)}, bf16[2,2,2,64,512]{4,3,2,1,0:T(8,128)(2,1)S(1)}, u32[]{:S(2)}, u32[]{:S(2)}) collective-permute-start(bf16[2,2,2,64,512]{4,3,2,1,0:T(8,128)(2,1)} %bitcast.113), channel_id=1, source_target_pairs={{0,1},{1,0},{2,3},{3,2},{4,5},{5,4},{6,7},{7,6},{8,9},{9,8},{10,11... | collective-permute-start | bytes 1572872 | tf_op jit(solution)/shard_map/ppermute | solution.py:711
  94.3 44.3 %collective-permute-start.4 = (bf16[2,2,2,64,512]{4,3,2,1,0:T(8,128)(2,1)}, bf16[2,2,2,64,512]{4,3,2,1,0:T(8,128)(2,1)S(1)}, u32[]{:S(2)}, u32[]{:S(2)}) collective-permute-start(bf16[2,2,2,64,512]{4,3,2,1,0:T(8,128)(2,1)} %bitcast.111), channel_id=1, source_target_pairs={{0,2},{1,3},{2,0},{3,1},{4,6},{5,7},{6,4},{7,5},{8,10},{9,11},{10,... | collective-permute-start | bytes 1572872 | tf_op jit(solution)/shard_map/ppermute | solution.py:711
  96.2 0.8 copy-start.20
  97.0 41.7 %collective-permute-start.5 = (bf16[2,2,2,64,512]{4,3,2,1,0:T(8,128)(2,1)}, bf16[2,2,2,64,512]{4,3,2,1,0:T(8,128)(2,1)S(1)}, u32[]{:S(2)}, u32[]{:S(2)}) collective-permute-start(bf16[2,2,2,64,512]{4,3,2,1,0:T(8,128)(2,1)} %bitcast.110), channel_id=1, source_target_pairs={{0,3},{1,2},{2,1},{3,0},{4,7},{5,6},{6,5},{7,4},{8,11},{9,10},{10,... | collective-permute-start | bytes 1572872 | tf_op jit(solution)/shard_map/ppermute | solution.py:711
  136.3 3.4 %collective-permute-start.9 = (bf16[2,2,2,64,512]{4,3,2,1,0:T(8,128)(2,1)}, bf16[2,2,2,64,512]{4,3,2,1,0:T(8,128)(2,1)S(1)}, u32[]{:S(2)}, u32[]{:S(2)}) collective-permute-start(bf16[2,2,2,64,512]{4,3,2,1,0:T(8,128)(2,1)} %bitcast.117), channel_id=1, source_target_pairs={{0,1},{1,0},{2,3},{3,2},{4,5},{5,4},{6,7},{7,6},{8,9},{9,8},{10,11... | collective-permute-start | bytes 1572872 | tf_op jit(solution)/shard_map/ppermute | solution.py:711
  136.7 31.9 %collective-permute-start.10 = (bf16[2,2,2,64,512]{4,3,2,1,0:T(8,128)(2,1)}, bf16[2,2,2,64,512]{4,3,2,1,0:T(8,128)(2,1)}, u32[]{:S(2)}, u32[]{:S(2)}) collective-permute-start(bf16[2,2,2,64,512]{4,3,2,1,0:T(8,128)(2,1)} %bitcast.115), channel_id=1, source_target_pairs={{0,2},{1,3},{2,0},{3,1},{4,6},{5,7},{6,4},{7,5},{8,10},{9,11},{10,... | collective-permute-start | bytes 1572872 | tf_op jit(solution)/shard_map/ppermute | solution.py:711
  138.5 0.8 copy-start.4
  138.5 30.0 %collective-permute-start.11 = (bf16[2,2,2,64,512]{4,3,2,1,0:T(8,128)(2,1)}, bf16[2,2,2,64,512]{4,3,2,1,0:T(8,128)(2,1)}, u32[]{:S(2)}, u32[]{:S(2)}) collective-permute-start(bf16[2,2,2,64,512]{4,3,2,1,0:T(8,128)(2,1)} %bitcast.36), channel_id=1, source_target_pairs={{0,3},{1,2},{2,1},{3,0},{4,7},{5,6},{6,5},{7,4},{8,11},{9,10},{10,... | collective-permute-start | bytes 1572872 | tf_op jit(solution)/shard_map/ppermute | solution.py:711
  138.6 0.9 copy-start.5
  138.7 1.0 copy-start.6
  139.7 1.3 copy-start.14
  139.7 0.8 copy-start.19
  168.6 14.8 %copy-start.17 = (f32[10,1,512]{2,1,0:T(1,128)S(1)}, f32[10,1,512]{2,1,0:T(1,128)}, u32[]{:S(2)}) copy-start(f32[10,1,512]{2,1,0:T(1,128)} %get-tuple-element.148) | copy-start | bytes 61444
  168.6 14.8 %copy-start.18 = (f32[10,1,512]{2,1,0:T(1,128)S(1)}, f32[10,1,512]{2,1,0:T(1,128)}, u32[]{:S(2)}) copy-start(f32[10,1,512]{2,1,0:T(1,128)} %get-tuple-element.149) | copy-start | bytes 61444
  168.6 18.7 %copy-start.2 = (s32[5]{0:T(128)S(1)}, s32[5]{0:T(128)}, u32[]{:S(2)}) copy-start(s32[5]{0:T(128)} %stack.32.refs_0_) | copy-start | bytes 64
  182.8 2.9 %collective-permute-start.12 = (bf16[2,4,2,64,512]{4,3,2,1,0:T(8,128)(2,1)}, bf16[2,4,2,64,512]{4,3,2,1,0:T(8,128)(2,1)S(1)}, u32[]{:S(2)}, u32[]{:S(2)}) collective-permute-start(bf16[2,4,2,64,512]{4,3,2,1,0:T(8,128)(2,1)} %bitcast.109), channel_id=1, source_target_pairs={{0,1},{1,0},{2,3},{3,2},{4,5},{5,4},{6,7},{7,6},{8,9},{9,8},{10,11... | collective-permute-start | bytes 3145736 | tf_op jit(solution)/shard_map/ppermute | solution.py:711
  183.1 4.2 %collective-permute-start.13 = (bf16[2,4,2,64,512]{4,3,2,1,0:T(8,128)(2,1)}, bf16[2,4,2,64,512]{4,3,2,1,0:T(8,128)(2,1)S(1)}, u32[]{:S(2)}, u32[]{:S(2)}) collective-permute-start(bf16[2,4,2,64,512]{4,3,2,1,0:T(8,128)(2,1)} %bitcast.108), channel_id=1, source_target_pairs={{0,1},{1,0},{2,3},{3,2},{4,5},{5,4},{6,7},{7,6},{8,9},{9,8},{10,11... | collective-permute-start | bytes 3145736 | tf_op jit(solution)/shard_map/ppermute | solution.py:711
  187.2 1.2 copy-start
  188.5 1.5 copy-start.1
  192.0 0.8 copy-start.7
  192.8 31.1 %collective-permute-start.16 = (bf16[4,256,256]{2,1,0:T(8,128)(2,1)}, bf16[4,256,256]{2,1,0:T(8,128)(2,1)S(1)}, u32[]{:S(2)}, u32[]{:S(2)}) collective-permute-start(bf16[4,256,256]{2,1,0:T(8,128)(2,1)} %get-tuple-element.151), channel_id=1, source_target_pairs={{0,4},{4,0},{8,12},{12,8},{16,20},{20,16},{24,28},{28,24},{1,5},{5... | collective-permute-start | bytes 1572872 | tf_op jit(solution)/shard_map/ppermute | solution.py:711
  194.5 29.4 %collective-permute-start.17 = (bf16[4,256,256]{2,1,0:T(8,128)(2,1)}, bf16[4,256,256]{2,1,0:T(8,128)(2,1)}, u32[]{:S(2)}, u32[]{:S(2)}) collective-permute-start(bf16[4,256,256]{2,1,0:T(8,128)(2,1)} %get-tuple-element.152), channel_id=1, source_target_pairs={{0,2},{1,3},{2,0},{3,1},{4,6},{5,7},{6,4},{7,5},{8,10},{9,11},{10,... | collective-permute-start | bytes 1572872 | tf_op jit(solution)/shard_map/ppermute | solution.py:711
  196.0 29.7 %collective-permute-start.18 = (bf16[4,256,256]{2,1,0:T(8,128)(2,1)S(1)}, bf16[4,256,256]{2,1,0:T(8,128)(2,1)}, u32[]{:S(2)}, u32[]{:S(2)}) collective-permute-start(bf16[4,256,256]{2,1,0:T(8,128)(2,1)S(1)} %get-tuple-element.153), channel_id=1, source_target_pairs={{0,6},{1,7},{2,4},{3,5},{4,2},{5,3},{6,0},{7,1},{8,14},{9,15},{10,... | collective-permute-start | bytes 1572872 | tf_op jit(solution)/shard_map/ppermute | solution.py:723
  196.3 25.8 %copy-start.15 = (f32[10,1,512]{2,1,0:T(1,128)S(1)}, f32[10,1,512]{2,1,0:T(1,128)}, u32[]{:S(2)}) copy-start(f32[10,1,512]{2,1,0:T(1,128)} %get-tuple-element.145) | copy-start | bytes 61444
  196.3 25.8 %copy-start.16 = (f32[10,1,512]{2,1,0:T(1,128)S(1)}, f32[10,1,512]{2,1,0:T(1,128)}, u32[]{:S(2)}) copy-start(f32[10,1,512]{2,1,0:T(1,128)} %get-tuple-element.146) | copy-start | bytes 61444
  196.3 29.4 %copy-start.3 = (s32[5]{0:T(128)S(1)}, s32[5]{0:T(128)}, u32[]{:S(2)}) copy-start(s32[5]{0:T(128)} %stack.32.refs_0_) | copy-start | bytes 64
  196.3 29.4 %copy-start.8 = (bf16[4,256,256]{2,1,0:T(8,128)(2,1)S(1)}, bf16[4,256,256]{2,1,0:T(8,128)(2,1)}, u32[]{:S(2)}) copy-start(bf16[4,256,256]{2,1,0:T(8,128)(2,1)} %copy-done.7) | copy-start | bytes 1572868
  222.0 8.8 %collective-permute-start.14 = (bf16[2,4,2,64,512]{4,3,2,1,0:T(8,128)(2,1)}, bf16[2,4,2,64,512]{4,3,2,1,0:T(8,128)(2,1)S(1)}, u32[]{:S(2)}, u32[]{:S(2)}) collective-permute-start(bf16[2,4,2,64,512]{4,3,2,1,0:T(8,128)(2,1)} %bitcast.107), channel_id=1, source_target_pairs={{0,1},{1,0},{2,3},{3,2},{4,5},{5,4},{6,7},{7,6},{8,9},{9,8},{10,11... | collective-permute-start | bytes 3145736 | tf_op jit(solution)/shard_map/ppermute | solution.py:711
  223.4 7.4 %collective-permute-start.15 = (bf16[1,4,2,16,512]{4,3,2,1,0:T(8,128)(2,1)S(1)}, bf16[1,4,2,16,512]{4,3,2,1,0:T(8,128)(2,1)S(1)}, u32[]{:S(2)}, u32[]{:S(2)}) collective-permute-start(bf16[1,4,2,16,512]{4,3,2,1,0:T(8,128)(2,1)S(1)} %bitcast.97), channel_id=1, source_target_pairs={{0,1},{1,0},{2,3},{3,2},{4,5},{5,4},{6,7},{7,6},{8,9},{9,8},{10,11... | collective-permute-start | bytes 393224 | tf_op jit(solution)/shard_map/ppermute | solution.py:711
  225.7 1.6 copy-start.10
  227.3 3.6 %copy-start.11 = (bf16[2,8,64,512]{3,2,1,0:T(8,128)(2,1)S(1)}, bf16[2,8,64,512]{3,2,1,0:T(8,128)(2,1)}, u32[]{:S(2)}) copy-start(bf16[2,8,64,512]{3,2,1,0:T(8,128)(2,1)} %get-tuple-element.144) | copy-start | bytes 3145732
  229.3 10.3 %collective-permute-start.22 = (bf16[256,256]{1,0:T(8,128)(2,1)S(1)}, bf16[256,256]{1,0:T(8,128)(2,1)S(1)}, u32[]{:S(2)}, u32[]{:S(2)}) collective-permute-start(bf16[256,256]{1,0:T(8,128)(2,1)S(1)} %get-tuple-element.159), channel_id=1, source_target_pairs={{0,8},{4,12},{8,0},{12,4},{16,24},{20,28},{24,16},{28,20},{1,9},{5... | collective-permute-start | bytes 393224 | tf_op jit(solution)/shard_map/ppermute | solution.py:711
  231.6 18.6 %collective-permute-start.19 = (bf16[4,144,256]{2,1,0:T(8,128)(2,1)S(1)}, bf16[4,144,256]{2,1,0:T(8,128)(2,1)S(1)}, u32[]{:S(2)}, u32[]{:S(2)}) collective-permute-start(bf16[4,144,256]{2,1,0:T(8,128)(2,1)S(1)} %get-tuple-element.156), channel_id=1, source_target_pairs={{0,4},{4,0},{8,12},{12,8},{16,20},{20,16},{24,28},{28,24},{1,5},{5... | collective-permute-start | bytes 884744 | tf_op jit(solution)/shard_map/ppermute | solution.py:711
  232.3 18.8 %collective-permute-start.20 = (bf16[4,144,256]{2,1,0:T(8,128)(2,1)S(1)}, bf16[4,144,256]{2,1,0:T(8,128)(2,1)S(1)}, u32[]{:S(2)}, u32[]{:S(2)}) collective-permute-start(bf16[4,144,256]{2,1,0:T(8,128)(2,1)S(1)} %get-tuple-element.157), channel_id=1, source_target_pairs={{0,2},{1,3},{2,0},{3,1},{4,6},{5,7},{6,4},{7,5},{8,10},{9,11},{10,... | collective-permute-start | bytes 884744 | tf_op jit(solution)/shard_map/ppermute | solution.py:711
  233.3 17.8 %collective-permute-start.21 = (bf16[4,144,256]{2,1,0:T(8,128)(2,1)S(1)}, bf16[4,144,256]{2,1,0:T(8,128)(2,1)S(1)}, u32[]{:S(2)}, u32[]{:S(2)}) collective-permute-start(bf16[4,144,256]{2,1,0:T(8,128)(2,1)S(1)} %get-tuple-element.158), channel_id=1, source_target_pairs={{0,6},{1,7},{2,4},{3,5},{4,2},{5,3},{6,0},{7,1},{8,14},{9,15},{10,... | collective-permute-start | bytes 884744 | tf_op jit(solution)/shard_map/ppermute | solution.py:723
  235.2 13.8 %collective-permute-start.23 = (bf16[256,256]{1,0:T(8,128)(2,1)S(1)}, bf16[256,256]{1,0:T(8,128)(2,1)S(1)}, u32[]{:S(2)}, u32[]{:S(2)}) collective-permute-start(bf16[256,256]{1,0:T(8,128)(2,1)S(1)} %get-tuple-element.160), channel_id=1, source_target_pairs={{0,16},{4,20},{8,24},{12,28},{16,0},{20,4},{24,8},{28,12},{1,17},{... | collective-permute-start | bytes 393224 | tf_op jit(solution)/shard_map/ppermute | solution.py:711
  239.5 9.5 %collective-permute-start.24 = (bf16[256,256]{1,0:T(8,128)(2,1)S(1)}, bf16[256,256]{1,0:T(8,128)(2,1)S(1)}, u32[]{:S(2)}, u32[]{:S(2)}) collective-permute-start(bf16[256,256]{1,0:T(8,128)(2,1)S(1)} %get-tuple-element.161), channel_id=1, source_target_pairs={{0,24},{4,28},{8,16},{12,20},{16,8},{20,12},{24,0},{28,4},{1,25},{... | collective-permute-start | bytes 393224 | tf_op jit(solution)/shard_map/ppermute | solution.py:711
  249.1 15.2 %collective-permute-start.28 = (bf16[256,256]{1,0:T(8,128)(2,1)S(1)}, bf16[256,256]{1,0:T(8,128)(2,1)S(1)}, u32[]{:S(2)}, u32[]{:S(2)}) collective-permute-start(bf16[256,256]{1,0:T(8,128)(2,1)S(1)} %sum_last.2.refs_5_.refs_1_), channel_id=1, source_target_pairs={{0,1},{1,0},{2,3},{3,2},{4,5},{5,4},{6,7},{7,6},{8,9},{9,8},{10,11... | collective-permute-start | bytes 393224 | tf_op jit(solution)/shard_map/ppermute | solution.py:711
  249.2 16.3 %collective-permute-start.29 = (bf16[256,256]{1,0:T(8,128)(2,1)S(1)}, bf16[256,256]{1,0:T(8,128)(2,1)S(1)}, u32[]{:S(2)}, u32[]{:S(2)}) collective-permute-start(bf16[256,256]{1,0:T(8,128)(2,1)S(1)} %sum_last.2.refs_5_.refs_1_), channel_id=1, source_target_pairs={{0,2},{1,3},{2,0},{3,1},{4,6},{5,7},{6,4},{7,5},{8,10},{9,11},{10,... | collective-permute-start | bytes 393224 | tf_op jit(solution)/shard_map/ppermute | solution.py:711
  250.3 15.9 %collective-permute-start.30 = (bf16[256,256]{1,0:T(8,128)(2,1)S(1)}, bf16[256,256]{1,0:T(8,128)(2,1)S(1)}, u32[]{:S(2)}, u32[]{:S(2)}) collective-permute-start(bf16[256,256]{1,0:T(8,128)(2,1)S(1)} %sum_last.2.refs_5_.refs_1_), channel_id=1, source_target_pairs={{0,3},{1,2},{2,1},{3,0},{4,7},{5,6},{6,5},{7,4},{8,11},{9,10},{10,... | collective-permute-start | bytes 393224 | tf_op jit(solution)/shard_map/ppermute | solution.py:711
  251.8 15.5 %collective-permute-start.25 = (bf16[144,256]{1,0:T(8,128)(2,1)S(1)}, bf16[144,256]{1,0:T(8,128)(2,1)S(1)}, u32[]{:S(2)}, u32[]{:S(2)}) collective-permute-start(bf16[144,256]{1,0:T(8,128)(2,1)S(1)} %get-tuple-element.163), channel_id=1, source_target_pairs={{0,8},{4,12},{8,0},{12,4},{16,24},{20,28},{24,16},{28,20},{1,9},{5... | collective-permute-start | bytes 221192 | tf_op jit(solution)/shard_map/ppermute | solution.py:711
  264.3 13.4 %collective-permute-start.34 = (bf16[384,256]{1,0:T(8,128)(2,1)}, bf16[384,256]{1,0:T(8,128)(2,1)S(1)}, u32[]{:S(2)}, u32[]{:S(2)}) collective-permute-start(bf16[384,256]{1,0:T(8,128)(2,1)} %bitcast.87), channel_id=1, source_target_pairs={{0,1},{1,0},{2,3},{3,2},{4,5},{5,4},{6,7},{7,6},{8,9},{9,8},{10,11... | collective-permute-start | bytes 589832 | tf_op jit(solution)/shard_map/ppermute | solution.py:711
  264.3 13.8 %collective-permute-start.35 = (bf16[384,256]{1,0:T(8,128)(2,1)}, bf16[384,256]{1,0:T(8,128)(2,1)S(1)}, u32[]{:S(2)}, u32[]{:S(2)}) collective-permute-start(bf16[384,256]{1,0:T(8,128)(2,1)} %bitcast.88), channel_id=1, source_target_pairs={{0,2},{1,3},{2,0},{3,1},{4,6},{5,7},{6,4},{7,5},{8,10},{9,11},{10,... | collective-permute-start | bytes 589832 | tf_op jit(solution)/shard_map/ppermute | solution.py:711
  265.4 12.6 %collective-permute-start.36 = (bf16[384,256]{1,0:T(8,128)(2,1)}, bf16[384,256]{1,0:T(8,128)(2,1)S(1)}, u32[]{:S(2)}, u32[]{:S(2)}) collective-permute-start(bf16[384,256]{1,0:T(8,128)(2,1)} %bitcast.89), channel_id=1, source_target_pairs={{0,3},{1,2},{2,1},{3,0},{4,7},{5,6},{6,5},{7,4},{8,11},{9,10},{10,... | collective-permute-start | bytes 589832 | tf_op jit(solution)/shard_map/ppermute | solution.py:711
  266.1 8.9 %collective-permute-start.26 = (bf16[144,256]{1,0:T(8,128)(2,1)S(1)}, bf16[144,256]{1,0:T(8,128)(2,1)S(1)}, u32[]{:S(2)}, u32[]{:S(2)}) collective-permute-start(bf16[144,256]{1,0:T(8,128)(2,1)S(1)} %get-tuple-element.164), channel_id=1, source_target_pairs={{0,16},{4,20},{8,24},{12,28},{16,0},{20,4},{24,8},{28,12},{1,17},{... | collective-permute-start | bytes 221192 | tf_op jit(solution)/shard_map/ppermute | solution.py:711
  267.3 7.7 %collective-permute-start.27 = (bf16[144,256]{1,0:T(8,128)(2,1)S(1)}, bf16[144,256]{1,0:T(8,128)(2,1)S(1)}, u32[]{:S(2)}, u32[]{:S(2)}) collective-permute-start(bf16[144,256]{1,0:T(8,128)(2,1)S(1)} %get-tuple-element.165), channel_id=1, source_target_pairs={{0,24},{4,28},{8,16},{12,20},{16,8},{20,12},{24,0},{28,4},{1,25},{... | collective-permute-start | bytes 221192 | tf_op jit(solution)/shard_map/ppermute | solution.py:711
  271.0 7.1 %copy-start.9 = (bf16[1,384,256]{2,1,0:T(8,128)(2,1)S(1)}, bf16[1,384,256]{2,1,0:T(8,128)(2,1)}, u32[]{:S(2)}) copy-start(bf16[1,384,256]{2,1,0:T(8,128)(2,1)} %reduce-scatter.2.cloned.1.call-done) | copy-start | bytes 589828
  275.0 1.0 copy-start.12
  276.1 3.8 %collective-permute-start.31 = (bf16[144,256]{1,0:T(8,128)(2,1)S(1)}, bf16[144,256]{1,0:T(8,128)(2,1)S(1)}, u32[]{:S(2)}, u32[]{:S(2)}) collective-permute-start(bf16[144,256]{1,0:T(8,128)(2,1)S(1)} %sum_last.3.refs_5_.refs_1_), channel_id=1, source_target_pairs={{0,1},{1,0},{2,3},{3,2},{4,5},{5,4},{6,7},{7,6},{8,9},{9,8},{10,11... | collective-permute-start | bytes 221192 | tf_op jit(solution)/shard_map/ppermute | solution.py:711
  276.2 4.9 %collective-permute-start.32 = (bf16[144,256]{1,0:T(8,128)(2,1)S(1)}, bf16[144,256]{1,0:T(8,128)(2,1)S(1)}, u32[]{:S(2)}, u32[]{:S(2)}) collective-permute-start(bf16[144,256]{1,0:T(8,128)(2,1)S(1)} %sum_last.3.refs_5_.refs_1_), channel_id=1, source_target_pairs={{0,2},{1,3},{2,0},{3,1},{4,6},{5,7},{6,4},{7,5},{8,10},{9,11},{10,... | collective-permute-start | bytes 221192 | tf_op jit(solution)/shard_map/ppermute | solution.py:711
  277.7 4.6 %collective-permute-start.33 = (bf16[144,256]{1,0:T(8,128)(2,1)S(1)}, bf16[144,256]{1,0:T(8,128)(2,1)S(1)}, u32[]{:S(2)}, u32[]{:S(2)}) collective-permute-start(bf16[144,256]{1,0:T(8,128)(2,1)S(1)} %sum_last.3.refs_5_.refs_1_), channel_id=1, source_target_pairs={{0,3},{1,2},{2,1},{3,0},{4,7},{5,6},{6,5},{7,4},{8,11},{9,10},{10,... | collective-permute-start | bytes 221192 | tf_op jit(solution)/shard_map/ppermute | solution.py:711
  282.2 1.0 copy-start.13
Sparse Core Ops, SparseCore 0:
  138.6 125.5 reduce-scatter.1
